TPU v7x, 32 devices: a whole 2x2x4 slice. The times are simulated.
32 devices in a mesh: dp: 8 (over z, core), tensor: 4 (over y, x).
Axes of the slice: x: 2, y: 2, z: 4, core: 2. Of those that a mesh axis runs over, the one named last changes fastest.
Arguments:
- hidden: bfloat16 [32768, 1536], P(('dp', 'tensor')), may hold values from -6 to 6
- norm_gain: float32 [1536], replicated, may hold values from 0.5 to 1.5
- head_weight: bfloat16 [1536, 2, 3072], P('dp', None, 'tensor'), may hold values from -0.15625 to 0.15625
- step_weight: bfloat16 [1536, 48], P('dp', 'tensor'), may hold values from -0.15625 to 0.15625
- map_weight: bfloat16 [1536, 256], P(('dp', 'tensor')), may hold values from -0.15625 to 0.15625
- conv_weight: float32 [4, 3328], replicated, may hold values from -3 to 3
- conv_bias: float32 [3328], replicated, may hold values from -0.5 to 0.5
- step_bias: float32 [48], replicated, may hold values from -6 to -3
- decay_log: float32 [48], replicated, may hold values from -2 to 1
- skip_gain: float32 [48], replicated, may hold values from 0.5 to 1.5
- gate_gain: float32 [3072], replicated, may hold values from 0.5 to 1.5
- out_weight: bfloat16 [1536, 3072], P('dp', 'tensor'), may hold values from -0.109375 to 0.109375
- cotangent: bfloat16 [32768, 1536], P(('dp', 'tensor')), may hold values from -6 to 6
Outputs:
- block_out: bfloat16 [32768, 1536], P(('dp', 'tensor'))
- grad_hidden: float32 [32768, 1536], P(('dp', 'tensor'))
- grad_norm_gain: float32 [1536], replicated
- grad_head_weight: float32 [1536, 2, 3072], P('dp', None, 'tensor')
- grad_step_weight: float32 [1536, 48], P('dp', 'tensor')
- grad_map_weight: float32 [1536, 256], P(('dp', 'tensor'))
- grad_conv_weight: float32 [4, 3328], replicated
- grad_conv_bias: float32 [3328], replicated
- grad_step_bias: float32 [48], replicated
- grad_decay_log: float32 [48], replicated
- grad_skip_gain: float32 [48], replicated
- grad_gate_gain: float32 [3072], replicated
- grad_out_weight: float32 [1536, 3072], P('dp', 'tensor')
All inputs are finite; a program needn't handle non-finite values.
Results may differ from a plain program's by a relative error of at most 0.014.
Values may be sent and summed in bfloat16 or wider, within the bound.
No kernel may reach another device: no remote copies, remote signals or barrier semaphores. Data moves between devices by JAX's collectives and lax.ppermute only.
A program may use at most 384 MiB of HBM per device.

v0:
```python
import jax
import jax.numpy as jnp
from jax import lax
from jax.sharding import PartitionSpec as P

D = 1536
H = 48
HEAD = 64
NS = 128
KW = 4
BLOCK = 256
LEN = 2048
DI = 3072


EPSILON = 1e-05
PRECISE = lax.Precision.HIGHEST


def conv_silu(before, weight, bias):
    channels = before.shape[1]
    seqs = before.shape[0] // LEN
    shaped = before.reshape(seqs, LEN, channels)
    padded = jnp.pad(shaped, ((0, 0), (KW - 1, 0), (0, 0)))
    total = bias + weight[0] * padded[:, 0:LEN]
    for shift_by in range(1, KW):
        total = total + weight[shift_by] * padded[:, shift_by : shift_by + LEN]
    return jax.nn.silu(total).reshape(seqs * LEN, channels)


def ssd(values, delta, in_map, out_map, rate, skip):
    seqs, length, heads, width = values.shape
    blocks = length // BLOCK

    def to_blocks(array):
        shaped = array.reshape((seqs, blocks, BLOCK) + array.shape[2:])
        return jnp.moveaxis(shaped, 1, 0)

    causal = jnp.arange(BLOCK)[:, None] >= jnp.arange(BLOCK)[None, :]

    def step(state, block):
        block_x, block_dt, block_b, block_c = block
        decay_sum = jnp.cumsum(block_dt * rate, axis=1)
        scores = jnp.einsum("sqn,skn->sqk", block_c, block_b, precision=PRECISE)
        spread_log = decay_sum[:, :, None, :] - decay_sum[:, None, :, :]
        weights = jnp.exp(jnp.where(causal[None, :, :, None], spread_log, -1e30))
        weights = weights * scores[:, :, :, None] * block_dt[:, None, :, :]
        within = jnp.einsum("sqkh,skhp->sqhp", weights, block_x, precision=PRECISE)
        across = jnp.exp(decay_sum)[:, :, :, None] * jnp.einsum(
            "sqn,shpn->sqhp", block_c, state, precision=PRECISE
        )
        to_end = jnp.exp(decay_sum[:, -1:, :] - decay_sum) * block_dt
        carried = jnp.exp(decay_sum[:, -1, :])[:, :, None, None] * state
        state = carried + jnp.einsum(
            "skh,skhp,skn->shpn", to_end, block_x, block_b, precision=PRECISE
        )
        return (state, within + across + skip[None, None, :, None] * block_x)

    initial = jnp.zeros((seqs, heads, width, in_map.shape[-1]), jnp.float32)
    _, outputs = lax.scan(
        jax.checkpoint(step),
        initial,
        (to_blocks(values), to_blocks(delta), to_blocks(in_map), to_blocks(out_map)),
    )
    return jnp.moveaxis(outputs, 0, 1).reshape(seqs, length, heads, width)


def mixer_tail(mixed, step_raw, gate, step_bias, decay_log, skip_gain):
    rows_all, inner = gate.shape
    heads = inner // HEAD
    seqs = rows_all // LEN
    block_x = mixed[:, :inner].reshape(seqs, LEN, heads, HEAD)
    in_map = mixed[:, inner : inner + NS].reshape(seqs, LEN, NS)
    out_map = mixed[:, inner + NS :].reshape(seqs, LEN, NS)
    delta = jax.nn.softplus(step_raw + step_bias).reshape(seqs, LEN, heads)
    result = ssd(block_x, delta, in_map, out_map, -jnp.exp(decay_log), skip_gain)
    return result.reshape(rows_all, inner) * jax.nn.silu(gate)


def place(piece, start, total, axis_dim):
    shape = list(piece.shape)
    shape[axis_dim] = total
    return lax.dynamic_update_slice_in_dim(jnp.zeros(shape, jnp.float32), piece, start, axis_dim)


def contract(left, right, left_dim, right_dim):
    return lax.dot_general(
        left, right, (((left_dim,), (right_dim,)), ((), ())), preferred_element_type=jnp.float32
    )


def shards(
    hidden,
    norm_gain,
    head_weight,
    step_weight,
    map_weight,
    conv_weight,
    conv_bias,
    step_bias,
    decay_log,
    skip_gain,
    gate_gain,
    out_weight,
    cotangent,
):
    part = lax.axis_index("tensor")
    inner = head_weight.shape[2]
    heads = step_weight.shape[1]
    head_start = part * inner
    step_start = part * heads
    rows = hidden.astype(jnp.float32)
    inverse = lax.rsqrt(jnp.mean(rows * rows, axis=-1, keepdims=True) + EPSILON)
    normed = (rows * inverse * norm_gain).astype(jnp.bfloat16)
    gathered = lax.all_gather(normed, "tensor", axis=0, tiled=True)
    full_head, full_step, full_out = (
        lax.all_gather(head_weight, "dp", axis=0, tiled=True),
        lax.all_gather(step_weight, "dp", axis=0, tiled=True),
        lax.all_gather(out_weight, "dp", axis=0, tiled=True),
    )
    full_map = lax.all_gather(map_weight, ("dp", "tensor"), axis=0, tiled=True)
    columns = jnp.concatenate([full_head.reshape(D, 2 * inner), full_step], axis=1)
    projected = jnp.dot(gathered, columns, preferred_element_type=jnp.float32)
    map_proj = jnp.dot(gathered, full_map, preferred_element_type=jnp.float32)
    gate = projected[:, :inner]
    step_raw = projected[:, 2 * inner :]
    before = jnp.concatenate([projected[:, inner : 2 * inner], map_proj], axis=1)
    conv_local = jnp.concatenate(
        [lax.dynamic_slice_in_dim(conv_weight, head_start, inner, 1), conv_weight[:, DI:]], axis=1
    )
    bias_local = jnp.concatenate(
        [lax.dynamic_slice_in_dim(conv_bias, head_start, inner, 0), conv_bias[DI:]], axis=0
    )
    step_local = lax.dynamic_slice_in_dim(step_bias, step_start, heads, 0)
    decay_local = lax.dynamic_slice_in_dim(decay_log, step_start, heads, 0)
    skip_local = lax.dynamic_slice_in_dim(skip_gain, step_start, heads, 0)
    gain_local = lax.dynamic_slice_in_dim(gate_gain, head_start, inner, 0)
    mixed, conv_pull = jax.vjp(conv_silu, before, conv_local, bias_local)
    mixed_low = lax.optimization_barrier(mixed.astype(jnp.bfloat16)).astype(jnp.float32)
    gated, tail_pull = jax.vjp(
        mixer_tail, mixed_low, step_raw, gate, step_local, decay_local, skip_local
    )
    total_square = lax.psum(jnp.sum(gated * gated, axis=-1), "tensor")
    gate_inverse = lax.rsqrt(total_square / DI + EPSILON)[:, None]
    scaled = (gated * gate_inverse * gain_local).astype(jnp.bfloat16)
    branch = lax.psum_scatter(
        contract(scaled, full_out, 1, 1).astype(jnp.bfloat16),
        "tensor",
        scatter_dimension=0,
        tiled=True,
    ).astype(jnp.float32)
    block_out = (rows + branch).astype(jnp.bfloat16)
    grad_all = lax.all_gather(cotangent, "tensor", axis=0, tiled=True)
    grad_scaled = jnp.dot(grad_all, full_out, preferred_element_type=jnp.float32)
    grad_out_weight = contract(grad_all, scaled, 0, 0)
    weighted = grad_scaled * gain_local
    dots = lax.psum(jnp.sum(weighted * gated, axis=-1), "tensor")
    grad_gated = gate_inverse * weighted - gated * gate_inverse**3 * (dots / DI)[:, None]
    grad_gain = jnp.sum(grad_scaled * gated * gate_inverse, axis=0)
    grad_mixed, grad_delta, grad_gate, grad_step, grad_decay, grad_skip = tail_pull(grad_gated)
    grad_before, grad_conv, grad_cbias = conv_pull(grad_mixed)
    grad_heads = jnp.concatenate([grad_gate, grad_before[:, :inner], grad_delta], axis=1).astype(
        jnp.bfloat16
    )
    grad_map_part = grad_before[:, inner:]
    grad_columns = contract(gathered, grad_heads, 0, 0)
    grad_head = grad_columns[:, : 2 * inner].reshape(D, 2, inner)
    grad_stepw = grad_columns[:, 2 * inner :]
    shard_head, shard_step, shard_out = (
        lax.psum_scatter(
            grad_head.astype(jnp.bfloat16), "dp", scatter_dimension=0, tiled=True
        ).astype(jnp.float32),
        lax.psum_scatter(
            grad_stepw.astype(jnp.bfloat16), "dp", scatter_dimension=0, tiled=True
        ).astype(jnp.float32),
        lax.psum_scatter(
            grad_out_weight.astype(jnp.bfloat16), "dp", scatter_dimension=0, tiled=True
        ).astype(jnp.float32),
    )
    own_in, own_map = (
        lax.psum_scatter(
            contract(grad_heads, columns, 1, 1), "tensor", scatter_dimension=0, tiled=True
        ),
        lax.psum_scatter(grad_map_part, "tensor", scatter_dimension=0, tiled=True),
    )
    map_low = own_map.astype(jnp.bfloat16)
    own_in = own_in + contract(map_low, full_map, 1, 1)
    map_shard = lax.psum_scatter(
        contract(normed, map_low, 0, 0), ("dp", "tensor"), scatter_dimension=0, tiled=True
    )
    scaled_in = own_in * norm_gain
    grad_hidden = (
        cotangent.astype(jnp.float32)
        + inverse * scaled_in
        - rows * inverse**3 * jnp.mean(scaled_in * rows, axis=-1, keepdims=True)
    )
    grad_norm = jnp.sum(own_in * rows * inverse, axis=0)
    conv_full = jnp.concatenate(
        [place(grad_conv[:, :inner], head_start, DI, 1), grad_conv[:, inner:]], axis=1
    )
    cbias_full = jnp.concatenate(
        [place(grad_cbias[:inner], head_start, DI, 0), grad_cbias[inner:]], axis=0
    )
    sums = lax.psum(
        (
            grad_norm,
            conv_full,
            cbias_full,
            place(grad_step, step_start, H, 0),
            place(grad_decay, step_start, H, 0),
            place(grad_skip, step_start, H, 0),
            place(grad_gain, head_start, DI, 0),
        ),
        ("dp", "tensor"),
    )
    return (
        block_out,
        grad_hidden,
        sums[0],
        shard_head,
        shard_step,
        map_shard,
        sums[1],
        sums[2],
        sums[3],
        sums[4],
        sums[5],
        sums[6],
        shard_out,
    )


def solution(mesh):
    placed = (
        P(("dp", "tensor"), None),
        P(),
        P("dp", None, "tensor"),
        P("dp", "tensor"),
        P(("dp", "tensor"), None),
        P(),
        P(),
        P(),
        P(),
        P(),
        P(),
        P("dp", "tensor"),
        P(("dp", "tensor"), None),
    )
    return jax.shard_map(
        shards,
        mesh=mesh,
        in_specs=placed,
        out_specs=(
            P(("dp", "tensor"), None),
            P(("dp", "tensor"), None),
            P(),
            P("dp", None, "tensor"),
            P("dp", "tensor"),
            P(("dp", "tensor"), None),
            P(),
            P(),
            P(),
            P(),
            P(),
            P(),
            P("dp", "tensor"),
        ),
        check_vma=False,
    )
```

profile of v0, /device:TPU:0, one launch (start us, length us, event | category | flops | bytes accessed | tf_op | source)
XLA Modules:
  0.0 2327.3 jit_solution(5118581308741181168)
XLA Ops:
  35.3 76.0 %all_gather.21 = bf16[1536,256]{1,0:T(8,128)(2,1)S(1)} all-gather(bf16[48,256]{1,0:T(8,128)(2,1)S(1)} %copy-done.35), channel_id=1, replica_groups=mesh['dp'=8,'tensor'=4] {'dp','tensor'}, dimensions={0}, use_global_device_ids=true | all-gather | bytes 811008 | tf_op jit(solution)/shard_map/all_gather | solution.py:121
  118.2 76.3 %all-gather.6.cloned.1.call-done = bf16[4096,1536]{1,0:T(8,128)(2,1)} async-done(((bf16[1024,1536]{1,0:T(8,128)(2,1)}), bf16[4096,1536]{1,0:T(8,128)(2,1)}) %all-gather.6.cloned.1.call-update) | async-done | bytes 12582928 | tf_op jit(solution)/shard_map/all_gather | solution.py:115
  194.5 26.8 %fusion.112 = f32[4096,1548]{0,1:T(8,128)} fusion(bf16[4096,1536]{1,0:T(8,128)(2,1)} %all-gather.6.cloned.1.call-done, bf16[1536,12]{1,0:T(8,128)(2,1)S(1)} %bitcast.408, bf16[1536,1536]{1,0:T(8,128)(2,1)} %bitcast.398), kind=kOutput, calls=%fused_computation.188 | convolution fusion | flops 19487858688 | bytes 42700800 | tf_op jit(solution)/shard_map/dot_general | solution.py:123
  254.8 17.5 copy.206
  272.3 33.6 %multiply_convert_fusion = (bf16[2,2048,1024]{2,1,0:T(8,128)(2,1)}, f32[2,2048,1024]{2,1,0:T(8,128)}) fusion(f32[2,2048,1024]{2,1,0:T(8,128)} %bitcast.372, f32[1024]{0:T(1024)S(1)} %bitcast.416, f32[1024]{0:T(1024)S(1)} %bitcast.418, f32[1024]{0:T(1024)S(1)} %bitcast.414, f32[1024]{0:T(1024)S(1)} %bitcast.412, f32[1024]{0:T(1024)S(1)} %pad_maximum_fusion.10), kind=kLoop, calls=%fused_computation.145 | loop fusion | flops 54525952 | bytes 41963520 | tf_op jit(solution)/shard_map/convert_element_type | solution.py:139
  369.7 164.3 %while.43 = (s32[]{:T(128)}, f32[2,12,64,128]{3,2,1,0:T(8,128)S(1)}, f32[8,2,256,12,64]{2,4,3,1,0:T(8,128)}, f32[8,2,12,64,128]{4,3,2,1,0:T(8,128)}, f32[8,2,256...) while((s32[]{:T(128)}, ...), condition=%wide.region_4.5_spmd.clone, body=%wide.region_1.4_spmd.clone.sunk | while | flops 2627291136 | bytes 16349803 | solution.py:60
  533.9 17.9 copy.212
  595.7 20.5 multiply_reduce_fusion.9
  630.6 25.6 %fusion.99 = (bf16[4096,768]{0,1:T(8,128)(2,1)}, f32[4096,768]{0,1:T(8,128)}) fusion(f32[4096,768]{0,1:T(8,128)} %reshape.303, f32[4096,1548]{0,1:T(8,128)} %fusion.112, f32[4096]{0:T(1024)S(1)} %broadcast_multiply_fusion.5, f32[4096,768]{0,1:T(8,128)} %get-tuple-element.822, f32[4096]{0:T(1024)S(1)} %get-tuple-element.849, ...), kind=kLoop, calls=%fused_computation.160 | loop fusion | flops 56623104 | bytes 69258240 | tf_op jit(solution)/shard_map/convert.2
  671.3 16.8 copy.289
  699.3 651.9 %while.44 = (s32[]{:T(128)}, f32[12]{0:T(128)}, f32[12]{0:T(128)}, f32[2,12,64,128]{3,2,1,0:T(8,128)}, f32[8,2,256,12,64]{2,4,3,1,0:T(8,128)}, /*index=5*/f32[8,...) while((s32[]{:T(128)}, f32[12]{0:T(128)}, f32[12]{0:T(128)}, ...), condition=%wide.region_24.25_spmd.clone, body=%wide.region_10.24_spmd.clone.sunk | while | flops 6074361856 | bytes 52066556 | solution.py:60
  1351.2 17.9 copy.219
  1395.7 40.6 %multiply_reduce_fusion.7 = (f32[1024]{0:T(1024)}, f32[1024]{0:T(1024)}, f32[1024]{0:T(1024)}, f32[1024]{0:T(1024)}, f32[1024]{0:T(1024)}, /*index=5*/f32[2,2048,1024]{2,1,0:T(8,128)}) fusion(f32[2,2048,1024]{2,1,0:T(8,128)} %bitcast.373, f32[4096,1024]{1,0:T(8,128)} %copy.206, f32[2,2048,1024]{2,1,0:T(8,128)} %get-tuple-element.824, ...), kind=kLoop, calls=%fused_computation.142 | loop fusion | flops 83880960 | bytes 83906560 | tf_op jit(solution)/shard_map/transpose(jvp())/reduce_sum | solution.py:27
  1436.3 25.9 %broadcast_multiply_fusion.1 = (f32[2,2048,1024]{2,1,0:T(8,128)}, f32[2,2048,1024]{2,1,0:T(8,128)}, f32[2,2048,1024]{2,1,0:T(8,128)}, f32[2,2048,1024]{2,1,0:T(8,128)}) fusion(f32[2,2048,1024]{2,1,0:T(8,128)} %get-tuple-element.820, f32[1024]{0:T(1024)S(1)} %bitcast.417, f32[1024]{0:T(1024)S(1)} %bitcast.413, f32[1024]{0:T(1024)S(1)} %bitcast.415, ...), kind=kLoop, calls=%fused_computation.169 | loop fusion | flops 16777216 | bytes 83902464 | tf_op jit(solution)/shard_map/transpose(jvp())/mul | solution.py:27
  1462.2 28.9 %pad_add_fusion = f32[2,2048,1024]{2,1,0:T(8,128)} fusion(f32[2,2048,1024]{2,1,0:T(8,128)} %get-tuple-element.842, f32[2,2048,1024]{2,1,0:T(8,128)} %get-tuple-element.843, f32[2,2048,1024]{2,1,0:T(8,128)} %get-tuple-element.844, f32[2,2048,1024]{2,1,0:T(8,128)} %get-tuple-element.841), kind=kLoop, calls=%fused_computation.136 | loop fusion | flops 12582912 | bytes 83886080 | tf_op jit(solution)/shard_map/transpose(jvp())/add_any | solution.py:25
  1515.3 30.7 %convolution_convert_fusion.1 = bf16[1536,1548]{0,1:T(8,128)(2,1)} fusion(bf16[4096,1536]{1,0:T(8,128)(2,1)} %all-gather.6.cloned.1.call-done, bf16[4096,12]{0,1:T(8,128)(2,1)S(1)} %get-tuple-element.819, bf16[4096,768]{0,1:T(8,128)(2,1)} %copy.279, bf16[4096,768]{0,1:T(8,128)(2,1)} %get-tuple-element.839), kind=kOutput, calls=%fused_computation.173 | convolution fusion | flops 19518769152 | bytes 30019584 | tf_op jit(solution)/shard_map/dot_general | solution.py:87
  1584.5 29.9 %fusion.111 = f32[4096,1536]{1,0:T(8,128)} fusion(bf16[4096,12]{0,1:T(8,128)(2,1)S(1)} %get-tuple-element.819, bf16[4096,768]{0,1:T(8,128)(2,1)} %copy.279, bf16[4096,768]{0,1:T(8,128)(2,1)} %get-tuple-element.839, bf16[1536,12]{1,0:T(8,128)(2,1)S(1)} %bitcast.409, bf16[1536,1536]{1,0:T(8,128)(2,1)} %bitcast.399), kind=kOutput, calls=%fused_computation.184 | convolution fusion | flops 19525902336 | bytes 42602496 | tf_op jit(solution)/shard_map/dot_general | solution.py:87
  1616.1 18.0 convolution_convert_fusion
  1645.6 43.9 %all-reduce.19.cloned.1.call-done = bf16[1536,2,768]{2,1,0:T(2,128)(2,1)} async-done(((bf16[1536,2,768]{2,1,0:T(2,128)(2,1)}), bf16[1536,2,768]{2,1,0:T(2,128)(2,1)}) %all-reduce.19.cloned.1.call-update) | async-done | bytes 4718608
  1691.9 36.2 %reduce-scatter.21.cloned.1.call-done = bf16[192,768]{1,0:T(8,128)(2,1)} async-done(((bf16[1536,768]{1,0:T(8,128)(2,1)}), bf16[192,768]{1,0:T(8,128)(2,1)}) %reduce-scatter.21.cloned.1.call-update) | async-done | bytes 294928
  1730.2 222.2 %reduce-scatter.13.cloned.1.call-done = f32[1024,1536]{1,0:T(8,128)} async-done(((f32[4096,1536]{1,0:T(8,128)}), f32[1024,1536]{1,0:T(8,128)}) %reduce-scatter.13.cloned.1.call-update) | async-done | bytes 6291472 | tf_op jit(solution)/shard_map/reduce_scatter | solution.py:181
  1961.0 115.3 %reduce-scatter.11.cloned.1.call-done = bf16[1024,1536]{1,0:T(8,128)(2,1)} async-done(((bf16[4096,1536]{1,0:T(8,128)(2,1)}), bf16[1024,1536]{1,0:T(8,128)(2,1)}) %reduce-scatter.11.cloned.1.call-update) | async-done | bytes 3145744 | tf_op jit(solution)/shard_map/reduce_scatter | solution.py:146
  2084.4 95.8 %reduce-scatter.17.cloned.1.call-done = f32[48,256]{1,0:T(8,128)} async-done(((f32[1536,256]{1,0:T(8,128)}), f32[48,256]{1,0:T(8,128)}) %reduce-scatter.17.cloned.1.call-update) | async-done | bytes 49168 | tf_op jit(solution)/shard_map/reduce_scatter | solution.py:188
  2180.1 131.0 %all-reduce.21.cloned.1.call-done = (f32[1536]{0:T(1024)}, f32[4,3328]{1,0:T(4,128)}, f32[3328]{0:T(1024)}, f32[48]{0:T(128)}, f32[48]{0:T(128)}, /*index=5*/f32[48]{0:T(128)}, f32[3072]{0:T(1024)}) async-done(((f32[1536]{0:T(1024)}, f32[4,3328]{1,0:T(4,128)}, f32[3328]{0:T(1024)}, f32[48]{0:T(128)}, f32[48]{0:T(128)}, /*index=5*/f32[48]{0:T(128)}, f32[3072]{0:T(1024)}), (f32[1536]{0:T(1024)}, ...) | async-done | bytes 85584 | tf_op jit(solution)/shard_map/psum | solution.py:204
  (1044 shorter events, 1160.8 us)
Async XLA Ops:
  7.2 105.6 %all-gather.8.cloned.1.call-start = ((), (), s32[]{:S(2)}) async-start(), calls=%async_computation.7 | async-start | bytes 5308416 | tf_op jit(solution)/shard_map/all_gather | solution.py:117
  7.9 186.6 %all-gather.6.cloned.1.call-start = ((), (), s32[]{:S(2)}) async-start(), calls=%async_computation.6 | async-start | bytes 15728640 | tf_op jit(solution)/shard_map/all_gather | solution.py:115
  16.2 579.5 %all-gather.10.cloned.1.call-start = ((), (), s32[]{:S(2)}) async-start(), calls=%async_computation.8 | async-start | bytes 2654208 | tf_op jit(solution)/shard_map/all_gather | solution.py:119
  17.0 578.8 %all-gather.12.cloned.1.call-start = ((), (), s32[]{:S(2)}) async-start(), calls=%async_computation.10 | async-start | bytes 15728640 | tf_op jit(solution)/shard_map/all_gather | solution.py:153
  17.5 1620.8 %reduce-scatter.15.cloned.1.call-start = ((), (), s32[]{:S(2)}) async-start(), calls=%async_computation.12 | async-start | bytes 5242880 | tf_op jit(solution)/shard_map/reduce_scatter | solution.py:184
  19.3 202.0 %copy-start.48 = (f32[12]{0:T(128)}, f32[12]{0:T(128)S(1)}, u32[]{:S(2)}) copy-start(f32[12]{0:T(128)S(1)} %dynamic_slice.96) | copy-start | bytes 148
  35.3 186.0 %copy-start.13 = (bf16[8,192,12]{2,1,0:T(8,128)(2,1)}, bf16[8,192,12]{2,1,0:T(8,128)(2,1)S(1)}, u32[]{:S(2)}) copy-start(bf16[8,192,12]{2,1,0:T(8,128)(2,1)S(1)} %copy.237) | copy-start | bytes 110596
  111.4 124.0 %copy-start.8 = (bf16[1536,256]{1,0:T(8,128)(2,1)}, bf16[1536,256]{1,0:T(8,128)(2,1)S(1)}, u32[]{:S(2)}) copy-start(bf16[1536,256]{1,0:T(8,128)(2,1)S(1)} %all_gather.21) | copy-start | bytes 2359300
  112.8 159.5 %copy-start.23 = (f32[1,1024]{1,0:T(1,128)}, f32[1,1024]{1,0:T(1,128)S(1)}, u32[]{:S(2)}) copy-start(f32[1,1024]{1,0:T(1,128)S(1)} %get-tuple-element.851) | copy-start | bytes 12292
  112.8 159.5 %copy-start.25 = (f32[1,1024]{1,0:T(1,128)}, f32[1,1024]{1,0:T(1,128)S(1)}, u32[]{:S(2)}) copy-start(f32[1,1024]{1,0:T(1,128)S(1)} %get-tuple-element.852) | copy-start | bytes 12292
  112.8 159.5 %copy-start.27 = (f32[1,1024]{1,0:T(1,128)}, f32[1,1024]{1,0:T(1,128)S(1)}, u32[]{:S(2)}) copy-start(f32[1,1024]{1,0:T(1,128)S(1)} %get-tuple-element.853) | copy-start | bytes 12292
  112.8 159.5 %copy-start.29 = (f32[1,1024]{1,0:T(1,128)}, f32[1,1024]{1,0:T(1,128)S(1)}, u32[]{:S(2)}) copy-start(f32[1,1024]{1,0:T(1,128)S(1)} %get-tuple-element.854) | copy-start | bytes 12292
  1495.8 148.3 %reduce-scatter.19.cloned.1.call-start = ((), (), s32[]{:S(2)}) async-start(), calls=%async_computation.14 | async-start | bytes 442368
  1547.8 141.6 %all-reduce.19.cloned.1.call-start = ((), (), s32[]{:S(2)}) async-start(), calls=%async_computation.16 | async-start | bytes 9437184
  1565.2 162.9 %reduce-scatter.21.cloned.1.call-start = ((), (), s32[]{:S(2)}) async-start(), calls=%async_computation.15 | async-start | bytes 2654208
  1584.4 368.0 %reduce-scatter.13.cloned.1.call-start = ((), (), s32[]{:S(2)}) async-start(), calls=%async_computation.11 | async-start | bytes 31457280 | tf_op jit(solution)/shard_map/reduce_scatter | solution.py:181
  1614.4 462.0 %reduce-scatter.11.cloned.1.call-start = ((), (), s32[]{:S(2)}) async-start(), calls=%async_computation.9 | async-start | bytes 15728640 | tf_op jit(solution)/shard_map/reduce_scatter | solution.py:146
  1634.2 546.0 %reduce-scatter.17.cloned.1.call-start = ((), (), s32[]{:S(2)}) async-start(), calls=%async_computation.13 | async-start | bytes 1622016 | tf_op jit(solution)/shard_map/reduce_scatter | solution.py:188
  1638.3 314.1 %copy-start.3 = (bf16[1024,1536]{1,0:T(8,128)(2,1)S(1)}, bf16[1024,1536]{1,0:T(8,128)(2,1)}, u32[]{:S(2)}) copy-start(bf16[1024,1536]{1,0:T(8,128)(2,1)} %param.17) | copy-start | bytes 9437188
  1638.3 314.1 %copy-start.15 = (f32[1536]{0:T(1024)S(1)}, f32[1536]{0:T(1024)}, u32[]{:S(2)}) copy-start(f32[1536]{0:T(1024)} %param.18) | copy-start | bytes 18436
  1638.3 314.1 %copy-start.19 = (f32[1024]{0:T(1024)S(1)}, f32[1024]{0:T(1024)}, u32[]{:S(2)}) copy-start(f32[1024]{0:T(1024)} %copy-done.18) | copy-start | bytes 12292
  1642.8 668.4 %all-reduce.21.cloned.1.call-start = ((), (), s32[]{:S(2)}) async-start(), calls=%async_computation.17 | async-start | bytes 183296 | tf_op jit(solution)/shard_map/psum | solution.py:204
  1643.4 317.6 %copy-start.50 = (f32[48]{0:T(128)}, f32[48]{0:T(128)S(1)}, u32[]{:S(2)}) copy-start(f32[48]{0:T(128)S(1)} %multiply_dynamic-update-slice_fusion) | copy-start | bytes 580
  1730.2 346.2 %copy-start.39 = (f32[1024]{0:T(1024)S(1)}, f32[1024]{0:T(1024)}, u32[]{:S(2)}) copy-start(f32[1024]{0:T(1024)} %get-tuple-element.855) | copy-start | bytes 12292
  (134 other events, 2012.1 us)
Sparse Core Ops, SparseCore 0:
  9.7 56.1 all-gather.7
  68.3 126.1 all-gather.5
  196.2 31.6 all-gather.9
  229.5 121.6 all-gather.11
  1495.9 52.4 reduce-scatter.14
  1551.1 30.6 reduce-scatter.18
  1584.8 104.5 all-reduce.18
  1691.7 36.2 reduce-scatter.20
  1731.2 221.1 reduce-scatter.12
  1955.6 120.7 reduce-scatter.10
  2083.1 97.0 reduce-scatter.16
  2188.7 122.4 all-reduce.20
where the time goes:
time: 2340 us; the launch traced here: 2330 us
  waiting for transfers between devices  723 us (31%)
  matrix products  665 us (28%)
  local copies, waits for them, and re-layouts  448 us (19%)
  other arithmetic  350 us (15%)
  blocking collectives  121 us (5%)
    dot_general x24, matrix products, step(): within = jnp.einsum('sqkh,skhp->sqhp', weights, block_x, precision=PRECISE)  228 us
    reduce_scatter x1, waiting for transfers between devices, shards(): lax.psum_scatter(contract(grad_heads, columns, 1, 1), 'tensor', scatter_d...  222 us
    psum x1, waiting for transfers between devices, shards(): lax.psum((grad_norm, conv_full, cbias_full, place(grad_step, step_start,...  131 us
    reduce_scatter x1, waiting for transfers between devices, shards(): lax.psum_scatter(contract(scaled, full_out, 1, 1).astype(jnp.bfloat16), '...  115 us
    dot_general x6, matrix products, contract(): lax.dot_general(left, right, (((left_dim,), (right_dim,)), ((), ())), pre...  108 us
    dot_general x32, matrix products, step(): jnp.einsum('sqn,shpn->sqhp', block_c, state, precision=PRECISE)  107 us
    dot_general x24, matrix products, step(): jnp.einsum('skh,skhp,skn->shpn', to_end, block_x, block_b, precision=PREC...  97.3 us
    reduce_scatter x1, waiting for transfers between devices, shards(): lax.psum_scatter(contract(normed, map_low, 0, 0), ('dp', 'tensor'), scatt...  95.8 us
  transfers between devices with their start and end apart: 12, of which 7 were waited for; matrix products, arithmetic and copies ran while one was open for 24% of the time, Pallas kernels for 0%

commit v1 on v0

v1 whole, which is shorter than its diff:
```python
import functools
import math

import jax
import jax.numpy as jnp
from jax import lax
from jax.experimental import pallas as pl
from jax.experimental.pallas import tpu as pltpu
from jax.sharding import PartitionSpec as P

D = 1536
H = 48
HEAD = 64
NS = 128
KW = 4
LEN = 2048
DI = 3072
EPSILON = 1e-05

CHUNK = 128
HALO = 16
LANES = 128
LOG2E = math.log2(math.e)
NEG = -1e30
VMEM = 58 * 2**20
F32 = jnp.float32
BF16 = jnp.bfloat16
PRECISE = lax.Precision.HIGHEST
NT = (((1,), (1,)), ((), ()))
TN = (((0,), (0,)), ((), ()))


def dot(a, b, dims=(((1,), (0,)), ((), ())), precision=None):
    return lax.dot_general(a, b, dims, precision=precision, preferred_element_type=F32)


def iota(shape, axis):
    return lax.broadcasted_iota(jnp.int32, shape, axis)


def first_half(shape):
    return iota(shape, len(shape) - 1) < HEAD


def mix(columns, head, rows=CHUNK):
    shape = (rows, LANES)
    left = jnp.broadcast_to(columns[:, head : head + 1], shape)
    right = jnp.broadcast_to(columns[:, head + 1 : head + 2], shape)
    return jnp.where(first_half(shape), left, right)


def mix_row(row, head):
    shape = (1, LANES)
    left = jnp.broadcast_to(row[:, head : head + 1], shape)
    right = jnp.broadcast_to(row[:, head + 1 : head + 2], shape)
    return jnp.where(first_half(shape), left, right)


def halves(block):
    left = first_half(block.shape)
    zero = jnp.zeros_like(block)
    return jnp.where(left, block, zero), jnp.where(left, zero, block)


def shifted(block):
    return [pltpu.roll(block, KW - 1 - tap, 0)[HALO:] if tap < KW - 1 else block[HALO:] for tap in range(KW)]


def conv_total(taps, weight, bias):
    total = bias + weight[KW - 1 : KW] * taps[KW - 1]
    for tap in range(KW - 1):
        total = total + weight[tap : tap + 1] * taps[tap]
    return total


def conv_pull(grad, after, weight):
    rows = grad.shape[0]
    ext = jnp.concatenate([grad, after], axis=0)
    out = weight[KW - 1 : KW] * grad
    for ahead in range(1, KW):
        out = out + weight[KW - 1 - ahead : KW - ahead] * pltpu.roll(ext, rows + 8 - ahead, 0)[:rows]
    return out


def fold(block):
    total = block[0:8]
    for at in range(8, block.shape[0], 8):
        total = total + block[at : at + 8]
    return total


def col_sum(block):
    return jnp.sum(block, axis=0, keepdims=True)


def prep_kernel(heads, n_ref, wm_ref, ws_ref, cw_ref, cb_ref, sb_ref, dl_ref, pre_ref, bc_ref, v_ref, c2_ref, cd_ref, c2t_ref, cdt_ref, wf_ref, ei_ref, tot_ref, c2_s, cd_s):
    rows = bc_ref.shape[0]
    groups = c2_ref.shape[0]
    count = rows // CHUNK
    pre_ref[...] = dot(n_ref[...], wm_ref[...]).astype(BF16)
    for at in range(count):
        for pair in range(2):
            cols = slice(pair * LANES, (pair + 1) * LANES)
            block = pre_ref[at * CHUNK : at * CHUNK + CHUNK + HALO, cols].astype(F32)
            total = conv_total(shifted(block), cw_ref[:, cols], cb_ref[:, cols])
            bc_ref[at * CHUNK : (at + 1) * CHUNK, cols] = (total * jax.nn.sigmoid(total)).astype(BF16)
    rate = -jnp.exp(dl_ref[...]) * LOG2E
    lower = (iota((CHUNK, CHUNK), 0) >= iota((CHUNK, CHUNK), 1)).astype(F32)
    raw = dot(n_ref[HALO:], ws_ref[...])
    totals = []
    for at in range(count):
        here = slice(at * CHUNK, (at + 1) * CHUNK)
        v = raw[here] + sb_ref[...]
        delta = jnp.maximum(v, 0.0) + jnp.log1p(jnp.exp(-jnp.abs(v)))
        log_delta = jnp.where(v < -15.0, v, jnp.log(jnp.maximum(delta, 1e-30)))
        c2 = dot(lower, delta * rate, precision=PRECISE)
        cd = c2 - log_delta * LOG2E
        c2_s[here] = c2
        cd_s[here] = cd
        totals.append(c2[CHUNK - 1 : CHUNK])
        v_t, c2_t, cd_t = v.T, c2.T, cd.T
        for g in range(groups):
            own = slice(g * heads, (g + 1) * heads)
            c2_ref[g, here] = c2[:, own]
            cd_ref[g, here] = cd[:, own]
            v_ref[g, :, here] = v_t[own]
            c2t_ref[g, :, here] = c2_t[own]
            cdt_ref[g, :, here] = cd_t[own]
    before = jnp.zeros_like(totals[0])
    for at in range(count):
        here = slice(at * CHUNK, (at + 1) * CHUNK)
        to_here = jnp.exp2(before + c2_s[here])
        before = before + totals[at]
        for g in range(groups):
            ei_ref[g, here] = to_here[:, g * heads : (g + 1) * heads]
    tot_ref[...] = before
    after = jnp.zeros_like(totals[0])
    for at in range(count - 1, -1, -1):
        here = slice(at * CHUNK, (at + 1) * CHUNK)
        after = after + totals[at]
        to_end = jnp.exp2(after - cd_s[here])
        for g in range(groups):
            wf_ref[g, here] = to_end[:, g * heads : (g + 1) * heads]


def prep(normed, map_w, step_w, conv_w, conv_b, step_b, decay_log, groups, heads):
    rows = normed.shape[0] - HALO
    cols = jax.ShapeDtypeStruct((groups, rows, heads), F32)
    flat = jax.ShapeDtypeStruct((groups, heads, rows), F32)
    return pl.pallas_call(
        functools.partial(prep_kernel, heads),
        out_shape=(
            jax.ShapeDtypeStruct((rows + HALO, 2 * NS), BF16),
            jax.ShapeDtypeStruct((rows, 2 * NS), BF16),
            flat,
            cols,
            cols,
            flat,
            flat,
            cols,
            cols,
            jax.ShapeDtypeStruct((1, LANES), F32),
        ),
        scratch_shapes=[pltpu.VMEM((rows, LANES), F32), pltpu.VMEM((rows, LANES), F32)],
        compiler_params=pltpu.CompilerParams(vmem_limit_bytes=VMEM),
        name="prep",
    )(normed, map_w, step_w, conv_w, conv_b, step_b, decay_log)


def proj_kernel(tile, n_ref, w_ref, cw_ref, cb_ref, bc_ref, wf_ref, pre_ref, x_ref, s_ref, xw_s):
    rows, inner = x_ref.shape
    for at in range(0, inner, tile):
        cols = slice(at, at + tile)
        pre_ref[:, cols] = dot(n_ref[...], w_ref[0, :, cols]).astype(BF16)

        def chunk(k, carry, at=at):
            start = pl.multiple_of(k * CHUNK, CHUNK)
            weights = wf_ref[0, pl.ds(start, CHUNK)]
            for q in range(at // LANES, (at + tile) // LANES):
                lanes = slice(q * LANES, (q + 1) * LANES)
                block = pre_ref[pl.ds(start, CHUNK + HALO), lanes].astype(F32)
                total = conv_total(shifted(block), cw_ref[:, lanes], cb_ref[:, lanes])
                x = (total * jax.nn.sigmoid(total)).astype(BF16)
                x_ref[pl.ds(start, CHUNK), lanes] = x
                xw_s[pl.ds(start, CHUNK), lanes] = (x.astype(F32) * mix(weights, 2 * q)).astype(BF16)
            return carry

        lax.fori_loop(0, rows // CHUNK, chunk, 0)
    s_ref[...] = dot(bc_ref[:, :NS], xw_s[...], TN)


def project(normed, weight, conv_w, conv_b, bc, wf):
    ext = normed.shape[0]
    rows = ext - HALO
    groups, _, inner = weight.shape
    heads = inner // HEAD
    tile = 256 if inner % 256 == 0 else LANES
    return pl.pallas_call(
        functools.partial(proj_kernel, tile),
        grid=(groups,),
        in_specs=[
            pl.BlockSpec((ext, D), lambda g: (0, 0)),
            pl.BlockSpec((1, D, inner), lambda g: (g, 0, 0)),
            pl.BlockSpec((KW, inner), lambda g: (0, g)),
            pl.BlockSpec((1, inner), lambda g: (0, g)),
            pl.BlockSpec((rows, 2 * NS), lambda g: (0, 0)),
            pl.BlockSpec((1, rows, heads), lambda g: (g, 0, 0)),
        ],
        out_specs=[
            pl.BlockSpec((ext, inner), lambda g: (0, g)),
            pl.BlockSpec((rows, inner), lambda g: (0, g)),
            pl.BlockSpec((NS, inner), lambda g: (0, g)),
        ],
        out_shape=(
            jax.ShapeDtypeStruct((ext, groups * inner), BF16),
            jax.ShapeDtypeStruct((rows, groups * inner), BF16),
            jax.ShapeDtypeStruct((NS, groups * inner), F32),
        ),
        scratch_shapes=[pltpu.VMEM((rows, inner), BF16)],
        compiler_params=pltpu.CompilerParams(vmem_limit_bytes=VMEM),
        name="project",
    )(normed, weight, conv_w, conv_b, bc, wf)


def scan_kernel(x_ref, bc_ref, c2_ref, cd_ref, cdt_ref, s0_ref, skip_ref, y_ref, sin_ref, state, ya_s, xw_s):
    rows, inner = x_ref.shape
    heads = inner // HEAD
    causal = iota((CHUNK, CHUNK), 0) >= iota((CHUNK, CHUNK), 1)
    state[...] = s0_ref[...]

    def chunk(k, carry):
        start = pl.multiple_of(k * CHUNK, CHUNK)
        here = pl.ds(start, CHUNK)
        in_map, out_map = bc_ref[here, :NS], bc_ref[here, NS:]
        c2, cd = c2_ref[0, here], cd_ref[0, here]
        cd_t = cdt_ref[0, :, here]
        last = c2[CHUNK - 1 : CHUNK]
        from_start, to_end, whole = jnp.exp2(c2), jnp.exp2(last - cd), jnp.exp2(last)
        held = state[...].astype(BF16)
        sin_ref[k] = held
        ya_s[...] = dot(out_map, held)
        scores = dot(out_map, in_map, NT)
        for q in range(heads // 2):
            lanes = slice(q * LANES, (q + 1) * LANES)
            x = x_ref[here, lanes]
            x32 = x.astype(F32)
            weights = []
            for head in (2 * q, 2 * q + 1):
                spread = c2[:, head : head + 1] - cd_t[head : head + 1]
                weights.append((scores * jnp.exp2(jnp.where(causal, spread, NEG))).astype(BF16))
            within = dot(jnp.concatenate(weights, axis=1), jnp.concatenate(halves(x), axis=0))
            y = within + mix(from_start, 2 * q) * ya_s[:, lanes] + skip_ref[:, lanes] * x32
            y_ref[here, lanes] = y.astype(BF16)
            xw_s[:, lanes] = (x32 * mix(to_end, 2 * q)).astype(BF16)
            state[:, lanes] = state[:, lanes] * mix_row(whole, 2 * q)
        state[...] += dot(in_map, xw_s[...], TN)
        return carry

    lax.fori_loop(0, rows // CHUNK, chunk, 0)


def scan(x, bc, c2, cd, cdt, state, skip):
    rows = x.shape[0]
    groups, _, heads = c2.shape
    inner = heads * HEAD
    count = rows // CHUNK
    return pl.pallas_call(
        scan_kernel,
        grid=(groups,),
        in_specs=[
            pl.BlockSpec((rows, inner), lambda g: (0, g)),
            pl.BlockSpec((rows, 2 * NS), lambda g: (0, 0)),
            pl.BlockSpec((1, rows, heads), lambda g: (g, 0, 0)),
            pl.BlockSpec((1, rows, heads), lambda g: (g, 0, 0)),
            pl.BlockSpec((1, heads, rows), lambda g: (g, 0, 0)),
            pl.BlockSpec((NS, inner), lambda g: (0, g)),
            pl.BlockSpec((1, inner), lambda g: (0, g)),
        ],
        out_specs=[
            pl.BlockSpec((rows, inner), lambda g: (0, g)),
            pl.BlockSpec((count, NS, inner), lambda g: (0, 0, g)),
        ],
        out_shape=(
            jax.ShapeDtypeStruct((rows, groups * inner), BF16),
            jax.ShapeDtypeStruct((count, NS, groups * inner), BF16),
        ),
        scratch_shapes=[
            pltpu.VMEM((NS, inner), F32),
            pltpu.VMEM((CHUNK, inner), F32),
            pltpu.VMEM((CHUNK, inner), BF16),
        ],
        compiler_params=pltpu.CompilerParams(vmem_limit_bytes=VMEM),
        name="scan",
    )(x, bc, c2, cd, cdt, state, skip)


def gate_kernel(y_ref, z_ref, cot_ref, hid_ref, w_ref, gain_ref, bc_ref, ei_ref, sc_ref, out_ref, dy_ref, dz_ref, gg_ref, u_ref, gs_s, ga_s, de_s):
    rows = y_ref.shape[0]
    groups, _, inner = w_ref.shape
    tiles = groups * inner // LANES

    @pl.when(pl.program_id(0) == 0)
    def _():
        gg_ref[...] = jnp.zeros_like(gg_ref)
        u_ref[...] = jnp.zeros_like(u_ref)

    for g in range(groups):
        gs_s[:, g * inner : (g + 1) * inner] = dot(cot_ref[...], w_ref[g])
    for part in range(0, rows, CHUNK):
        here = slice(part, part + CHUNK)

        def measure(c, sums):
            lanes = pl.ds(pl.multiple_of(c * LANES, LANES), LANES)
            z = z_ref[here, lanes].astype(F32)
            gated = y_ref[here, lanes].astype(F32) * (z * jax.nn.sigmoid(z))
            ga_s[here, lanes] = gated
            return sums[0] + gated * gated, sums[1] + gs_s[here, lanes] * gain_ref[:, lanes] * gated

        zero = jnp.zeros((CHUNK, LANES), F32)
        squares, dots = lax.fori_loop(0, tiles, measure, (zero, zero))
        inverse = lax.rsqrt(jnp.sum(squares, axis=1, keepdims=True) / DI + EPSILON)
        pull = inverse * inverse * inverse * (jnp.sum(dots, axis=1, keepdims=True) / DI)
        inverse = jnp.broadcast_to(inverse, (CHUNK, LANES))
        pull = jnp.broadcast_to(pull, (CHUNK, LANES))
        for c in range(tiles):
            lanes = slice(c * LANES, (c + 1) * LANES)
            z = z_ref[here, lanes].astype(F32)
            sig = jax.nn.sigmoid(z)
            gated = ga_s[here, lanes]
            weighted = gs_s[here, lanes]
            unit = gated * inverse
            gain = gain_ref[:, lanes]
            sc_ref[here, lanes] = (unit * gain).astype(BF16)
            gg_ref[:, lanes] += fold(weighted * unit)
            grad = inverse * weighted * gain - gated * pull
            dy = (grad * (z * sig)).astype(BF16)
            dy_ref[here, lanes] = dy
            slope = sig * (1.0 + z * (1.0 - sig))
            dz_ref[here, lanes] = (grad * y_ref[here, lanes].astype(F32) * slope).astype(BF16)
            head = c * (LANES // HEAD)
            decay = mix(ei_ref[head * HEAD // inner, here], head % (inner // HEAD))
            de_s[here, lanes] = (dy.astype(F32) * decay).astype(BF16)
    total = hid_ref[...].astype(F32)
    for g in range(groups):
        cols = slice(g * inner, (g + 1) * inner)
        total = total + dot(sc_ref[:, cols], w_ref[g], NT)
        u_ref[:, cols] += dot(bc_ref[:, NS:], de_s[:, cols], TN)
    out_ref[...] = total.astype(BF16)


def gate(y, z, cot, hidden, weight, gain, bc, ei):
    rows = y.shape[0]
    groups, _, inner = weight.shape
    heads = inner // HEAD
    tile = 256
    wide = groups * inner
    row = lambda i: (i, 0)
    fixed = lambda i: (0, 0)
    return pl.pallas_call(
        gate_kernel,
        grid=(rows // tile,),
        in_specs=[
            pl.BlockSpec((tile, wide), row),
            pl.BlockSpec((tile, wide), row),
            pl.BlockSpec((tile, D), row),
            pl.BlockSpec((tile, D), row),
            pl.BlockSpec((groups, D, inner), lambda i: (0, 0, 0), pipeline_mode=pl.Buffered(1)),
            pl.BlockSpec((1, wide), fixed),
            pl.BlockSpec((tile, 2 * NS), row),
            pl.BlockSpec((groups, tile, heads), lambda i: (0, i, 0)),
        ],
        out_specs=[
            pl.BlockSpec((tile, wide), row),
            pl.BlockSpec((tile, D), row),
            pl.BlockSpec((tile, wide), row),
            pl.BlockSpec((tile, wide), row),
            pl.BlockSpec((8, wide), fixed),
            pl.BlockSpec((NS, wide), fixed),
        ],
        out_shape=(
            jax.ShapeDtypeStruct((rows, wide), BF16),
            jax.ShapeDtypeStruct((rows, D), BF16),
            jax.ShapeDtypeStruct((rows, wide), BF16),
            jax.ShapeDtypeStruct((rows, wide), BF16),
            jax.ShapeDtypeStruct((8, wide), F32),
            jax.ShapeDtypeStruct((NS, wide), F32),
        ),
        scratch_shapes=[
            pltpu.VMEM((tile, wide), F32),
            pltpu.VMEM((tile, wide), F32),
            pltpu.VMEM((tile, wide), BF16),
        ],
        compiler_params=pltpu.CompilerParams(vmem_limit_bytes=VMEM),
        name="gate",
    )(y, z, cot, hidden, weight, gain, bc, ei)


def back_kernel(pre_ref, dy_ref, bc_ref, c2_ref, cd_ref, c2t_ref, sin_ref, u_ref, skip_ref, cw_ref, cb_ref, dpre_ref, dbc_ref, acc_ref, q_ref, da_ref, state, next_s, x_s, slope_s, de_s, xw_s, ya_s, bs_s):
    rows, inner = dy_ref.shape
    heads = inner // HEAD
    count = rows // CHUNK
    square = (CHUNK, CHUNK)
    flipped = iota(square, 1) >= iota(square, 0)
    later = (iota(square, 0) >= iota(square, 1)).astype(F32)
    earlier = (iota(square, 0) < iota(square, 1)).astype(F32)
    state[...] = u_ref[...]
    next_s[...] = jnp.zeros_like(next_s)
    acc_ref[...] = jnp.zeros_like(acc_ref)

    @pl.when(pl.program_id(0) == 0)
    def _():
        dbc_ref[...] = jnp.zeros_like(dbc_ref)

    def chunk(step, carry):
        k = count - 1 - step
        start = pl.multiple_of(k * CHUNK, CHUNK)
        here = pl.ds(start, CHUNK)
        in_map, out_map = bc_ref[here, :NS], bc_ref[here, NS:]
        c2, cd = c2_ref[0, here], cd_ref[0, here]
        c2_t = c2t_ref[0, :, here]
        last = c2[CHUNK - 1 : CHUNK]
        from_start, to_end, whole = jnp.exp2(c2), jnp.exp2(last - cd), jnp.exp2(last)
        for q in range(heads // 2):
            lanes = slice(q * LANES, (q + 1) * LANES)
            block = pre_ref[pl.ds(start, CHUNK + HALO), lanes].astype(F32)
            total = conv_total(shifted(block), cw_ref[:, lanes], cb_ref[:, lanes])
            sig = jax.nn.sigmoid(total)
            x = (total * sig).astype(BF16)
            x_s[:, lanes] = x
            slope_s[:, lanes] = sig * (1.0 + total * (1.0 - sig))
            de_s[:, lanes] = (dy_ref[here, lanes].astype(F32) * mix(from_start, 2 * q)).astype(BF16)
            xw_s[:, lanes] = (x.astype(F32) * mix(to_end, 2 * q)).astype(BF16)
        held = sin_ref[k]
        after = state[...]
        after_low = after.astype(BF16)
        ya_s[...] = dot(out_map, held)
        bs_s[...] = dot(in_map, after_low)
        grad_out = dot(de_s[...], held, NT)
        grad_in = dot(xw_s[...], after_low, NT)
        through = col_sum(after * held.astype(F32))
        state[...] = dot(out_map, de_s[...], TN)
        scores = dot(in_map, out_map, NT)
        grad_scores = jnp.zeros(square, F32)
        rc_rows, st_rows, q_rows, tails = [], [], [], []
        for q in range(heads // 2):
            lanes = slice(q * LANES, (q + 1) * LANES)
            x, dy = x_s[:, lanes], dy_ref[here, lanes]
            x_parts, dy_parts = halves(x), halves(dy)
            weights, row_sums = [], []
            for side, head in enumerate((2 * q, 2 * q + 1)):
                spread = c2_t[head : head + 1] - cd[:, head : head + 1]
                decay = jnp.exp2(jnp.where(flipped, spread, NEG))
                weight = (scores * decay).astype(BF16)
                weights.append(weight)
                grad_weight = dot(x_parts[side], dy, NT)
                grad_scores = grad_scores + grad_weight * decay
                row_sums.append(col_sum(weight.astype(F32) * grad_weight))
            dx_in = dot(jnp.concatenate(weights, axis=1), jnp.concatenate(dy_parts, axis=0))
            dx_out = bs_s[:, lanes] * mix(to_end, 2 * q)
            x32, dy32 = x.astype(F32), dy.astype(F32)
            inside = x32 * dx_in
            outside = x32 * dx_out
            crossed = (de_s[:, lanes].astype(F32) * ya_s[:, lanes] - inside).T
            outside_t = outside.T
            both_t = (inside + outside).T
            through_q = through[:, lanes] * mix_row(whole, 2 * q)
            for side in range(2):
                part = slice(side * HEAD, (side + 1) * HEAD)
                rc_rows.append(row_sums[side] + col_sum(crossed[part]))
                st_rows.append(col_sum(outside_t[part]))
                q_rows.append(col_sum(both_t[part]))
                own = first_half((1, LANES)) if side == 0 else ~first_half((1, LANES))
                tails.append(jnp.sum(jnp.where(own, through_q, 0.0), axis=1, keepdims=True))
            state[:, lanes] += after[:, lanes] * mix_row(whole, 2 * q)
            grad = (dx_in + dx_out + skip_ref[:, lanes] * dy32) * slope_s[:, lanes]
            taps = shifted(pre_ref[pl.ds(start, CHUNK + HALO), lanes].astype(F32))
            for tap in range(KW):
                acc_ref[tap * 8 : tap * 8 + 8, lanes] += fold(grad * taps[tap])
            acc_ref[32:40, lanes] += fold(grad)
            acc_ref[40:48, lanes] += fold(dy32 * x32)
            dpre = conv_pull(grad, next_s[:, lanes], cw_ref[:, lanes])
            dpre_ref[pl.ds(pl.multiple_of(start + HALO, HALO), CHUNK), lanes] = dpre.astype(BF16)
            next_s[:, lanes] = grad[0:8]
        low_scores = grad_scores.astype(BF16)
        dbc_ref[here, :NS] += grad_in + dot(low_scores, out_map)
        dbc_ref[here, NS:] += grad_out + dot(low_scores, in_map, TN)
        da = dot(jnp.concatenate(rc_rows, axis=0), later, precision=PRECISE)
        da = da + dot(jnp.concatenate(st_rows, axis=0), earlier, precision=PRECISE)
        da_ref[0, :, here] = da + jnp.concatenate(tails, axis=0)
        q_ref[0, :, here] = jnp.concatenate(q_rows, axis=0)
        return carry

    lax.fori_loop(0, count, chunk, 0)
    for q in range(heads // 2):
        lanes = slice(q * LANES, (q + 1) * LANES)
        empty = jnp.zeros((HALO, LANES), F32)
        dpre_ref[0:HALO, lanes] = conv_pull(empty, next_s[:, lanes], cw_ref[:, lanes]).astype(BF16)


def back(pre, dy, bc, c2, cd, c2t, states, pull, skip, conv_w, conv_b):
    ext = pre.shape[0]
    rows = ext - HALO
    groups, _, heads = c2.shape
    inner = heads * HEAD
    wide = groups * inner
    count = rows // CHUNK
    return pl.pallas_call(
        back_kernel,
        grid=(groups,),
        in_specs=[
            pl.BlockSpec((ext, inner), lambda g: (0, g)),
            pl.BlockSpec((rows, inner), lambda g: (0, g)),
            pl.BlockSpec((rows, 2 * NS), lambda g: (0, 0)),
            pl.BlockSpec((1, rows, heads), lambda g: (g, 0, 0)),
            pl.BlockSpec((1, rows, heads), lambda g: (g, 0, 0)),
            pl.BlockSpec((1, heads, rows), lambda g: (g, 0, 0)),
            pl.BlockSpec((count, NS, inner), lambda g: (0, 0, g)),
            pl.BlockSpec((NS, inner), lambda g: (0, g)),
            pl.BlockSpec((1, inner), lambda g: (0, g)),
            pl.BlockSpec((KW, inner), lambda g: (0, g)),
            pl.BlockSpec((1, inner), lambda g: (0, g)),
        ],
        out_specs=[
            pl.BlockSpec((ext, inner), lambda g: (0, g)),
            pl.BlockSpec((rows, 2 * NS), lambda g: (0, 0)),
            pl.BlockSpec((48, inner), lambda g: (0, g)),
            pl.BlockSpec((1, heads, rows), lambda g: (g, 0, 0)),
            pl.BlockSpec((1, heads, rows), lambda g: (g, 0, 0)),
        ],
        out_shape=(
            jax.ShapeDtypeStruct((ext, wide), BF16),
            jax.ShapeDtypeStruct((rows, 2 * NS), F32),
            jax.ShapeDtypeStruct((48, wide), F32),
            jax.ShapeDtypeStruct((groups, heads, rows), F32),
            jax.ShapeDtypeStruct((groups, heads, rows), F32),
        ),
        scratch_shapes=[
            pltpu.VMEM((NS, inner), F32),
            pltpu.VMEM((8, inner), F32),
            pltpu.VMEM((CHUNK, inner), BF16),
            pltpu.VMEM((CHUNK, inner), F32),
            pltpu.VMEM((CHUNK, inner), BF16),
            pltpu.VMEM((CHUNK, inner), BF16),
            pltpu.VMEM((CHUNK, inner), F32),
            pltpu.VMEM((CHUNK, inner), F32),
        ],
        compiler_params=pltpu.CompilerParams(vmem_limit_bytes=VMEM),
        name="back",
    )(pre, dy, bc, c2, cd, c2t, states, pull, skip, conv_w, conv_b)


def map_back_kernel(pre_ref, grad_ref, cw_ref, cb_ref, dpre_ref, acc_ref, next_s):
    rows, wide = grad_ref.shape
    count = rows // CHUNK
    next_s[...] = jnp.zeros_like(next_s)
    acc_ref[...] = jnp.zeros_like(acc_ref)
    for k in range(count - 1, -1, -1):
        start = k * CHUNK
        for q in range(wide // LANES):
            lanes = slice(q * LANES, (q + 1) * LANES)
            taps = shifted(pre_ref[start : start + CHUNK + HALO, lanes].astype(F32))
            total = conv_total(taps, cw_ref[:, lanes], cb_ref[:, lanes])
            sig = jax.nn.sigmoid(total)
            grad = grad_ref[start : start + CHUNK, lanes] * (sig * (1.0 + total * (1.0 - sig)))
            for tap in range(KW):
                acc_ref[tap * 8 : tap * 8 + 8, lanes] += fold(grad * taps[tap])
            acc_ref[32:40, lanes] += fold(grad)
            dpre = conv_pull(grad, next_s[:, lanes], cw_ref[:, lanes])
            dpre_ref[start + HALO : start + HALO + CHUNK, lanes] = dpre.astype(BF16)
            next_s[:, lanes] = grad[0:8]
    for q in range(wide // LANES):
        lanes = slice(q * LANES, (q + 1) * LANES)
        empty = jnp.zeros((HALO, LANES), F32)
        dpre_ref[0:HALO, lanes] = conv_pull(empty, next_s[:, lanes], cw_ref[:, lanes]).astype(BF16)


def map_back(pre, grad, conv_w, conv_b):
    return pl.pallas_call(
        map_back_kernel,
        out_shape=(jax.ShapeDtypeStruct(pre.shape, BF16), jax.ShapeDtypeStruct((40, pre.shape[1]), F32)),
        scratch_shapes=[pltpu.VMEM((8, pre.shape[1]), F32)],
        compiler_params=pltpu.CompilerParams(vmem_limit_bytes=VMEM),
        name="map_back",
    )(pre, grad, conv_w, conv_b)


def shards(
    tp,
    hidden,
    norm_gain,
    head_weight,
    step_weight,
    map_weight,
    conv_weight,
    conv_bias,
    step_bias,
    decay_log,
    skip_gain,
    gate_gain,
    out_weight,
    cotangent,
):
    rows = hidden.shape[0]
    inner = head_weight.shape[2]
    heads = step_weight.shape[1]
    span = LEN // rows
    forward = [(i, i + 1) for i in range(tp - 1) if (i + 1) % span]
    backward = [(j, i) for i, j in forward]

    halo = lax.ppermute(hidden[rows - HALO :], "tensor", forward)
    everything = ("tensor", "dp")
    gather = lambda part: lax.all_gather(part, everything, axis=0, tiled=True)
    map_full = lax.all_gather(map_weight, ("dp", "tensor"), axis=0, tiled=True)
    step_full = gather(step_weight).reshape(tp, D, heads)
    x_full = gather(head_weight[:, 1]).reshape(tp, D, inner)
    z_full = gather(head_weight[:, 0]).reshape(tp, D, inner)
    out_full = gather(out_weight).reshape(tp, D, inner)

    tokens = jnp.concatenate([halo, hidden], axis=0).astype(F32)
    inverse_ext = lax.rsqrt(jnp.mean(tokens * tokens, axis=-1, keepdims=True) + EPSILON)
    normed_ext = (tokens * inverse_ext * norm_gain).astype(BF16)
    normed = normed_ext[HALO:]

    lane_pad = lambda a: jnp.pad(a, ((0, 0), (0, LANES - H)))
    step_flat = jnp.moveaxis(step_full, 0, 1).reshape(D, H)
    conv_x, bias_x = conv_weight[:, :DI], conv_bias[None, :DI]
    conv_m, bias_m = conv_weight[:, DI:], conv_bias[None, DI:]
    pre_m, bc, v, c2, cd, c2t, cdt, wf, ei, total = prep(
        normed_ext, map_full, lane_pad(step_flat), conv_m, bias_m, lane_pad(step_bias[None]), lane_pad(decay_log[None]), tp, heads
    )
    skip = jnp.repeat(skip_gain, HEAD)[None]
    device_decay = jnp.repeat(jnp.exp2(total[0, :H]), HEAD)[None]

    pre, x, local_state = project(normed_ext, x_full, conv_x, bias_x, bc, wf)
    state = jnp.zeros_like(local_state)
    for _ in range(span - 1):
        state = lax.ppermute(local_state + device_decay * state, "tensor", forward)
    y, states = scan(x, bc, c2, cd, cdt, state, skip)
    z = jnp.einsum("rd,gdi->rgi", normed, z_full, preferred_element_type=F32).astype(BF16).reshape(rows, DI)

    scaled, block_out, dy, dz, gain_sums, local_pull = gate(y, z, cotangent, hidden, out_full, gate_gain[None], bc, ei)
    pull = jnp.zeros_like(local_pull)
    for _ in range(span - 1):
        pull = lax.ppermute(local_pull + device_decay * pull, "tensor", backward)

    def weight_grad(left, right):
        whole = jnp.einsum("rd,rgi->gdi", left, right.reshape(right.shape[0], tp, inner), preferred_element_type=F32)
        whole = whole.astype(BF16).reshape(tp * D, inner)
        return lax.psum_scatter(whole, everything, scatter_dimension=0, tiled=True).astype(F32)

    grad_out = weight_grad(cotangent, scaled)
    grad_z = weight_grad(normed, dz)
    dpre, dbc, sums, q, da = back(pre, dy, bc, c2, cd, c2t, states, pull, skip, conv_x, bias_x)
    dpre_m, sums_m = map_back(pre_m, dbc, conv_m, bias_m)
    grad_x = weight_grad(normed_ext, dpre)

    v, q, da = (a.reshape(H, rows) for a in (v, q, da))
    delta, sig = jax.nn.softplus(v), jax.nn.sigmoid(v)
    rate = -jnp.exp(decay_log)[:, None]
    ratio = jnp.where(v < -15.0, 1.0, sig / jnp.maximum(delta, 1e-30))
    dstep = q * ratio + da * rate * sig
    dstep_low = dstep.astype(BF16)
    grad_step_bias = jnp.sum(dstep, axis=1)
    grad_decay = jnp.sum(da * delta, axis=1) * rate[:, 0]
    grad_skip = jnp.sum(sums[40:48].reshape(8, H, HEAD), axis=(0, 2))
    grad_gain = jnp.sum(gain_sums, axis=0)
    taps = jnp.concatenate([sums[:32], sums_m[:32]], axis=1).reshape(KW, 8, -1).sum(1)
    taps_bias = jnp.concatenate([sums[32:40], sums_m[32:40]], axis=1).sum(0)

    grad_map = dot(normed_ext, dpre_m, TN)
    grad_step = lax.dot_general(normed, dstep_low, (((0,), (1,)), ((), ())), preferred_element_type=F32)
    map_shard = lax.psum_scatter(grad_map, ("dp", "tensor"), scatter_dimension=0, tiled=True)
    grad_step = jnp.moveaxis(grad_step.reshape(D, tp, heads), 1, 0).reshape(tp * D, heads)
    step_shard = lax.psum_scatter(grad_step, everything, scatter_dimension=0, tiled=True)

    dn = jnp.einsum("rgi,gdi->rd", dpre.reshape(-1, tp, inner), x_full, preferred_element_type=F32)
    dn = dn + dot(dpre_m, map_full, NT)
    dn_halo, dn = dn[:HALO], dn[HALO:]
    dn = dn + jnp.einsum("rgi,gdi->rd", dz.reshape(-1, tp, inner), z_full, preferred_element_type=F32)
    dn = dn + lax.dot_general(dstep_low, step_flat, (((0,), (1,)), ((), ())), preferred_element_type=F32)
    dn_next = lax.ppermute(dn_halo, "tensor", backward)
    dn = dn + jnp.pad(dn_next, ((rows - HALO, 0), (0, 0)))

    tokens, inverse = tokens[HALO:], inverse_ext[HALO:]
    scaled_in = dn * norm_gain
    grad_hidden = (
        cotangent.astype(F32)
        + inverse * scaled_in
        - tokens * inverse**3 * jnp.mean(scaled_in * tokens, axis=-1, keepdims=True)
    )
    grad_norm = jnp.sum(dn * tokens * inverse, axis=0)
    flat = jnp.concatenate([grad_norm, taps.reshape(-1), taps_bias, grad_step_bias, grad_decay, grad_skip, grad_gain])
    flat = lax.psum(flat, ("dp", "tensor"))
    wide = DI + 2 * NS
    cuts = [D, KW * wide, wide, H, H, H, DI]
    parts, at = [], 0
    for size in cuts:
        parts.append(flat[at : at + size])
        at += size
    grad_head = jnp.stack([grad_z, grad_x], axis=1)
    return (
        block_out,
        grad_hidden,
        parts[0],
        grad_head,
        step_shard,
        map_shard,
        parts[1].reshape(KW, wide),
        parts[2],
        parts[3],
        parts[4],
        parts[5],
        parts[6],
        grad_out,
    )


def solution(mesh):
    both = ("dp", "tensor")
    placed = (
        P(both, None),
        P(),
        P("dp", None, "tensor"),
        P("dp", "tensor"),
        P(both, None),
        P(),
        P(),
        P(),
        P(),
        P(),
        P(),
        P("dp", "tensor"),
        P(both, None),
    )
    outs = (
        P(both, None),
        P(both, None),
        P(),
        P("dp", None, "tensor"),
        P("dp", "tensor"),
        P(both, None),
        P(),
        P(),
        P(),
        P(),
        P(),
        P(),
        P("dp", "tensor"),
    )
    return jax.shard_map(
        functools.partial(shards, mesh.shape["tensor"]), mesh=mesh, in_specs=placed, out_specs=outs, check_vma=False
    )
```

time: 2340 us -> 1290 us (0.55)
  matrix products: 665 us -> 113 us
  local copies, waits for them, and re-layouts: 448 us -> 107 us
  other arithmetic: 350 us -> 31.5 us
  Pallas kernels: 0 us -> 215 us
  waiting for transfers between devices: 723 us -> 667 us
    dot_general x121 -> x10, matrix products: 665 us -> 113 us  [the longest x3 47.5 us: weight_grad(): jnp.einsum('rd,rgi->gdi', left, right.reshape(right.shape[0], tp, inner),...]
    pallas_call x0 -> x6, Pallas kernels: none -> 215 us  [the longest x1 78.9 us: back(): pl.pallas_call(back_kernel, grid=(groups,), in_specs=[pl.BlockSpec((ext,...]
    psum x1, waiting for transfers between devices: 131 us -> 15.1 us  [shards(): flat = lax.psum(flat, ('dp', 'tensor'))]
    another operation x89 -> x1, other arithmetic: 95.6 us -> 1.13 us  [shards(): grad_head = jnp.stack([grad_z, grad_x], axis=1)]
    reduce_scatter x4, waiting for transfers between devices: 433 us -> 519 us  [the longest x3 419 us: weight_grad(): lax.psum_scatter(whole, everything, scatter_dimension=0, tiled=True)]
    all_gather x4 -> x3, waiting for transfers between devices: 76.3 us -> 0.02 us  [shards(): gather = lambda part: lax.all_gather(part, everything, axis=0, tiled=True)]
    reduce_sum x20 -> x7, other arithmetic: 81 us -> 6.2 us  [the longest x2 2.82 us: shards(): grad_skip = jnp.sum(sums[40:48].reshape(8, H, HEAD), axis=(0, 2))]
    unnamed x120 -> x33, local copies, waits for them, and re-layouts: 85.4 us -> 11.9 us
  transfers between devices with their start and end apart: 12 -> 13, of which waited for: 7 -> 8; matrix products, arithmetic and copies ran while one was open for 24% -> 16% of each run, Pallas kernels for 0% -> 7%
where the time goes in v1:
time: 1290 us; the launch traced here: 1280 us
  waiting for transfers between devices  667 us (52%)
  Pallas kernels  215 us (17%)
  blocking collectives  118 us (9%)
  matrix products  113 us (9%)
  local copies, waits for them, and re-layouts  107 us (8%)
  other arithmetic  31.5 us (2%)
  between operations  14.6 us (1%)
    reduce_scatter x3, waiting for transfers between devices, weight_grad(): lax.psum_scatter(whole, everything, scatter_dimension=0, tiled=True)  419 us
    unnamed x10, waiting for transfers between devices  103 us
    reduce_scatter x1, waiting for transfers between devices, shards(): lax.psum_scatter(grad_map, ('dp', 'tensor'), scatter_dimension=0, tiled=T...  99.7 us
    all_gather x1, blocking collectives, shards(): map_full = lax.all_gather(map_weight, ('dp', 'tensor'), axis=0, tiled=True)  79.4 us
    pallas_call x1, Pallas kernels, back(): pl.pallas_call(back_kernel, grid=(groups,), in_specs=[pl.BlockSpec((ext,...  78.9 us
    dot_general x3, matrix products, weight_grad(): jnp.einsum('rd,rgi->gdi', left, right.reshape(right.shape[0], tp, inner),...  47.5 us
    pallas_call x1, Pallas kernels, gate(): pl.pallas_call(gate_kernel, grid=(rows // tile,), in_specs=[pl.BlockSpec(...  46.5 us
    pallas_call x1, Pallas kernels, project(): pl.pallas_call(functools.partial(proj_kernel, tile), grid=(groups,), in_s...  39.6 us
  transfers between devices with their start and end apart: 13, of which 8 were waited for; matrix products, arithmetic and copies ran while one was open for 16% of the time, Pallas kernels for 7%

profile of v1, /device:TPU:0, one launch (start us, length us, event | category | flops | bytes accessed | tf_op | source)
XLA Modules:
  0.0 1277.1 jit_solution(7184309154627632233)
XLA Ops:
  26.2 79.4 %all_gather.16.wm_ref = bf16[1536,256]{1,0:T(8,128)(2,1)} all-gather(bf16[48,256]{1,0:T(8,128)(2,1)} %param.17), channel_id=1, replica_groups=mesh['dp'=8,'tensor'=4] {'dp','tensor'}, dimensions={0}, use_global_device_ids=true | all-gather | bytes 811008 | tf_op jit(solution)/shard_map/all_gather | solution.py:613
  105.6 38.7 %all-gather.2 = bf16[32,192,12]{1,2,0:T(8,128)(2,1)S(1)} all-gather(bf16[1,192,12]{1,2,0:T(8,128)(2,1)} %bitcast.101), channel_id=1, replica_groups=mesh['dp'=8,'tensor'=4] {'tensor','dp'}, dimensions={0}, use_global_device_ids=true | all-gather | bytes 152064 | tf_op jit(solution)/shard_map/all_gather | solution.py:612
  155.2 11.4 prep.1
  171.0 39.6 %project.1 = (bf16[1040,3072]{1,0:T(8,128)(2,1)}, bf16[1024,3072]{1,0:T(8,128)(2,1)}, f32[128,3072]{1,0:T(8,128)}) custom-call(bf16[1040,1536]{1,0:T(8,128)(2,1)} %multiply_convert_fusion.n_ref, bf16[4,1536,768]{2,1,0:T(8,128)(2,1)} %bitcast.85, f32[4,3072]{1,0:T(4,128)} %slice.80.cw_ref, f32[1,3072]{1,0:T(1,128)} %bitcast.94, ...), custom_call_target="tpu_custom_call" | custom-call | tf_op jit(solution)/shard_map/project/pallas_call | solution.py:198
  216.1 14.4 %convolution_convert_fusion = bf16[1024,4,768]{0,2,1:T(8,128)(2,1)} fusion(bf16[4,1536,768]{2,1,0:T(8,128)(2,1)} %bitcast.102, bf16[1040,1536]{1,0:T(8,128)(2,1)S(1)} %copy-done.1), kind=kOutput, calls=%fused_computation.17 | convolution fusion | flops 9666822144 | bytes 18874368 | tf_op jit(solution)/shard_map/rd,gdi->rgi/dot_general | solution.py:639
  239.1 27.2 %collective-permute-done.1.s0_ref = f32[128,3072]{1,0:T(8,128)} collective-permute-done((f32[128,3072]{1,0:T(8,128)}, f32[128,3072]{1,0:T(8,128)}, u32[]{:S(2)}, u32[]{:S(2)}) %collective-permute-start.1) | collective-permute-done | bytes 1572896 | tf_op jit(solution)/shard_map/ppermute | solution.py:637
  266.4 34.6 %scan.1 = (bf16[1024,3072]{1,0:T(8,128)(2,1)}, bf16[8,128,3072]{2,1,0:T(8,128)(2,1)}) custom-call(bf16[1024,3072]{1,0:T(8,128)(2,1)} %get-tuple-element.43.x_ref, bf16[1024,256]{1,0:T(8,128)(2,1)} %get-tuple-element.41.bc_ref, f32[4,1024,12]{2,1,0:T(8,128)} %get-tuple-element.44.c2_ref, f32[4,1024,12]{2,1,0:T(8,128)} %get-tuple-element.45.cd_ref, ...), custom_call_target="tpu_custom_call" | custom-call | tf_op jit(solution)/shard_map/scan/pallas_call | solution.py:267
  301.0 46.5 %gate.1 = (bf16[1024,3072]{1,0:T(8,128)(2,1)}, bf16[1024,1536]{1,0:T(8,128)(2,1)}, bf16[1024,3072]{1,0:T(8,128)(2,1)}, bf16[1024,3072]{1,0:T(8,128)(2,1)}, f32[8,3072]{1,0:T(8,128)}, /*index=5*/f32[128,3072]{1,0:T(8,128)}) custom-call(bf16[1024,3072]{1,0:T(8,128)(2,1)} %get-tuple-element.49.y_ref, bf16[1024,3072]{1,0:T(8,128)(2,1)} %copy.86.z_ref, ...), custom_call_target="tpu_custom_call" | custom-call | tf_op jit(solution)/shard_map/gate/pallas_call | solution.py:359
  369.6 15.5 %fusion.15 = f32[1024,1536,1]{1,0,2:T(8,128)} fusion(bf16[1024,4,768]{0,2,1:T(8,128)(2,1)} %bitcast.87, bf16[4,1536,768]{2,1,0:T(8,128)(2,1)} %bitcast.103), kind=kOutput, calls=%fused_computation.45 | convolution fusion | flops 9663676416 | bytes 22020096 | tf_op jit(solution)/shard_map/rgi,gdi->rd/dot_general | solution.py:679
  388.1 78.9 %back.1 = (bf16[1040,3072]{1,0:T(8,128)(2,1)}, f32[1024,256]{1,0:T(8,128)}, f32[48,3072]{1,0:T(8,128)}, f32[4,12,1024]{2,1,0:T(8,128)}, f32[4,12,1024]{2,1,0:T(8,128)}) custom-call(bf16[1040,3072]{1,0:T(8,128)(2,1)} %get-tuple-element.52.pre_ref, bf16[1024,3072]{1,0:T(8,128)(2,1)} %get-tuple-element.53.dy_ref, bf16[1024,256]{1,0:T(8,128)(2,1)} %get-tuple-element.41.bc_ref, ...), custom_call_target="tpu_custom_call" | custom-call | tf_op jit(solution)/shard_map/back/pallas_call | solution.py:507
  469.2 15.8 %convolution_bitcast_fusion = f32[1040,1536]{1,0:T(8,128)} fusion(bf16[4,1536,768]{2,1,0:T(8,128)(2,1)} %bitcast.86, bf16[130,4,8,768]{3,2,1,0:T(8,128)(2,1)} %bitcast.104), kind=kOutput, calls=%fused_computation.4 | convolution fusion | flops 9814671360 | bytes 22216704 | tf_op jit(solution)/shard_map/rgi,gdi->rd/dot_general | solution.py:676
  504.9 11.2 multiply_reduce_fusion.1
  522.2 15.2 %convert_bitcast_fusion = bf16[4,1536,768]{1,2,0:T(8,128)(2,1)} fusion(bf16[1024,4,768]{0,2,1:T(8,128)(2,1)} %bitcast.89, bf16[1024,1536]{1,0:T(8,128)(2,1)} %cot_ref.1), kind=kOutput, calls=%fused_computation.1 | convolution fusion | flops 9668395008 | bytes 18874368 | tf_op jit(solution)/shard_map/rd,rgi->gdi/dot_general | solution.py:647
  537.4 12.7 copy.83
  550.2 14.9 %convert_bitcast_fusion.2 = bf16[4,1536,768]{1,2,0:T(8,128)(2,1)} fusion(bf16[1024,4,768]{0,2,1:T(8,128)(2,1)} %bitcast.88, bf16[1040,1536]{1,0:T(8,128)(2,1)S(1)} %copy-done.1), kind=kOutput, calls=%fused_computation.3 | convolution fusion | flops 9668395008 | bytes 18874368 | tf_op jit(solution)/shard_map/rd,rgi->gdi/dot_general | solution.py:647
  565.1 12.7 copy.78
  578.1 17.5 %convert_bitcast_fusion.1 = bf16[4,1536,768]{1,2,0:T(8,128)(2,1)} fusion(bf16[130,4,8,768]{3,2,1,0:T(8,128)(2,1)} %bitcast.105, bf16[1040,1536]{1,0:T(8,128)(2,1)S(1)} %copy-done.1), kind=kOutput, calls=%fused_computation.2 | convolution fusion | flops 9819389952 | bytes 19021824 | tf_op jit(solution)/shard_map/rd,rgi->gdi/dot_general | solution.py:647
  595.6 12.7 copy.80
  621.1 15.1 %all-reduce.6.cloned.1.call-done = f32[21392]{0:T(1024)} async-done(((f32[21392]{0:T(1024)}), f32[21392]{0:T(1024)}) %all-reduce.6.cloned.1.call-update) | async-done | bytes 85584 | tf_op jit(solution)/shard_map/psum | solution.py:693
  643.1 101.8 %reduce-scatter.16.cloned.1.call-done = f32[192,12]{1,0:T(8,128)} async-done(((f32[6144,12]{1,0:T(8,128)}), f32[192,12]{1,0:T(8,128)}) %reduce-scatter.16.cloned.1.call-update) | async-done | bytes 9232
  746.5 138.8 %reduce-scatter.14.cloned.1.call-done = bf16[192,768]{1,0:T(8,128)(2,1)} async-done(((bf16[6144,768]{1,0:T(8,128)(2,1)}), bf16[192,768]{1,0:T(8,128)(2,1)}) %reduce-scatter.14.cloned.1.call-update) | async-done | bytes 294928 | tf_op jit(solution)/shard_map/reduce_scatter | solution.py:649
  887.2 139.7 %reduce-scatter.8.cloned.1.call-done = bf16[192,768]{1,0:T(8,128)(2,1)} async-done(((bf16[6144,768]{1,0:T(8,128)(2,1)}), bf16[192,768]{1,0:T(8,128)(2,1)}) %reduce-scatter.8.cloned.1.call-update) | async-done | bytes 294928 | tf_op jit(solution)/shard_map/reduce_scatter | solution.py:649
  1026.9 140.5 %reduce-scatter.10.cloned.1.call-done = bf16[192,768]{1,0:T(8,128)(2,1)} async-done(((bf16[6144,768]{1,0:T(8,128)(2,1)}), bf16[192,768]{1,0:T(8,128)(2,1)}) %reduce-scatter.10.cloned.1.call-update) | async-done | bytes 294928 | tf_op jit(solution)/shard_map/reduce_scatter | solution.py:649
  1170.5 99.7 %reduce-scatter.12.cloned.1.call-done = f32[48,256]{1,0:T(8,128)} async-done(((f32[1536,256]{1,0:T(8,128)}), f32[48,256]{1,0:T(8,128)}) %reduce-scatter.12.cloned.1.call-update) | async-done | bytes 49168 | tf_op jit(solution)/shard_map/reduce_scatter | solution.py:672
  (123 shorter events, 128.1 us)
Async XLA Ops:
  7.2 144.9 %copy-start = (bf16[1024,1536]{1,0:T(8,128)(2,1)S(1)}, bf16[1024,1536]{1,0:T(8,128)(2,1)}, u32[]{:S(2)}) copy-start(bf16[1024,1536]{1,0:T(8,128)(2,1)} %hid_ref.1) | copy-start | bytes 9437188
  7.2 142.2 %copy-start.12 = (f32[48]{0:T(128)S(1)}, f32[48]{0:T(128)}, u32[]{:S(2)}) copy-start(f32[48]{0:T(128)} %param.22) | copy-start | bytes 580
  7.2 145.7 %copy-start.8 = (f32[1536]{0:T(1024)S(1)}, f32[1536]{0:T(1024)}, u32[]{:S(2)}) copy-start(f32[1536]{0:T(1024)} %param.14) | copy-start | bytes 18436
  7.2 163.8 %all-gather.9.cloned.1.call-start = ((), (), s32[]{:S(2)}) async-start(), calls=%async_computation.11 | async-start | bytes 9732096 | tf_op jit(solution)/shard_map/all_gather | solution.py:612
  11.3 204.8 %all-gather.11.cloned.1.call-start = ((), (), s32[]{:S(2)}) async-start(), calls=%async_computation.12 | async-start | bytes 9732096 | tf_op jit(solution)/shard_map/all_gather | solution.py:612
  13.2 287.8 %all-gather.7.cloned.1.call-start = ((), (), s32[]{:S(2)}) async-start(), calls=%async_computation.5 | async-start | bytes 9732096 | tf_op jit(solution)/shard_map/all_gather | solution.py:612
  13.9 622.3 %all-reduce.6.cloned.1.call-start = ((), (), s32[]{:S(2)}) async-start(), calls=%async_computation.6 | async-start | bytes 172032 | tf_op jit(solution)/shard_map/psum | solution.py:693
  15.4 136.7 %collective-permute-start = (bf16[16,1536]{1,0:T(8,128)(2,1)}, bf16[16,1536]{1,0:T(8,128)(2,1)S(1)}, u32[]{:S(2)}, u32[]{:S(2)}) collective-permute-start(bf16[16,1536]{1,0:T(8,128)(2,1)} %slice.78), channel_id=1, source_target_pairs={{0,1},{2,3},{4,5},{6,7},{8,9},{10,11},{12,13},{14,15},{16,17},{18,... | collective-permute-start | bytes 147464 | tf_op jit(solution)/shard_map/ppermute | solution.py:610
  171.0 45.1 %copy-start.1 = (bf16[1040,1536]{1,0:T(8,128)(2,1)S(1)}, bf16[1040,1536]{1,0:T(8,128)(2,1)}, u32[]{:S(2)}) copy-start(bf16[1040,1536]{1,0:T(8,128)(2,1)} %multiply_convert_fusion.n_ref) | copy-start | bytes 9584644
  213.2 53.1 %collective-permute-start.1 = (f32[128,3072]{1,0:T(8,128)}, f32[128,3072]{1,0:T(8,128)}, u32[]{:S(2)}, u32[]{:S(2)}) collective-permute-start(f32[128,3072]{1,0:T(8,128)} %broadcast_add_fusion.1), channel_id=1, source_target_pairs={{0,1},{2,3},{4,5},{6,7},{8,9},{10,11},{12,13},{14,15},{16,17},{18,... | collective-permute-start | bytes 4718600 | tf_op jit(solution)/shard_map/ppermute | solution.py:637
  350.2 37.9 %collective-permute-start.2 = (f32[128,3072]{1,0:T(8,128)}, f32[128,3072]{1,0:T(8,128)}, u32[]{:S(2)}, u32[]{:S(2)}) collective-permute-start(f32[128,3072]{1,0:T(8,128)} %broadcast_add_fusion), channel_id=1, source_target_pairs={{1,0},{3,2},{5,4},{7,6},{9,8},{11,10},{13,12},{15,14},{17,16},{19,... | collective-permute-start | bytes 4718600 | tf_op jit(solution)/shard_map/ppermute | solution.py:644
  351.5 8.9 copy-start.7
  469.2 19.6 %copy-start.3 = (bf16[1536,256]{1,0:T(8,128)(2,1)S(1)}, bf16[1536,256]{1,0:T(8,128)(2,1)}, u32[]{:S(2)}) copy-start(bf16[1536,256]{1,0:T(8,128)(2,1)} %all_gather.16.wm_ref) | copy-start | bytes 2359300
  488.8 8.9 copy-start.4
  488.8 9.0 copy-start.5
  488.8 9.0 copy-start.6
  488.8 9.4 copy-start.13
  488.8 10.0 copy-start.10
  496.2 8.7 collective-permute-start.3
  517.6 227.3 %reduce-scatter.16.cloned.1.call-start = ((), (), s32[]{:S(2)}) async-start(), calls=%async_computation.13 | async-start | bytes 3244032
  522.2 363.2 %reduce-scatter.14.cloned.1.call-start = ((), (), s32[]{:S(2)}) async-start(), calls=%async_computation.10 | async-start | bytes 9732096 | tf_op jit(solution)/shard_map/reduce_scatter | solution.py:649
  550.2 476.7 %reduce-scatter.8.cloned.1.call-start = ((), (), s32[]{:S(2)}) async-start(), calls=%async_computation.7 | async-start | bytes 9732096 | tf_op jit(solution)/shard_map/reduce_scatter | solution.py:649
  577.8 589.6 %reduce-scatter.10.cloned.1.call-start = ((), (), s32[]{:S(2)}) async-start(), calls=%async_computation.8 | async-start | bytes 9732096 | tf_op jit(solution)/shard_map/reduce_scatter | solution.py:649
  608.4 661.8 %reduce-scatter.12.cloned.1.call-start = ((), (), s32[]{:S(2)}) async-start(), calls=%async_computation.9 | async-start | bytes 1622016 | tf_op jit(solution)/shard_map/reduce_scatter | solution.py:672
  (3 other events, 9.9 us)
Sparse Core Ops, SparseCore 0:
  11.6 93.8 all-gather.8
  108.6 80.8 all-gather.10
  192.5 89.4 all-gather.6
  517.7 118.4 all-reduce.5
  641.5 103.3 reduce-scatter.15
  750.7 134.6 reduce-scatter.13
  892.3 134.5 reduce-scatter.7
  1032.8 134.5 reduce-scatter.9
  1174.1 96.0 reduce-scatter.11

commit v2 on v1

v2 whole, which is shorter than its diff:
```python
import functools
import math

import jax
import jax.numpy as jnp
from jax import lax
from jax.experimental import pallas as pl
from jax.experimental.pallas import tpu as pltpu
from jax.sharding import Mesh
from jax.sharding import PartitionSpec as P

D = 1536
H = 48
HEAD = 64
NS = 128
KW = 4
LEN = 2048
DI = 3072
EPSILON = 1e-05

CHUNK = 128
HALO = 16
TAIL = 112
LANES = 128
LOG2E = math.log2(math.e)
NEG = -1e30
VMEM = 58 * 2**20
F32 = jnp.float32
BF16 = jnp.bfloat16
PRECISE = lax.Precision.HIGHEST
NT = (((1,), (1,)), ((), ()))
TN = (((0,), (0,)), ((), ()))


def dot(a, b, dims=(((1,), (0,)), ((), ())), precision=None):
    return lax.dot_general(a, b, dims, precision=precision, preferred_element_type=F32)


def iota(shape, axis):
    return lax.broadcasted_iota(jnp.int32, shape, axis)


def first_half(shape):
    return iota(shape, len(shape) - 1) < HEAD


def mix(columns, head, rows=CHUNK):
    shape = (rows, LANES)
    left = jnp.broadcast_to(columns[:, head : head + 1], shape)
    right = jnp.broadcast_to(columns[:, head + 1 : head + 2], shape)
    return jnp.where(first_half(shape), left, right)


def mix_row(row, head):
    shape = (1, LANES)
    left = jnp.broadcast_to(row[:, head : head + 1], shape)
    right = jnp.broadcast_to(row[:, head + 1 : head + 2], shape)
    return jnp.where(first_half(shape), left, right)


def halves(block):
    left = first_half(block.shape)
    zero = jnp.zeros_like(block)
    return jnp.where(left, block, zero), jnp.where(left, zero, block)


def shifted(block):
    return [pltpu.roll(block, KW - 1 - tap, 0)[HALO:] if tap < KW - 1 else block[HALO:] for tap in range(KW)]


def conv_total(taps, weight, bias):
    total = bias + weight[KW - 1 : KW] * taps[KW - 1]
    for tap in range(KW - 1):
        total = total + weight[tap : tap + 1] * taps[tap]
    return total


def conv_pull(grad, after, weight):
    rows = grad.shape[0]
    ext = jnp.concatenate([grad, after], axis=0)
    out = weight[KW - 1 : KW] * grad
    for ahead in range(1, KW):
        out = out + weight[KW - 1 - ahead : KW - ahead] * pltpu.roll(ext, rows + 8 - ahead, 0)[:rows]
    return out


def fold(block):
    total = block[0:8]
    for at in range(8, block.shape[0], 8):
        total = total + block[at : at + 8]
    return total


def col_sum(block):
    return jnp.sum(block, axis=0, keepdims=True)


def cost(us):
    return pl.CostEstimate(flops=0, bytes_accessed=int(us), transcendentals=0)


def times(left_ref, blocks):
    total, at = None, 0
    for block in blocks:
        term = dot(left_ref[:, at : at + block.shape[0]], block[...])
        total = term if total is None else total + term
        at += block.shape[0]
    return total


def split(refs, counts):
    out, at = [], 0
    for count in counts:
        out.append(refs[at : at + count])
        at += count
    return out


def place_spec(place):
    array, index = place
    return pl.BlockSpec((D // 2, array.shape[1]), lambda *_: (index, 0), pipeline_mode=pl.Buffered(1))


def whole_spec(array):
    return pl.BlockSpec(array.shape, lambda *_: (0,) * array.ndim, pipeline_mode=pl.Buffered(1))


def prep_kernel(heads, pitch, n_ref, wm_ref, ws_ref, cw_ref, cb_ref, sb_ref, dl_ref, pre_ref, bc_ref, v_ref, c2_ref, cd_ref, c2t_ref, cdt_ref, wf_ref, ei_ref, tot_ref, c2_s, cd_s):
    rows = bc_ref.shape[0]
    groups = c2_ref.shape[0]
    count = rows // CHUNK
    pre_ref[...] = dot(n_ref[...], wm_ref[...]).astype(BF16)
    for at in range(count):
        for pair in range(2):
            cols = slice(pair * LANES, (pair + 1) * LANES)
            block = pre_ref[at * CHUNK : at * CHUNK + CHUNK + HALO, cols].astype(F32)
            total = conv_total(shifted(block), cw_ref[:, cols], cb_ref[:, cols])
            bc_ref[at * CHUNK : (at + 1) * CHUNK, cols] = (total * jax.nn.sigmoid(total)).astype(BF16)
    rate = -jnp.exp(dl_ref[...]) * LOG2E
    lower = (iota((CHUNK, CHUNK), 0) >= iota((CHUNK, CHUNK), 1)).astype(F32)
    raw = dot(n_ref[HALO:], ws_ref[...], NT)
    totals = []
    for at in range(count):
        here = slice(at * CHUNK, (at + 1) * CHUNK)
        v = raw[here] + sb_ref[...]
        delta = jnp.maximum(v, 0.0) + jnp.log1p(jnp.exp(-jnp.abs(v)))
        log_delta = jnp.where(v < -15.0, v, jnp.log(jnp.maximum(delta, 1e-30)))
        c2 = dot(lower, delta * rate, precision=PRECISE)
        cd = c2 - log_delta * LOG2E
        c2_s[here] = c2
        cd_s[here] = cd
        totals.append(c2[CHUNK - 1 : CHUNK])
        v_t, c2_t, cd_t = v.T, c2.T, cd.T
        for g in range(groups):
            own = slice(g * pitch, g * pitch + heads)
            c2_ref[g, here] = c2[:, own]
            cd_ref[g, here] = cd[:, own]
            v_ref[g, :, here] = v_t[own]
            c2t_ref[g, :, here] = c2_t[own]
            cdt_ref[g, :, here] = cd_t[own]
    before = jnp.zeros_like(totals[0])
    for at in range(count):
        here = slice(at * CHUNK, (at + 1) * CHUNK)
        to_here = jnp.exp2(before + c2_s[here])
        before = before + totals[at]
        for g in range(groups):
            ei_ref[g, here] = to_here[:, g * pitch : g * pitch + heads]
    tot_ref[...] = before
    after = jnp.zeros_like(totals[0])
    for at in range(count - 1, -1, -1):
        here = slice(at * CHUNK, (at + 1) * CHUNK)
        after = after + totals[at]
        to_end = jnp.exp2(after - cd_s[here])
        for g in range(groups):
            wf_ref[g, here] = to_end[:, g * pitch : g * pitch + heads]


def prep(normed, map_w, step_w, conv_w, conv_b, step_b, decay_log, groups, heads, pitch):
    rows = normed.shape[0] - HALO - TAIL
    cols = jax.ShapeDtypeStruct((groups, rows, heads), F32)
    flat = jax.ShapeDtypeStruct((groups, heads, rows), F32)
    return pl.pallas_call(
        functools.partial(prep_kernel, heads, pitch),
        out_shape=(
            jax.ShapeDtypeStruct((rows + HALO, 2 * NS), BF16),
            jax.ShapeDtypeStruct((rows, 2 * NS), BF16),
            flat,
            cols,
            cols,
            flat,
            flat,
            cols,
            cols,
            jax.ShapeDtypeStruct((1, LANES), F32),
        ),
        grid=(1,),
        in_specs=[pl.BlockSpec((rows + HALO, D), lambda i: (0, 0))]
        + [whole_spec(a) for a in (map_w, step_w, conv_w, conv_b, step_b, decay_log)],
        scratch_shapes=[pltpu.VMEM((rows, LANES), F32), pltpu.VMEM((rows, LANES), F32)],
        compiler_params=pltpu.CompilerParams(vmem_limit_bytes=VMEM),
        cost_estimate=cost(11),
        name="prep",
    )(normed, map_w, step_w, conv_w, conv_b, step_b, decay_log)


def proj_kernel(tile, count, n_ref, *refs):
    blocks = refs[:count]
    cw_ref, cb_ref, bc_ref, wf_ref, pre_ref, x_ref, s_ref, xw_s = refs[count:]
    rows, inner = x_ref.shape
    for at in range(0, inner, tile):
        cols = slice(at, at + tile)
        pre_ref[:, cols] = times(n_ref, [block.at[:, cols] for block in blocks]).astype(BF16)

        def chunk(k, carry, at=at):
            start = pl.multiple_of(k * CHUNK, CHUNK)
            weights = wf_ref[0, pl.ds(start, CHUNK)]
            for q in range(at // LANES, (at + tile) // LANES):
                lanes = slice(q * LANES, (q + 1) * LANES)
                block = pre_ref[pl.ds(start, CHUNK + HALO), lanes].astype(F32)
                total = conv_total(shifted(block), cw_ref[:, lanes], cb_ref[:, lanes])
                x = (total * jax.nn.sigmoid(total)).astype(BF16)
                x_ref[pl.ds(start, CHUNK), lanes] = x
                xw_s[pl.ds(start, CHUNK), lanes] = (x.astype(F32) * mix(weights, 2 * q)).astype(BF16)
            return carry

        lax.fori_loop(0, rows // CHUNK, chunk, 0)
    s_ref[...] = dot(bc_ref[:, :NS], xw_s[...], TN).astype(BF16)


def project(g, normed, blocks, conv_w, conv_b, bc, wf):
    rows = normed.shape[0] - HALO - TAIL
    ext = rows + HALO
    inner = blocks[0][0].shape[1]
    heads = inner // HEAD
    tile = 256 if inner % 256 == 0 else LANES
    return pl.pallas_call(
        functools.partial(proj_kernel, tile, len(blocks)),
        grid=(1,),
        in_specs=[
            pl.BlockSpec((ext, D), lambda i: (0, 0)),
            *map(place_spec, blocks),
            pl.BlockSpec((KW, inner), lambda i: (0, g)),
            pl.BlockSpec((1, inner), lambda i: (0, g)),
            whole_spec(bc),
            pl.BlockSpec((1, rows, heads), lambda i: (g, 0, 0)),
        ],
        out_specs=[
            pl.BlockSpec((ext, inner), lambda i: (0, 0)),
            pl.BlockSpec((rows, inner), lambda i: (0, 0)),
            pl.BlockSpec((NS, inner), lambda i: (0, 0)),
        ],
        out_shape=(
            jax.ShapeDtypeStruct((ext, inner), BF16),
            jax.ShapeDtypeStruct((rows, inner), BF16),
            jax.ShapeDtypeStruct((NS, inner), BF16),
        ),
        scratch_shapes=[pltpu.VMEM((rows, inner), BF16)],
        compiler_params=pltpu.CompilerParams(vmem_limit_bytes=VMEM),
        cost_estimate=cost(10),
        name="project",
    )(normed, *(array for array, _ in blocks), conv_w, conv_b, bc, wf)


def product_kernel(count, n_ref, *refs):
    refs[count][...] = times(n_ref, refs[:count]).astype(BF16)


def product(left, blocks):
    rows = left.shape[0]
    inner = blocks[0][0].shape[1]
    tile = 256 if inner % 256 == 0 else LANES
    return pl.pallas_call(
        functools.partial(product_kernel, len(blocks)),
        grid=(inner // tile,),
        in_specs=[whole_spec(left), *(pl.BlockSpec((D // 2, tile), functools.partial(lambda index, j: (index, j), index)) for _, index in blocks)],
        out_specs=pl.BlockSpec((rows, tile), lambda j: (0, j)),
        out_shape=jax.ShapeDtypeStruct((rows, inner), BF16),
        compiler_params=pltpu.CompilerParams(vmem_limit_bytes=VMEM),
        cost_estimate=cost(4),
        name="product",
    )(left, *(array for array, _ in blocks))


def scan_kernel(x_ref, bc_ref, c2_ref, cd_ref, cdt_ref, s0_ref, skip_ref, y_ref, sin_ref, state, ya_s, xw_s):
    rows, inner = x_ref.shape
    heads = inner // HEAD
    causal = iota((CHUNK, CHUNK), 0) >= iota((CHUNK, CHUNK), 1)
    state[...] = s0_ref[...].astype(F32)

    def chunk(k, carry):
        start = pl.multiple_of(k * CHUNK, CHUNK)
        here = pl.ds(start, CHUNK)
        in_map, out_map = bc_ref[here, :NS], bc_ref[here, NS:]
        c2, cd = c2_ref[0, here], cd_ref[0, here]
        cd_t = cdt_ref[0, :, here]
        last = c2[CHUNK - 1 : CHUNK]
        from_start, to_end, whole = jnp.exp2(c2), jnp.exp2(last - cd), jnp.exp2(last)
        held = state[...].astype(BF16)
        sin_ref[k] = held
        ya_s[...] = dot(out_map, held)
        scores = dot(out_map, in_map, NT)
        for q in range(heads // 2):
            lanes = slice(q * LANES, (q + 1) * LANES)
            x = x_ref[here, lanes]
            x32 = x.astype(F32)
            weights = []
            for head in (2 * q, 2 * q + 1):
                spread = c2[:, head : head + 1] - cd_t[head : head + 1]
                weights.append((scores * jnp.exp2(jnp.where(causal, spread, NEG))).astype(BF16))
            within = dot(jnp.concatenate(weights, axis=1), jnp.concatenate(halves(x), axis=0))
            y = within + mix(from_start, 2 * q) * ya_s[:, lanes] + skip_ref[:, lanes] * x32
            y_ref[here, lanes] = y.astype(BF16)
            xw_s[:, lanes] = (x32 * mix(to_end, 2 * q)).astype(BF16)
            state[:, lanes] = state[:, lanes] * mix_row(whole, 2 * q)
        state[...] += dot(in_map, xw_s[...], TN)
        return carry

    lax.fori_loop(0, rows // CHUNK, chunk, 0)


def scan(g, x, bc, c2, cd, cdt, state, skip):
    rows = x.shape[0]
    heads = c2.shape[2]
    inner = heads * HEAD
    count = rows // CHUNK
    return pl.pallas_call(
        scan_kernel,
        grid=(1,),
        in_specs=[
            whole_spec(x),
            whole_spec(bc),
            pl.BlockSpec((1, rows, heads), lambda i: (g, 0, 0)),
            pl.BlockSpec((1, rows, heads), lambda i: (g, 0, 0)),
            pl.BlockSpec((1, heads, rows), lambda i: (g, 0, 0)),
            whole_spec(state),
            pl.BlockSpec((1, inner), lambda i: (0, g)),
        ],
        out_specs=[
            pl.BlockSpec((rows, inner), lambda i: (0, 0)),
            pl.BlockSpec((count, NS, inner), lambda i: (0, 0, 0)),
        ],
        out_shape=(
            jax.ShapeDtypeStruct((rows, inner), BF16),
            jax.ShapeDtypeStruct((count, NS, inner), BF16),
        ),
        scratch_shapes=[
            pltpu.VMEM((NS, inner), F32),
            pltpu.VMEM((CHUNK, inner), F32),
            pltpu.VMEM((CHUNK, inner), BF16),
        ],
        compiler_params=pltpu.CompilerParams(vmem_limit_bytes=VMEM),
        cost_estimate=cost(9),
        name="scan",
    )(x, bc, c2, cd, cdt, state, skip)


def gate_kernel(groups, width, out_counts, z_counts, *refs):
    ys, zs, outs_w, zs_w, rest, scs, dys, dzs, us, tail = split(
        refs, (groups, groups, sum(out_counts), sum(z_counts), 6, groups, groups, groups, groups, 8)
    )
    outs_w, zs_w = split(outs_w, out_counts), split(zs_w, z_counts)
    cot_ref, hid_ref, gain_ref, bc_ref, ei_ref, flag_ref = rest
    out_ref, dn_ref, gg_ref, gs_s, ga_s, de_s, sum_s, u_s = tail
    rows, inner = ys[0].shape
    tiles = inner // LANES

    @pl.when(pl.program_id(0) == 0)
    def _():
        gg_ref[...] = jnp.zeros_like(gg_ref)
        u_s[...] = jnp.zeros_like(u_s)

    for g in range(groups):
        gs_s[:, g * inner : (g + 1) * inner] = times(cot_ref, outs_w[g])
    for part in range(0, rows, CHUNK):
        here = slice(part, part + CHUNK)
        squares = jnp.zeros((CHUNK, LANES), F32)
        dots = jnp.zeros((CHUNK, LANES), F32)
        for g in range(groups):

            def measure(c, sums, g=g):
                lanes = pl.ds(pl.multiple_of(c * LANES, LANES), LANES)
                wide = pl.ds(pl.multiple_of(g * inner + c * LANES, LANES), LANES)
                z = zs[g][here, lanes].astype(F32)
                gated = ys[g][here, lanes].astype(F32) * (z * jax.nn.sigmoid(z))
                ga_s[here, wide] = gated
                return sums[0] + gated * gated, sums[1] + gs_s[here, wide] * gain_ref[:, wide] * gated

            squares, dots = lax.fori_loop(0, tiles, measure, (squares, dots))
        inverse = lax.rsqrt(jnp.sum(squares, axis=1, keepdims=True) / DI + EPSILON)
        pull = inverse * inverse * inverse * (jnp.sum(dots, axis=1, keepdims=True) / DI)
        inverse = jnp.broadcast_to(inverse, (CHUNK, LANES))
        pull = jnp.broadcast_to(pull, (CHUNK, LANES))
        for g in range(groups):
            for c in range(tiles):
                lanes = slice(c * LANES, (c + 1) * LANES)
                wide = slice(g * inner + c * LANES, g * inner + (c + 1) * LANES)
                z = zs[g][here, lanes].astype(F32)
                sig = jax.nn.sigmoid(z)
                gated = ga_s[here, wide]
                weighted = gs_s[here, wide]
                unit = gated * inverse
                gain = gain_ref[:, wide]
                scs[g][here, lanes] = (unit * gain).astype(BF16)
                gg_ref[:, wide] += fold(weighted * unit)
                grad = inverse * weighted * gain - gated * pull
                dy = (grad * (z * sig)).astype(BF16)
                dys[g][here, lanes] = dy
                slope = sig * (1.0 + z * (1.0 - sig))
                dzs[g][here, lanes] = (grad * ys[g][here, lanes].astype(F32) * slope).astype(BF16)
                de_s[here, wide] = (dy.astype(F32) * mix(ei_ref[g, here], 2 * c)).astype(BF16)
    for g in range(groups):
        cols = slice(g * inner, (g + 1) * inner)
        u_s[:, cols] += dot(bc_ref[:, NS:], de_s[:, cols], TN)
        us[g][...] = u_s[:, cols].astype(BF16)
    back_times(sum_s, scs, outs_w, hid_ref)
    natural(out_ref, sum_s, flag_ref, width)
    back_times(dn_ref, dzs, zs_w, None)


def natural(out_ref, source_ref, flag_ref, width):
    first = flag_ref[0:1, 0:1] == 0.0
    half = source_ref.shape[1] // 2
    for z in range(half // width):
        own = source_ref[:, z * width : (z + 1) * width]
        other = source_ref[:, half + z * width : half + (z + 1) * width]
        pair = jnp.concatenate([jnp.where(first, own, other), jnp.where(first, other, own)], axis=1)
        out_ref[:, 2 * z * width : 2 * (z + 1) * width] = pair.astype(out_ref.dtype)


def back_times(out_ref, lefts, weights, base_ref):
    cuts = sorted({0} | {sum(b.shape[0] for b in blocks[: i + 1]) for blocks in weights for i in range(len(blocks))})
    for low, high in zip(cuts[:-1], cuts[1:]):
        total = None if base_ref is None else base_ref[:, low:high].astype(F32)
        for left, blocks in zip(lefts, weights):
            at = 0
            for block in blocks:
                if at <= low < at + block.shape[0]:
                    term = dot(left[...], block[low - at : high - at], NT)
                    total = term if total is None else total + term
                at += block.shape[0]
        out_ref[:, low:high] = total.astype(out_ref.dtype)


def arrays(places):
    return [array for array, _ in flat(places)]


def flat(lists):
    return [item for items in lists for item in items]


def gate(ys, zs, outs_w, zs_w, cot, hidden, gain, bc, ei, flag, width):
    groups = len(ys)
    rows, inner = ys[0].shape
    heads = inner // HEAD
    tile = 256
    wide = groups * inner
    row = lambda i: (i, 0)
    fixed = lambda i: (0, 0)
    group = [pl.BlockSpec((tile, inner), row)] * groups
    group_shape = [jax.ShapeDtypeStruct((rows, inner), BF16)] * groups
    out = pl.pallas_call(
        functools.partial(gate_kernel, groups, width, tuple(map(len, outs_w)), tuple(map(len, zs_w))),
        grid=(rows // tile,),
        in_specs=[
            *group,
            *group,
            *map(place_spec, flat(outs_w)),
            *map(place_spec, flat(zs_w)),
            pl.BlockSpec((tile, D), row),
            pl.BlockSpec((tile, D), row),
            pl.BlockSpec((1, wide), fixed),
            pl.BlockSpec((tile, 2 * NS), row),
            pl.BlockSpec((groups, tile, heads), lambda i: (0, i, 0)),
            whole_spec(flag),
        ],
        out_specs=[
            *group,
            *group,
            *group,
            *[pl.BlockSpec((NS, inner), fixed)] * groups,
            pl.BlockSpec((tile, D), row),
            pl.BlockSpec((tile, D), row),
            pl.BlockSpec((8, wide), fixed),
        ],
        out_shape=(
            *group_shape,
            *group_shape,
            *group_shape,
            *[jax.ShapeDtypeStruct((NS, inner), BF16)] * groups,
            jax.ShapeDtypeStruct((rows, D), BF16),
            jax.ShapeDtypeStruct((rows, D), F32),
            jax.ShapeDtypeStruct((8, wide), F32),
        ),
        scratch_shapes=[
            pltpu.VMEM((tile, wide), F32),
            pltpu.VMEM((tile, wide), F32),
            pltpu.VMEM((tile, wide), BF16),
            pltpu.VMEM((tile, D), F32),
            pltpu.VMEM((NS, wide), F32),
        ],
        compiler_params=pltpu.CompilerParams(vmem_limit_bytes=VMEM),
        cost_estimate=cost(55),
        name="gate",
    )(*ys, *zs, *arrays(outs_w), *arrays(zs_w), cot, hidden, gain, bc, ei, flag)
    return split(out, (groups, groups, groups, groups)) + list(out[4 * groups :])


def back_kernel(pre_ref, dy_ref, bc_ref, c2_ref, cd_ref, c2t_ref, sin_ref, u_ref, skip_ref, cw_ref, cb_ref, dpre_ref, dbc_ref, acc_ref, q_ref, da_ref, state, next_s, x_s, slope_s, de_s, xw_s, ya_s, bs_s):
    rows, inner = dy_ref.shape
    heads = inner // HEAD
    count = rows // CHUNK
    square = (CHUNK, CHUNK)
    flipped = iota(square, 1) >= iota(square, 0)
    later = (iota(square, 0) >= iota(square, 1)).astype(F32)
    earlier = (iota(square, 0) < iota(square, 1)).astype(F32)
    state[...] = u_ref[...].astype(F32)
    next_s[...] = jnp.zeros_like(next_s)
    acc_ref[...] = jnp.zeros_like(acc_ref)

    def chunk(step, carry):
        k = count - 1 - step
        start = pl.multiple_of(k * CHUNK, CHUNK)
        here = pl.ds(start, CHUNK)
        in_map, out_map = bc_ref[here, :NS], bc_ref[here, NS:]
        c2, cd = c2_ref[0, here], cd_ref[0, here]
        c2_t = c2t_ref[0, :, here]
        last = c2[CHUNK - 1 : CHUNK]
        from_start, to_end, whole = jnp.exp2(c2), jnp.exp2(last - cd), jnp.exp2(last)
        for q in range(heads // 2):
            lanes = slice(q * LANES, (q + 1) * LANES)
            block = pre_ref[pl.ds(start, CHUNK + HALO), lanes].astype(F32)
            total = conv_total(shifted(block), cw_ref[:, lanes], cb_ref[:, lanes])
            sig = jax.nn.sigmoid(total)
            x = (total * sig).astype(BF16)
            x_s[:, lanes] = x
            slope_s[:, lanes] = sig * (1.0 + total * (1.0 - sig))
            de_s[:, lanes] = (dy_ref[here, lanes].astype(F32) * mix(from_start, 2 * q)).astype(BF16)
            xw_s[:, lanes] = (x.astype(F32) * mix(to_end, 2 * q)).astype(BF16)
        held = sin_ref[k]
        after = state[...]
        after_low = after.astype(BF16)
        ya_s[...] = dot(out_map, held)
        bs_s[...] = dot(in_map, after_low)
        grad_out = dot(de_s[...], held, NT)
        grad_in = dot(xw_s[...], after_low, NT)
        through = col_sum(after * held.astype(F32))
        state[...] = dot(out_map, de_s[...], TN)
        scores = dot(in_map, out_map, NT)
        grad_scores = jnp.zeros(square, F32)
        rc_rows, st_rows, q_rows, tails = [], [], [], []
        for q in range(heads // 2):
            lanes = slice(q * LANES, (q + 1) * LANES)
            x, dy = x_s[:, lanes], dy_ref[here, lanes]
            x_parts, dy_parts = halves(x), halves(dy)
            weights, row_sums = [], []
            for side, head in enumerate((2 * q, 2 * q + 1)):
                spread = c2_t[head : head + 1] - cd[:, head : head + 1]
                decay = jnp.exp2(jnp.where(flipped, spread, NEG))
                weight = (scores * decay).astype(BF16)
                weights.append(weight)
                grad_weight = dot(x_parts[side], dy, NT)
                grad_scores = grad_scores + grad_weight * decay
                row_sums.append(col_sum(weight.astype(F32) * grad_weight))
            dx_in = dot(jnp.concatenate(weights, axis=1), jnp.concatenate(dy_parts, axis=0))
            dx_out = bs_s[:, lanes] * mix(to_end, 2 * q)
            x32, dy32 = x.astype(F32), dy.astype(F32)
            inside = x32 * dx_in
            outside = x32 * dx_out
            crossed = (de_s[:, lanes].astype(F32) * ya_s[:, lanes] - inside).T
            outside_t = outside.T
            both_t = (inside + outside).T
            through_q = through[:, lanes] * mix_row(whole, 2 * q)
            for side in range(2):
                part = slice(side * HEAD, (side + 1) * HEAD)
                rc_rows.append(row_sums[side] + col_sum(crossed[part]))
                st_rows.append(col_sum(outside_t[part]))
                q_rows.append(col_sum(both_t[part]))
                own = first_half((1, LANES)) if side == 0 else ~first_half((1, LANES))
                tails.append(jnp.sum(jnp.where(own, through_q, 0.0), axis=1, keepdims=True))
            state[:, lanes] += after[:, lanes] * mix_row(whole, 2 * q)
            grad = (dx_in + dx_out + skip_ref[:, lanes] * dy32) * slope_s[:, lanes]
            taps = shifted(pre_ref[pl.ds(start, CHUNK + HALO), lanes].astype(F32))
            for tap in range(KW):
                acc_ref[tap * 8 : tap * 8 + 8, lanes] += fold(grad * taps[tap])
            acc_ref[32:40, lanes] += fold(grad)
            acc_ref[40:48, lanes] += fold(dy32 * x32)
            dpre = conv_pull(grad, next_s[:, lanes], cw_ref[:, lanes])
            dpre_ref[pl.ds(pl.multiple_of(start + HALO, HALO), CHUNK), lanes] = dpre.astype(BF16)
            next_s[:, lanes] = grad[0:8]
        low_scores = grad_scores.astype(BF16)
        dbc_ref[here, :NS] = grad_in + dot(low_scores, out_map)
        dbc_ref[here, NS:] = grad_out + dot(low_scores, in_map, TN)
        da = dot(jnp.concatenate(rc_rows, axis=0), later, precision=PRECISE)
        da = da + dot(jnp.concatenate(st_rows, axis=0), earlier, precision=PRECISE)
        da_ref[0, :, here] = da + jnp.concatenate(tails, axis=0)
        q_ref[0, :, here] = jnp.concatenate(q_rows, axis=0)
        return carry

    lax.fori_loop(0, count, chunk, 0)
    for q in range(heads // 2):
        lanes = slice(q * LANES, (q + 1) * LANES)
        empty = jnp.zeros((HALO, LANES), F32)
        dpre_ref[0:HALO, lanes] = conv_pull(empty, next_s[:, lanes], cw_ref[:, lanes]).astype(BF16)
    dpre_ref[HALO + rows :] = jnp.zeros((TAIL, inner), BF16)


def back(g, pre, dy, bc, c2, cd, c2t, states, pull, skip, conv_w, conv_b):
    ext = pre.shape[0]
    rows = ext - HALO
    heads = c2.shape[2]
    inner = heads * HEAD
    count = rows // CHUNK
    return pl.pallas_call(
        back_kernel,
        grid=(1,),
        in_specs=[
            whole_spec(pre),
            whole_spec(dy),
            whole_spec(bc),
            pl.BlockSpec((1, rows, heads), lambda i: (g, 0, 0)),
            pl.BlockSpec((1, rows, heads), lambda i: (g, 0, 0)),
            pl.BlockSpec((1, heads, rows), lambda i: (g, 0, 0)),
            whole_spec(states),
            whole_spec(pull),
            pl.BlockSpec((1, inner), lambda i: (0, g)),
            pl.BlockSpec((KW, inner), lambda i: (0, g)),
            pl.BlockSpec((1, inner), lambda i: (0, g)),
        ],
        out_specs=[
            pl.BlockSpec((ext + TAIL, inner), lambda i: (0, 0)),
            pl.BlockSpec((rows, 2 * NS), lambda i: (0, 0)),
            pl.BlockSpec((48, inner), lambda i: (0, 0)),
            pl.BlockSpec((1, heads, rows), lambda i: (0, 0, 0)),
            pl.BlockSpec((1, heads, rows), lambda i: (0, 0, 0)),
        ],
        out_shape=(
            jax.ShapeDtypeStruct((ext + TAIL, inner), BF16),
            jax.ShapeDtypeStruct((rows, 2 * NS), F32),
            jax.ShapeDtypeStruct((48, inner), F32),
            jax.ShapeDtypeStruct((1, heads, rows), F32),
            jax.ShapeDtypeStruct((1, heads, rows), F32),
        ),
        scratch_shapes=[
            pltpu.VMEM((NS, inner), F32),
            pltpu.VMEM((8, inner), F32),
            pltpu.VMEM((CHUNK, inner), BF16),
            pltpu.VMEM((CHUNK, inner), F32),
            pltpu.VMEM((CHUNK, inner), BF16),
            pltpu.VMEM((CHUNK, inner), BF16),
            pltpu.VMEM((CHUNK, inner), F32),
            pltpu.VMEM((CHUNK, inner), F32),
        ],
        compiler_params=pltpu.CompilerParams(vmem_limit_bytes=VMEM),
        cost_estimate=cost(18),
        name="back",
    )(pre, dy, bc, c2, cd, c2t, states, pull, skip, conv_w, conv_b)


def map_back_kernel(pre_ref, grad_ref, cw_ref, cb_ref, dpre_ref, acc_ref, next_s):
    rows, wide = grad_ref.shape
    count = rows // CHUNK
    next_s[...] = jnp.zeros_like(next_s)
    acc_ref[...] = jnp.zeros_like(acc_ref)
    for k in range(count - 1, -1, -1):
        start = k * CHUNK
        for q in range(wide // LANES):
            lanes = slice(q * LANES, (q + 1) * LANES)
            taps = shifted(pre_ref[start : start + CHUNK + HALO, lanes].astype(F32))
            total = conv_total(taps, cw_ref[:, lanes], cb_ref[:, lanes])
            sig = jax.nn.sigmoid(total)
            grad = grad_ref[start : start + CHUNK, lanes] * (sig * (1.0 + total * (1.0 - sig)))
            for tap in range(KW):
                acc_ref[tap * 8 : tap * 8 + 8, lanes] += fold(grad * taps[tap])
            acc_ref[32:40, lanes] += fold(grad)
            dpre = conv_pull(grad, next_s[:, lanes], cw_ref[:, lanes])
            dpre_ref[start + HALO : start + HALO + CHUNK, lanes] = dpre.astype(BF16)
            next_s[:, lanes] = grad[0:8]
    for q in range(wide // LANES):
        lanes = slice(q * LANES, (q + 1) * LANES)
        empty = jnp.zeros((HALO, LANES), F32)
        dpre_ref[0:HALO, lanes] = conv_pull(empty, next_s[:, lanes], cw_ref[:, lanes]).astype(BF16)
    dpre_ref[HALO + rows :] = jnp.zeros((TAIL, wide), BF16)


def map_back(pre, grad, conv_w, conv_b):
    return pl.pallas_call(
        map_back_kernel,
        out_shape=(jax.ShapeDtypeStruct((pre.shape[0] + TAIL, pre.shape[1]), BF16), jax.ShapeDtypeStruct((40, pre.shape[1]), F32)),
        scratch_shapes=[pltpu.VMEM((8, pre.shape[1]), F32)],
        compiler_params=pltpu.CompilerParams(vmem_limit_bytes=VMEM),
        cost_estimate=cost(4),
        name="map_back",
    )(pre, grad, conv_w, conv_b)


def final_kernel(groups, width, counts, *refs):
    ds, ws, rest = split(refs, (groups, sum(counts), 15))
    ws = split(ws, counts)
    dm_ref, wm_ref, dt_ref, wt_ref, halo_ref, dn_ref, hid_ref, cot_ref, gain_ref, flag_ref, gh_ref, gn_ref, left_s, total_s, grad_s = rest
    rows, wide = hid_ref.shape
    inner = ds[0].shape[1]
    start = pl.multiple_of(pl.program_id(0) * rows, HALO)

    @pl.when(pl.program_id(0) == 0)
    def _():
        gn_ref[...] = jnp.zeros_like(gn_ref)

    own = pl.ds(pl.multiple_of(start + HALO, HALO), rows)
    for g in range(groups):
        left_s[:, g * inner : (g + 1) * inner] = ds[g][own]
    left_s[:, groups * inner :] = dm_ref[own]

    @pl.when(pl.program_id(0) == pl.num_programs(0) - 1)
    def _():
        last = slice(rows - HALO, rows)
        left_s[last] = (left_s[last].astype(F32) + halo_ref[...].astype(F32)).astype(BF16)

    lefts = [left_s.at[:, g * inner : (g + 1) * inner] for g in range(groups)]
    lefts += [left_s.at[:, groups * inner :]]
    back_times(total_s, lefts, ws + [[wm_ref]], dn_ref)
    total_s[...] += dot(dt_ref[...], wt_ref[...])
    squares = jnp.zeros((rows, 1), F32)
    for c in range(wide // LANES):
        lanes = slice(c * LANES, (c + 1) * LANES)
        tokens = hid_ref[:, lanes].astype(F32)
        squares = squares + jnp.sum(tokens * tokens, axis=1, keepdims=True)
    inverse = lax.rsqrt(squares / wide + EPSILON)
    dots = jnp.zeros((rows, 1), F32)
    for c in range(wide // LANES):
        lanes = slice(c * LANES, (c + 1) * LANES)
        tokens = hid_ref[:, lanes].astype(F32)
        dots = dots + jnp.sum(total_s[:, lanes] * gain_ref[:, lanes] * tokens, axis=1, keepdims=True)
    pull = inverse * inverse * inverse * (dots / wide)
    for c in range(wide // LANES):
        lanes = slice(c * LANES, (c + 1) * LANES)
        tokens = hid_ref[:, lanes].astype(F32)
        grad = total_s[:, lanes]
        grad_s[:, lanes] = cot_ref[:, lanes].astype(F32) + inverse * (grad * gain_ref[:, lanes]) - tokens * pull
        gn_ref[:, lanes] += fold(grad * tokens * inverse)
    natural(gh_ref, grad_s, flag_ref, width)


def final(ds, ws, dm, wm, dt, wt, halo, dn, hidden, cot, gain, flag, width):
    groups = len(ds)
    rows = hidden.shape[0]
    inner = ds[0].shape[1]
    tile = 256
    row = lambda i: (i, 0)
    fixed = lambda i: (0, 0)
    return pl.pallas_call(
        functools.partial(final_kernel, groups, width, tuple(map(len, ws))),
        grid=(rows // tile,),
        in_specs=[
            *map(whole_spec, ds),
            *map(place_spec, flat(ws)),
            whole_spec(dm),
            whole_spec(wm),
            pl.BlockSpec((tile, LANES), row),
            whole_spec(wt),
            whole_spec(halo),
            pl.BlockSpec((tile, D), row),
            pl.BlockSpec((tile, D), row),
            pl.BlockSpec((tile, D), row),
            pl.BlockSpec((1, D), fixed),
            whole_spec(flag),
        ],
        out_specs=[pl.BlockSpec((tile, D), row), pl.BlockSpec((8, D), fixed)],
        out_shape=(jax.ShapeDtypeStruct((rows, D), F32), jax.ShapeDtypeStruct((8, D), F32)),
        scratch_shapes=[pltpu.VMEM((tile, groups * inner + 2 * NS), BF16), pltpu.VMEM((tile, D), F32), pltpu.VMEM((tile, D), F32)],
        compiler_params=pltpu.CompilerParams(vmem_limit_bytes=VMEM),
        cost_estimate=cost(20),
        name="final",
    )(*ds, *arrays(ws), dm, wm, dt, wt, halo, dn, hidden, cot, gain, flag)


def across(value, axis, size, bit):
    return lax.ppermute(value, axis, [(i, i ^ bit) for i in range(size)])


def bits(size):
    return [1 << i for i in range(size.bit_length() - 1)]


def after(value, *others):
    return lax.optimization_barrier((value, others))[0]


def shards(
    zn,
    tp,
    hidden,
    norm_gain,
    head_weight,
    step_weight,
    map_weight,
    conv_weight,
    conv_bias,
    step_bias,
    decay_log,
    skip_gain,
    gate_gain,
    out_weight,
    cotangent,
):
    rows = hidden.shape[0]
    width, _, inner = head_weight.shape
    heads = step_weight.shape[1]
    span = LEN // rows
    forward = [(i, i + 1) for i in range(tp - 1) if (i + 1) % span]
    backward = [(j, i) for i, j in forward]
    core, z_me, t_me = (lax.axis_index(name) for name in ("core", "z", "tensor"))
    swap = lambda value: across(value, "core", 2, 1)
    near = lambda value, bit: across(value, "tensor", tp, bit)
    steps = [("z", zn, b) for b in bits(zn)] + [("tensor", tp, b) for b in bits(tp)] + [("core", 2, 1)]
    half = zn * width // 2

    def to_own(array):
        parts = array.reshape(array.shape[:-1] + (zn, 2, width))
        first, second = parts[..., 0, :], parts[..., 1, :]
        both = [jnp.where(core == 0, first, second), jnp.where(core == 0, second, first)]
        return jnp.concatenate([a.reshape(array.shape[:-1] + (zn * width,)) for a in both], axis=-1)

    def from_own(array):
        lead = array.shape[:-1]
        own, other = (array[..., i * zn * width : (i + 1) * zn * width].reshape(lead + (zn, 1, width)) for i in (0, 1))
        both = [jnp.where(core == 0, own, other), jnp.where(core == 0, other, own)]
        return jnp.concatenate(both, axis=-2).reshape(lead + (D,))

    groups_now = jnp.arange(tp) ^ t_me
    z_now = jnp.arange(zn) ^ z_me
    core_now = jnp.arange(2)[:, None, None] * (zn * tp)
    by_place = (core_now + groups_now[None, None] * zn + z_now[None, :, None]).reshape(-1)
    by_group = (core_now + jnp.arange(tp)[None, None] * zn + z_now[None, :, None]).reshape(-1)

    def regroup(array):
        lead, last = array.shape[:-1], array.shape[-1]
        return jnp.take(array.reshape(lead + (tp, last // tp)), groups_now, axis=-2).reshape(array.shape)

    def send_own(mine):
        return [near(mine, 1), near(mine, 2)] if tp == 4 else [near(mine, g) for g in range(1, tp)]

    def send_far(got):
        if tp != 4:
            return [], []
        halves_now = [got[0][:half], got[1][half:]]
        return halves_now, [near(halves_now[0], 2), near(halves_now[1], 1)]

    def places(mine, mine_other, rest):
        other = swap(rest)
        return [[(mine, 0), (mine_other, 0)]] + [[(rest, g), (other, g)] for g in range(tp - 1)]

    coming = []

    class Scatter:
        def __init__(self, left, via):
            self.left, self.via, self.others = left, via, [None] * tp
            self.add = [[] for _ in range(tp)]

        def away(self, right):
            return dot(self.left[:, zn * width :], right, TN).astype(BF16)

        def swap(self, g, right):
            self.others[g] = swap(self.away(right))
            return self.others[g]

        def partial(self, g, right):
            total = dot(self.left[:, : zn * width], right, TN) + self.others[g].astype(F32)
            for term in self.add[g]:
                total = total + term.astype(F32)
            return total.astype(BF16)

        def send(self, g, right):
            part = self.partial(g, right)
            if tp == 4 and g == 3 and self.via is None:
                self.add[1].append(jnp.pad(near(part[:half], 2), ((0, half), (0, 0))))
                self.add[2].append(jnp.pad(near(part[half:], 1), ((half, 0), (0, 0))))
                coming.extend([self.add[1][-1], self.add[2][-1]])
                return part
            if tp == 4 and g == 3:
                got, at = near(part, 3 - self.via), self.via
            else:
                got, at = near(part, g), 0
            self.add[at].append(got)
            coming.append(got)
            return part

        def halves(self, g):
            return (1, 2) if tp == 4 and g == 3 and self.via is None else (0,)

        def finish(self, right):
            return self.partial(0, right)

    def scatter(total):
        return lax.psum_scatter(total, "z", scatter_dimension=0, tiled=True).astype(F32)

    def everywhere(vector):
        for axis, size, bit in steps:
            vector = vector + across(vector, axis, size, bit)
        return vector

    flag = jnp.full((8, LANES), core, F32)
    shard_x, shard_z = head_weight[:, 1], head_weight[:, 0]
    x_mine = lax.all_gather(shard_x, "z", axis=0, tiled=True)
    z_mine = lax.all_gather(after(shard_z, shard_x), "z", axis=0, tiled=True)
    out_mine = lax.all_gather(after(out_weight, shard_z), "z", axis=0, tiled=True)

    map_rows = map_weight.shape[0]
    pitch = -(-heads // 16) * 16
    strips = -(-width // LANES)
    pad_step = lambda a: jnp.pad(a, ((0, 0),) * (a.ndim - 2) + ((0, pitch - heads), (0, strips * LANES - width)))
    strip = lambda a: jnp.concatenate([a[..., i * LANES : (i + 1) * LANES] for i in range(a.shape[-1] // LANES)], axis=-2)
    small = jnp.concatenate([strip(map_weight), strip(pad_step(step_weight.T))], axis=0)[None]
    depth = small.shape[1]
    for axis, count, bit in steps:
        small = jnp.concatenate([small, across(small, axis, count, bit)], axis=0)
    pick = lambda a, index, axis: jnp.take(a, index, axis=axis, mode="clip")
    maps = pick(small[:, : 2 * map_rows], by_place, 0)
    map_w = jnp.concatenate([maps[:, i * map_rows : (i + 1) * map_rows].reshape(D, LANES) for i in (0, 1)], axis=1)
    steps_w = pick(small[:, 2 * map_rows :], by_group, 0).reshape(2, zn, tp, strips, pitch, LANES)
    steps_w = jnp.transpose(steps_w, (2, 4, 0, 1, 3, 5)).reshape(tp * pitch, 2 * zn, strips * LANES)
    step_w = steps_w[..., :width].reshape(tp * pitch, D)
    step_w = jnp.pad(step_w, ((0, LANES - tp * pitch), (0, 0)))

    x_mine = after(x_mine, map_w, step_w)
    x_own_other, x_near = swap(x_mine), send_own(x_mine)
    hidden, cotangent, norm_gain, conv_weight, conv_bias, step_bias, decay_log, skip_gain, gate_gain = after(
        (hidden, cotangent, norm_gain, conv_weight, conv_bias, step_bias, decay_log, skip_gain, gate_gain), map_w, step_w
    )
    hidden, norm_gain = to_own(hidden), to_own(norm_gain)
    halo = lax.ppermute(hidden[rows - HALO :], "tensor", forward)
    tokens = jnp.concatenate([halo, hidden], axis=0).astype(F32)
    inverse = lax.rsqrt(jnp.mean(tokens * tokens, axis=-1, keepdims=True) + EPSILON)
    normed_ext = jnp.pad((tokens * inverse * norm_gain).astype(BF16), ((0, TAIL), (0, 0)))
    normed = normed_ext[HALO : HALO + rows]

    def per_pitch(a):
        a = jnp.pad(a.reshape(tp, heads), ((0, 0), (0, pitch - heads))).reshape(1, tp * pitch)
        return jnp.pad(a, ((0, 0), (0, LANES - tp * pitch)))

    x_near, z_mine = after((x_near, z_mine), normed_ext)
    x_cut, x_far = send_far(x_near)
    z_mine = after(z_mine, *x_near)
    z_own_other, z_near = swap(z_mine), send_own(z_mine)
    cotangent, conv_weight, conv_bias, step_bias, decay_log, skip_gain, gate_gain = after(
        (cotangent, conv_weight, conv_bias, step_bias, decay_log, skip_gain, gate_gain), *x_cut
    )
    cotangent = to_own(cotangent)
    conv_x, bias_x = regroup(conv_weight[:, :DI]), regroup(conv_bias[None, :DI])
    conv_m, bias_m = conv_weight[:, DI:], conv_bias[None, DI:]
    step_bias, decay_log, skip_gain, gate_gain = (regroup(a[None]) for a in (step_bias, decay_log, skip_gain, gate_gain))
    skip = jnp.repeat(skip_gain, HEAD, axis=1)
    pre_m, bc, v, c2, cd, c2t, cdt, wf, ei, total = prep(
        normed_ext, after(map_w, *x_cut, x_own_other, out_mine, cotangent, conv_x, bias_x, skip, gate_gain), step_w, conv_m, bias_m, per_pitch(step_bias), per_pitch(decay_log), tp, heads, pitch
    )
    total = total[:, : tp * pitch].reshape(tp, pitch)[:, :heads].reshape(1, H)
    device_decay = jnp.repeat(jnp.exp2(total), HEAD, axis=1)
    groups = range(tp)
    span_of = lambda g: slice(g * inner, (g + 1) * inner)

    def pass_on(value, pairs, g):
        received = {}
        for gap in sorted({i ^ j for i, j in pairs}):
            received[g ^ gap] = lax.ppermute(value, "tensor", [(i, j) for i, j in pairs if i ^ j == gap])
        return received

    def chain(local, first, pairs):
        passed = gathered(first)
        for _ in range(span - 2):
            sums = [local[g].astype(F32) + device_decay[:, span_of(g)] * passed[g].astype(F32) for g in groups]
            passed = gathered([pass_on(total.astype(BF16), pairs, g) for g, total in enumerate(sums)])
        return passed

    def gathered(parts):
        out = [None] * tp
        for part in parts:
            for g, value in part.items():
                out[g] = value if out[g] is None else out[g] + value
        return [jnp.zeros((NS, inner), BF16) if value is None else value for value in out]

    pre, x, states, y, local = ([None] * tp for _ in range(5))

    first = []

    def run_project(g, *others):
        pre[g], x[g], local[g] = project(g, after(normed_ext, *others), x_w[g], conv_x, bias_x, bc, wf)
        first.append(pass_on(local[g], forward, g))

    def run_scan(g, *others):
        y[g], states[g] = scan(g, after(x[g], *others), bc, c2, cd, cdt, start[g], skip)

    x_w = [[(x_mine, 0), (x_own_other, 0)]]
    run_project(0)
    x_rest = jnp.concatenate(after(x_near + x_far, x[0]), axis=0)
    x_w = places(x_mine, x_own_other, x_rest)
    z = [product(after(normed, x_rest, z_own_other), [(z_mine, 0), (z_own_other, 0)])]
    run_project(1, z[0], x_w[1][1][0])
    z_near = after(z_near, x[1], *first[0].values())
    z_cut, z_far = send_far(z_near)
    if tp > 2:
        run_project(2, *z_cut)
    z_rest = jnp.concatenate(after(z_near + z_far, x[min(2, tp - 1)], *first[1].values()), axis=0)
    z_w = places(z_mine, z_own_other, z_rest)
    for g in range(3, tp):
        run_project(g, z_rest, x[g - 1])
    z.append(product(after(normed, x[tp - 1], z_w[1][1][0], *first[-2].values()), z_w[1]))
    start = after(chain(local, first, forward), z[1])
    out_mine = after(out_mine, *start)
    out_own_other, out_near = swap(out_mine), send_own(out_mine)
    run_scan(0)
    run_scan(1, y[0], out_own_other)
    out_near = after(out_near, y[1])
    out_cut, out_far = send_far(out_near)
    if tp > 2:
        run_scan(2, *out_cut)
    out_rest = jnp.concatenate(after(out_near + out_far, y[min(2, tp - 1)]), axis=0)
    out_w = places(out_mine, out_own_other, out_rest)
    for g in range(3, tp):
        run_scan(g, out_rest, y[g - 1])
    normed_late = after(normed, y[tp - 1], out_rest, out_w[1][1][0])
    z += [product(normed_late, z_w[g]) for g in range(2, tp)]

    scaled, dy, dz, local_pull, block_out, dn_z, gain_sums = gate(
        y, z, out_w, z_w, cotangent, hidden, gate_gain, bc, ei, flag, width
    )
    pulls = chain(local_pull, [pass_on(local_pull[g ^ 1], backward, g ^ 1) for g in reversed(groups)], backward)
    out_grad, z_grad, x_grad = Scatter(cotangent, 1), Scatter(normed, 2), Scatter(normed_ext, None)
    dpre, dbc, sums, q, da = ([None] * tp for _ in range(5))
    last = tp - 1
    order = list(reversed(groups))
    swapped = [out_grad.swap(last, scaled[last]), z_grad.swap(last, dz[last])]
    swapped += [out_grad.swap(g, after(scaled[g], *swapped)) for g in order[1:]]
    ready = swapped + pulls
    waiting = ready + [out_grad.send(last, after(scaled[last], *ready)), z_grad.send(last, after(dz[last], *ready))]
    later = []
    for at, g in enumerate(order):
        dpre[g], dbc[g], sums[g], q[g], da[g] = back(
            g, pre[g], after(dy[g], *waiting), bc, c2, cd, c2t, states[g], pulls[g], skip, conv_x, bias_x
        )
        arrivals = [dpre[g]] + coming
        coming.clear()
        now = lambda value: after(value, *arrivals)
        waiting = []
        if at < last:
            waiting.append(x_grad.swap(g, now(dpre[g])))
        if at == 0:
            waiting += [out_grad.send(i, now(scaled[i])) for i in order[1:-1]]
            waiting.append(x_grad.send(g, now(dpre[g])))
            later, coming[:] = coming[-len(x_grad.halves(g)) :], coming[: -len(x_grad.halves(g))]
            waiting += [z_grad.swap(i, now(dz[i])) for i in order[1:]]
        if at == 1:
            coming += later
            total = out_grad.finish(now(scaled[0]))
            waiting, total = lax.optimization_barrier((waiting, total))
            grad_out = scatter(total)
            waiting += [z_grad.send(i, now(dz[i])) for i in order[1:-1]]
        if at == last - 1:
            waiting += [x_grad.send(i, now(dpre[i])) for i in order[1:-1]]
        if at == min(2, last):
            total = z_grad.finish(now(dz[0]))
            waiting, total = lax.optimization_barrier((waiting, total))
            grad_z = scatter(total)
            waiting.append(grad_out)
    x_grad.swap(0, now(dpre[0]))
    total = x_grad.finish(now(dpre[0]))
    q, da, sums = after((q, da, sums), total)
    dbc_all, total = lax.optimization_barrier((after(functools.reduce(jnp.add, dbc), *waiting), total))
    grad_x = scatter(total)
    dpre_m, sums_m = map_back(pre_m, dbc_all, conv_m, bias_m)
    dn_z = after(dn_z, grad_z)

    v = v.reshape(H, rows)
    q, da = (jnp.concatenate(a, axis=0).reshape(H, rows) for a in (q, da))
    delta, sig = jax.nn.softplus(v), jax.nn.sigmoid(v)
    rate = -jnp.exp(decay_log).reshape(H, 1)
    ratio = jnp.where(v < -15.0, 1.0, sig / jnp.maximum(delta, 1e-30))
    dstep = q * ratio + da * rate * sig
    dstep_low = dstep.astype(BF16)
    dstep_t = jnp.pad(dstep_low.reshape(tp, heads, rows), ((0, 0), (0, pitch - heads), (0, 0))).reshape(tp * pitch, rows)
    dstep_t = jnp.pad(dstep_t, ((0, LANES - tp * pitch), (0, 0)))
    dstep_rows = dstep_t.T

    place_order = (core_now + z_now[None, None] * tp + groups_now[None, :, None]).reshape(-1)
    group_order = (core_now + z_now[None, None] * tp + jnp.arange(tp)[None, :, None]).reshape(-1)
    grad_map = dot(normed_ext, dpre_m, TN).reshape(2 * zn * tp, map_rows, 2 * NS)
    grad_map = pick(strip(grad_map), place_order, 0)
    grad_step = dot(dstep_t[: tp * pitch], normed).reshape(tp, pitch, 2, zn, width)[:, :heads]
    grad_step = strip(pad_step(jnp.transpose(grad_step, (2, 3, 0, 1, 4)).reshape(-1, heads, width)))
    grad_small = jnp.concatenate([grad_map, pick(grad_step, group_order, 0)], axis=-2)
    for axis, count, bit in reversed(steps):
        keep = grad_small.shape[0] // 2
        grad_small = grad_small[:keep] + across(grad_small[keep:], axis, count, bit)
    grad_small = grad_small[0]
    map_shard = jnp.concatenate([grad_small[:map_rows], grad_small[map_rows : 2 * map_rows]], axis=1)
    step_shard = grad_small[2 * map_rows :].reshape(strips, pitch, LANES)
    step_shard = jnp.concatenate([step_shard[i] for i in range(strips)], axis=1)[:heads, :width].T

    halo = jnp.zeros((HALO, DI + 2 * NS), BF16)
    edge = jnp.concatenate([a[:HALO] for a in dpre + [dpre_m]], axis=1)
    for gap in sorted({i ^ j for i, j in backward}):
        part = lax.ppermute(edge, "tensor", [(i, j) for i, j in backward if i ^ j == gap])
        halo = halo + jnp.concatenate([part[:, span_of(g ^ gap)] for g in groups] + [part[:, DI:]], axis=1)
    grad_hidden, norm_sums = final(
        dpre, x_w, dpre_m, map_w, dstep_rows, step_w, halo, dn_z, hidden, cotangent, norm_gain[None], flag, width
    )
    fold8 = lambda a: a.reshape(-1, 8, a.shape[-1]).sum(1)
    sums = jnp.concatenate([fold8(part) for part in sums], axis=1)
    taps = jnp.concatenate([regroup(sums[:5]), fold8(sums_m)], axis=1)
    per_head = jnp.stack(
        [
            jnp.sum(dstep, axis=1),
            jnp.sum(da * delta, axis=1) * rate[:, 0],
            jnp.sum(sums[5].reshape(H, HEAD), axis=1),
        ]
    )
    vector = [taps.reshape(-1), regroup(per_head).reshape(-1), regroup(fold8(gain_sums))[0]]
    vector = everywhere(after(jnp.concatenate(vector + [from_own(jnp.sum(norm_sums, axis=0))]), grad_x))
    wide = DI + 2 * NS
    cuts = [KW * wide, wide, H, H, H, DI, D]
    parts, at = [], 0
    for count in cuts:
        parts.append(vector[at : at + count])
        at += count
    return (
        block_out,
        grad_hidden,
        parts[6],
        jnp.stack([grad_z, grad_x], axis=1),
        step_shard,
        map_shard,
        parts[0].reshape(KW, wide),
        parts[1],
        parts[2],
        parts[3],
        parts[4],
        parts[5],
        grad_out,
    )


def solution(mesh):
    dp, tp = mesh.shape["dp"], mesh.shape["tensor"]
    inner = Mesh(mesh.devices.reshape(dp // 2, 2, tp), ("z", "core", "tensor"))
    rows = P(("z", "core", "tensor"), None)
    split_dp = ("z", "core")
    head, step, out = P(split_dp, None, "tensor"), P(split_dp, "tensor"), P(split_dp, "tensor")
    whole = P()
    return jax.shard_map(
        functools.partial(shards, dp // 2, tp),
        mesh=inner,
        in_specs=(rows, whole, head, step, rows, whole, whole, whole, whole, whole, whole, out, rows),
        out_specs=(rows, rows, whole, head, step, rows, whole, whole, whole, whole, whole, whole, out),
        check_vma=False,
    )
```

time: 1290 us -> 723 us (0.56)
  waiting for transfers between devices: 667 us -> 113 us
  blocking collectives: 118 us -> 0 us
  Pallas kernels: 215 us -> 315 us
  starting transfers between devices: 11 us -> 71 us
  matrix products: 113 us -> 79.5 us
  local copies, waits for them, and re-layouts: 107 us -> 93.3 us
    reduce_scatter x4 -> x3, waiting for transfers between devices: 519 us -> 10.5 us  [scatter(): lax.psum_scatter(total, 'z', scatter_dimension=0, tiled=True).astype(F32)]
    all_gather x2 -> x0, blocking collectives: 118 us -> none  [the longest x1 79.4 us: shards(): map_full = lax.all_gather(map_weight, ('dp', 'tensor'), axis=0, tiled=True)]
    dot_general x8 -> x0, matrix products: 106 us -> none  [the longest x3 47.5 us: weight_grad(): jnp.einsum('rd,rgi->gdi', left, right.reshape(right.shape[0], tp, inner),...]
    unnamed x10 -> x6, waiting for transfers between devices: 103 us -> 0.1 us
    pallas_call x6 -> x20, Pallas kernels: 215 us -> 315 us  [the longest x4 89.8 us: back(): pl.pallas_call(back_kernel, grid=(1,), in_specs=[whole_spec(pre), whole_s...]
    dot_general x2 -> x26, matrix products: 7.58 us -> 79.5 us  [dot(): lax.dot_general(a, b, dims, precision=precision, preferred_element_type=F32)]
    ppermute x3 -> x64, starting transfers between devices: 5.55 us -> 66.9 us  [the longest x55 49.7 us: across(): return lax.ppermute(value, axis, [(i, i ^ bit) for i in range(size)])]
    ppermute x3 -> x64, waiting for transfers between devices: 30.2 us -> 88.4 us  [the longest x55 67.1 us: across(): return lax.ppermute(value, axis, [(i, i ^ bit) for i in range(size)])]
  transfers between devices with their start and end apart: 13 -> 71, of which waited for: 8 -> 31; matrix products, arithmetic and copies ran while one was open for 16% -> 23% of each run, Pallas kernels for 7% -> 33%
where the time goes in v2:
time: 723 us; the launch traced here: 716 us
  Pallas kernels  315 us (44%)
  waiting for transfers between devices  113 us (16%)
  local copies, waits for them, and re-layouts  93.3 us (13%)
  matrix products  79.5 us (11%)
  starting transfers between devices  71 us (10%)
  other arithmetic  28.4 us (4%)
  between operations  16 us (2%)
    pallas_call x4, Pallas kernels, back(): pl.pallas_call(back_kernel, grid=(1,), in_specs=[whole_spec(pre), whole_s...  89.8 us
    dot_general x26, matrix products, dot(): lax.dot_general(a, b, dims, precision=precision, preferred_element_type=F32)  79.5 us
    pallas_call x1, Pallas kernels, gate(): pl.pallas_call(functools.partial(gate_kernel, groups, width, tuple(map(le...  67.2 us
    ppermute x55, waiting for transfers between devices, across(): return lax.ppermute(value, axis, [(i, i ^ bit) for i in range(size)])  67.1 us
    pallas_call x4, Pallas kernels, project(): pl.pallas_call(functools.partial(proj_kernel, tile, len(blocks)), grid=(1...  50.7 us
    ppermute x55, starting transfers between devices, across(): return lax.ppermute(value, axis, [(i, i ^ bit) for i in range(size)])  49.7 us
    pallas_call x4, Pallas kernels, scan(): pl.pallas_call(scan_kernel, grid=(1,), in_specs=[whole_spec(x), whole_spe...  42.3 us
    unnamed x200, local copies, waits for them, and re-layouts  31.3 us
  transfers between devices with their start and end apart: 71, of which 31 were waited for; matrix products, arithmetic and copies ran while one was open for 23% of the time, Pallas kernels for 33%

profile of v2, /device:TPU:0, one launch (start us, length us, event | category | flops | bytes accessed | tf_op | source)
XLA Modules:
  0.0 716.3 jit_solution(5971542101663307295)
XLA Ops:
  62.8 13.0 %all-gather.5.cloned.1.call-done.refs_0_.refs_16_ = bf16[768,768]{1,0:T(8,128)(2,1)} async-done(((bf16[192,768]{1,0:T(8,128)(2,1)}), bf16[768,768]{1,0:T(8,128)(2,1)}) %all-gather.5.cloned.1.call-update) | async-done | bytes 1179664 | tf_op jit(solution)/shard_map/all_gather | solution.py:905
  75.8 6.7 collective-permute-done.7
  111.0 10.6 %prep.1 = (bf16[1040,256]{1,0:T(8,128)(2,1)}, bf16[1024,256]{1,0:T(8,128)(2,1)}, f32[4,12,1024]{2,1,0:T(8,128)}, f32[4,1024,12]{2,1,0:T(8,128)}, f32[4,1024,12]{...) custom-call(bf16[1152,1536]{1,0:T(8,128)(2,1)} %pad.48.n_ref, ...), custom_call_target="tpu_custom_call" | custom-call | bytes 11 | tf_op jit(solution)/shard_map/prep/pallas_call | solution.py:182
  121.6 12.7 %project.4 = (bf16[1040,768]{1,0:T(8,128)(2,1)}, bf16[1024,768]{1,0:T(8,128)(2,1)}, bf16[128,768]{1,0:T(8,128)(2,1)}) custom-call(bf16[1152,1536]{1,0:T(8,128)(2,1)} %pad.48.n_ref, bf16[768,768]{1,0:T(8,128)(2,1)} %bitcast.9.refs_0_.refs_4_, bf16[768,768]{1,0:T(8,128)(2,1)} %collective-permute-done.6.refs_1_.refs_5_, ...), custom_call_target="tpu_custom_call" | custom-call | bytes 10 | tf_op jit(solution)/shard_map/project/pallas_call | solution.py:236
  148.8 6.3 product.4.refs_4_
  155.2 12.7 %project.5 = (bf16[1040,768]{1,0:T(8,128)(2,1)}, bf16[1024,768]{1,0:T(8,128)(2,1)}, bf16[128,768]{1,0:T(8,128)(2,1)}) custom-call(bf16[1152,1536]{1,0:T(8,128)(2,1)} %pad.48.n_ref, bf16[2304,768]{1,0:T(8,128)(2,1)} %copy-done, bf16[2304,768]{1,0:T(8,128)(2,1)} %collective-permute-done.12.refs_1_.refs_7_.refs_9_.refs_11_, ...), custom_call_target="tpu_custom_call" | custom-call | bytes 10 | tf_op jit(solution)/shard_map/project/pallas_call | solution.py:236
  178.7 12.7 %project.6 = (bf16[1040,768]{1,0:T(8,128)(2,1)}, bf16[1024,768]{1,0:T(8,128)(2,1)}, bf16[128,768]{1,0:T(8,128)(2,1)}) custom-call(bf16[1152,1536]{1,0:T(8,128)(2,1)} %pad.48.n_ref, bf16[2304,768]{1,0:T(8,128)(2,1)} %copy-done, bf16[2304,768]{1,0:T(8,128)(2,1)} %collective-permute-done.12.refs_1_.refs_7_.refs_9_.refs_11_, ...), custom_call_target="tpu_custom_call" | custom-call | bytes 10 | tf_op jit(solution)/shard_map/project/pallas_call | solution.py:236
  200.8 12.7 %project.7 = (bf16[1040,768]{1,0:T(8,128)(2,1)}, bf16[1024,768]{1,0:T(8,128)(2,1)}, bf16[128,768]{1,0:T(8,128)(2,1)}) custom-call(bf16[1152,1536]{1,0:T(8,128)(2,1)} %pad.48.n_ref, bf16[2304,768]{1,0:T(8,128)(2,1)} %copy-done, bf16[2304,768]{1,0:T(8,128)(2,1)} %collective-permute-done.12.refs_1_.refs_7_.refs_9_.refs_11_, ...), custom_call_target="tpu_custom_call" | custom-call | bytes 10 | tf_op jit(solution)/shard_map/project/pallas_call | solution.py:236
  215.2 6.4 product.5.refs_5_
  223.3 10.5 %scan.4 = (bf16[1024,768]{1,0:T(8,128)(2,1)}, bf16[8,128,768]{2,1,0:T(8,128)(2,1)}) custom-call(bf16[1024,768]{1,0:T(8,128)(2,1)} %get-tuple-element.206.x_ref, bf16[1024,256]{1,0:T(8,128)(2,1)} %get-tuple-element.204.refs_4_.bc_ref.refs_27_, f32[4,1024,12]{2,1,0:T(8,128)} %get-tuple-element.207.c2_ref, f32[4,1024,12]{2,1,0:T(8,128)} %get-tuple-element.208.cd_ref, ...), custom_call_target="tpu_custom_call" | custom-call | bytes 9 | tf_op jit(solution)/shard_map/scan/pallas_call | solution.py:326
  233.8 10.9 %scan.5 = (bf16[1024,768]{1,0:T(8,128)(2,1)}, bf16[8,128,768]{2,1,0:T(8,128)(2,1)}) custom-call(bf16[1024,768]{1,0:T(8,128)(2,1)} %get-tuple-element.240.x_ref, bf16[1024,256]{1,0:T(8,128)(2,1)} %get-tuple-element.204.refs_4_.bc_ref.refs_27_, f32[4,1024,12]{2,1,0:T(8,128)} %get-tuple-element.207.c2_ref, f32[4,1024,12]{2,1,0:T(8,128)} %get-tuple-element.208.cd_ref, ...), custom_call_target="tpu_custom_call" | custom-call | bytes 9 | tf_op jit(solution)/shard_map/scan/pallas_call | solution.py:326
  253.5 10.5 %scan.6 = (bf16[1024,768]{1,0:T(8,128)(2,1)}, bf16[8,128,768]{2,1,0:T(8,128)(2,1)}) custom-call(bf16[1024,768]{1,0:T(8,128)(2,1)} %get-tuple-element.244.x_ref, bf16[1024,256]{1,0:T(8,128)(2,1)} %get-tuple-element.204.refs_4_.bc_ref.refs_27_, f32[4,1024,12]{2,1,0:T(8,128)} %get-tuple-element.207.c2_ref, f32[4,1024,12]{2,1,0:T(8,128)} %get-tuple-element.208.cd_ref, ...), custom_call_target="tpu_custom_call" | custom-call | bytes 9 | tf_op jit(solution)/shard_map/scan/pallas_call | solution.py:326
  273.2 10.5 %scan.7 = (bf16[1024,768]{1,0:T(8,128)(2,1)}, bf16[8,128,768]{2,1,0:T(8,128)(2,1)}) custom-call(bf16[1024,768]{1,0:T(8,128)(2,1)} %get-tuple-element.250.x_ref, bf16[1024,256]{1,0:T(8,128)(2,1)} %get-tuple-element.204.refs_4_.bc_ref.refs_27_, f32[4,1024,12]{2,1,0:T(8,128)} %get-tuple-element.207.c2_ref, f32[4,1024,12]{2,1,0:T(8,128)} %get-tuple-element.208.cd_ref, ...), custom_call_target="tpu_custom_call" | custom-call | bytes 9 | tf_op jit(solution)/shard_map/scan/pallas_call | solution.py:326
  283.7 6.3 product.7.refs_7_
  296.8 67.2 %gate.1 = (bf16[1024,768]{1,0:T(8,128)(2,1)}, bf16[1024,768]{1,0:T(8,128)(2,1)}, bf16[1024,768]{1,0:T(8,128)(2,1)}, bf16[1024,768]{1,0:T(8,128)(2,1)}, bf16[1024...) custom-call(bf16[1024,768]{1,0:T(8,128)(2,1)} %get-tuple-element.235, ...), custom_call_target="tpu_custom_call" | custom-call | bytes 55 | tf_op jit(solution)/shard_map/gate/pallas_call | solution.py:462
  379.6 7.0 collective-permute-done.33.u_ref
  404.2 22.3 %back.4 = (bf16[1152,768]{1,0:T(8,128)(2,1)}, f32[1024,256]{1,0:T(8,128)}, f32[48,768]{1,0:T(8,128)}, f32[1,12,1024]{2,1,0:T(8,128)}, f32[1,12,1024]{2,1,0:T(8,128)}) custom-call(bf16[1040,768]{1,0:T(8,128)(2,1)} %get-tuple-element.259.pre_ref, bf16[1024,768]{1,0:T(8,128)(2,1)} %get-tuple-element.275.dy_ref, ...), custom_call_target="tpu_custom_call" | custom-call | bytes 18 | tf_op jit(solution)/shard_map/back/pallas_call | solution.py:614
  452.3 22.4 %back.5 = (bf16[1152,768]{1,0:T(8,128)(2,1)}, f32[1024,256]{1,0:T(8,128)}, f32[48,768]{1,0:T(8,128)}, f32[1,12,1024]{2,1,0:T(8,128)}, f32[1,12,1024]{2,1,0:T(8,128)}) custom-call(bf16[1040,768]{1,0:T(8,128)(2,1)} %get-tuple-element.257.pre_ref, bf16[1024,768]{1,0:T(8,128)(2,1)} %get-tuple-element.288.dy_ref, ...), custom_call_target="tpu_custom_call" | custom-call | bytes 18 | tf_op jit(solution)/shard_map/back/pallas_call | solution.py:614
  493.2 22.3 %back.7 = (bf16[1152,768]{1,0:T(8,128)(2,1)}, f32[1024,256]{1,0:T(8,128)}, f32[48,768]{1,0:T(8,128)}, f32[1,12,1024]{2,1,0:T(8,128)}, f32[1,12,1024]{2,1,0:T(8,128)}) custom-call(bf16[1040,768]{1,0:T(8,128)(2,1)} %get-tuple-element.297.pre_ref, bf16[1024,768]{1,0:T(8,128)(2,1)} %get-tuple-element.301.dy_ref, ...), custom_call_target="tpu_custom_call" | custom-call | bytes 18 | tf_op jit(solution)/shard_map/back/pallas_call | solution.py:614
  515.5 9.9 %collective-permute-done.46 = bf16[384,768]{1,0:T(8,128)(2,1)} collective-permute-done((bf16[384,768]{1,0:T(8,128)(2,1)}, bf16[384,768]{1,0:T(8,128)(2,1)}, u32[]{:S(2)}, u32[]{:S(2)}) %collective-permute-start.46) | collective-permute-done | bytes 589856 | tf_op jit(solution)/shard_map/ppermute | solution.py:778
  557.0 10.4 %reduce-scatter.4.cloned.1.call-done = bf16[192,768]{1,0:T(8,128)(2,1)} async-done(((bf16[768,768]{1,0:T(8,128)(2,1)}), bf16[192,768]{1,0:T(8,128)(2,1)}) %reduce-scatter.4.cloned.1.call-update) | async-done | bytes 294928 | tf_op jit(solution)/shard_map/reduce_scatter | solution.py:895
  569.3 22.7 %back.6 = (bf16[1152,768]{1,0:T(8,128)(2,1)}, f32[1024,256]{1,0:T(8,128)}, f32[48,768]{1,0:T(8,128)}, f32[1,12,1024]{2,1,0:T(8,128)}, f32[1,12,1024]{2,1,0:T(8,128)}) custom-call(bf16[1040,768]{1,0:T(8,128)(2,1)} %get-tuple-element.255.pre_ref, bf16[1024,768]{1,0:T(8,128)(2,1)} %get-tuple-element.294.dy_ref, ...), custom_call_target="tpu_custom_call" | custom-call | bytes 18 | tf_op jit(solution)/shard_map/back/pallas_call | solution.py:614
  644.7 25.0 %final.1 = (f32[1024,1536]{1,0:T(8,128)}, f32[8,1536]{1,0:T(8,128)}) custom-call(bf16[1152,768]{1,0:T(8,128)(2,1)} %get-tuple-element.311.refs_0_, bf16[1152,768]{1,0:T(8,128)(2,1)} %get-tuple-element.310.refs_1_, bf16[1152,768]{1,0:T(8,128)(2,1)} %get-tuple-element.309.refs_2_, bf16[1152,768]{1,0:T(8,128)(2,1)} %get-tuple-element.279.refs_3_, ...), custom_call_target="tpu_custom_call" | custom-call | bytes 20 | tf_op jit(solution)/shard_map/final/pallas_call | solution.py:751
  693.7 6.9 collective-permute-done.63
  (554 shorter events, 341.9 us)
Async XLA Ops:
  7.2 47.4 %all-gather.9.cloned.1.call-start = ((), (), s32[]{:S(2)}) async-start(), calls=%async_computation.8 | async-start | bytes 1474560 | tf_op jit(solution)/shard_map/all_gather | solution.py:904
  10.3 65.4 %all-gather.5.cloned.1.call-start = ((), (), s32[]{:S(2)}) async-start(), calls=%async_computation.3 | async-start | bytes 1474560 | tf_op jit(solution)/shard_map/all_gather | solution.py:905
  11.1 97.3 %all-gather.7.cloned.1.call-start = ((), (), s32[]{:S(2)}) async-start(), calls=%async_computation.4 | async-start | bytes 1474560 | tf_op jit(solution)/shard_map/all_gather | solution.py:906
  14.4 553.1 %reduce-scatter.4.cloned.1.call-start = ((), (), s32[]{:S(2)}) async-start(), calls=%async_computation.5 | async-start | bytes 1474560 | tf_op jit(solution)/shard_map/reduce_scatter | solution.py:895
  62.8 45.7 %collective-permute-start.6 = (bf16[768,768]{1,0:T(8,128)(2,1)}, bf16[768,768]{1,0:T(8,128)(2,1)}, u32[]{:S(2)}, u32[]{:S(2)}) collective-permute-start(bf16[768,768]{1,0:T(8,128)(2,1)} %bitcast.9.refs_0_.refs_4_), channel_id=1, source_target_pairs={{0,4},{4,0},{1,5},{5,1},{2,6},{6,2},{3,7},{7,3},{8,12},{12,8},{9,1... | collective-permute-start | bytes 3538952 | tf_op jit(solution)/shard_map/ppermute | solution.py:778
  87.7 46.5 %collective-permute-start.10 = (bf16[384,768]{1,0:T(8,128)(2,1)}, bf16[384,768]{1,0:T(8,128)(2,1)}, u32[]{:S(2)}, u32[]{:S(2)}) collective-permute-start(bf16[384,768]{1,0:T(8,128)(2,1)} %slice.305), channel_id=1, source_target_pairs={{0,1},{1,0},{2,3},{3,2},{4,5},{5,4},{6,7},{7,6},{8,9},{9,8},{10,11... | collective-permute-start | bytes 1769480 | tf_op jit(solution)/shard_map/ppermute | solution.py:778
  88.1 46.1 %collective-permute-start.9 = (bf16[384,768]{1,0:T(8,128)(2,1)}, bf16[384,768]{1,0:T(8,128)(2,1)}, u32[]{:S(2)}, u32[]{:S(2)}) collective-permute-start(bf16[384,768]{1,0:T(8,128)(2,1)} %slice.304), channel_id=1, source_target_pairs={{0,2},{1,3},{2,0},{3,1},{4,6},{5,7},{6,4},{7,5},{8,10},{9,11},{10,... | collective-permute-start | bytes 1769480 | tf_op jit(solution)/shard_map/ppermute | solution.py:778
  140.0 31.5 %collective-permute-start.15 = (bf16[768,768]{1,0:T(8,128)(2,1)S(1)}, bf16[768,768]{1,0:T(8,128)(2,1)}, u32[]{:S(2)}, u32[]{:S(2)}) collective-permute-start(bf16[768,768]{1,0:T(8,128)(2,1)S(1)} %copy-done.12), channel_id=1, source_target_pairs={{0,1},{1,0},{2,3},{3,2},{4,5},{5,4},{6,7},{7,6},{8,9},{9,8},{10,11... | collective-permute-start | bytes 3538952 | tf_op jit(solution)/shard_map/ppermute | solution.py:778
  141.7 29.8 %collective-permute-start.16 = (bf16[768,768]{1,0:T(8,128)(2,1)S(1)}, bf16[768,768]{1,0:T(8,128)(2,1)}, u32[]{:S(2)}, u32[]{:S(2)}) collective-permute-start(bf16[768,768]{1,0:T(8,128)(2,1)S(1)} %copy-done.12), channel_id=1, source_target_pairs={{0,2},{1,3},{2,0},{3,1},{4,6},{5,7},{6,4},{7,5},{8,10},{9,11},{10,... | collective-permute-start | bytes 3538952 | tf_op jit(solution)/shard_map/ppermute | solution.py:778
  142.2 29.3 %collective-permute-start.14 = (bf16[128,768]{1,0:T(8,128)(2,1)}, bf16[128,768]{1,0:T(8,128)(2,1)S(1)}, u32[]{:S(2)}, u32[]{:S(2)}) collective-permute-start(bf16[128,768]{1,0:T(8,128)(2,1)} %get-tuple-element.219), channel_id=1, source_target_pairs={{0,1},{2,3},{4,5},{6,7},{8,9},{10,11},{12,13},{14,15},{16,17},{18,... | collective-permute-start | bytes 589832 | tf_op jit(solution)/shard_map/ppermute | solution.py:964
  221.7 28.4 %collective-permute-start.23 = (bf16[768,768]{1,0:T(8,128)(2,1)S(1)}, bf16[768,768]{1,0:T(8,128)(2,1)S(1)}, u32[]{:S(2)}, u32[]{:S(2)}) collective-permute-start(bf16[768,768]{1,0:T(8,128)(2,1)S(1)} %copy-done.19), channel_id=1, source_target_pairs={{0,1},{1,0},{2,3},{3,2},{4,5},{5,4},{6,7},{7,6},{8,9},{9,8},{10,11... | collective-permute-start | bytes 3538952 | tf_op jit(solution)/shard_map/ppermute | solution.py:778
  221.8 28.3 %collective-permute-start.24 = (bf16[768,768]{1,0:T(8,128)(2,1)S(1)}, bf16[768,768]{1,0:T(8,128)(2,1)S(1)}, u32[]{:S(2)}, u32[]{:S(2)}) collective-permute-start(bf16[768,768]{1,0:T(8,128)(2,1)S(1)} %copy-done.19), channel_id=1, source_target_pairs={{0,2},{1,3},{2,0},{3,1},{4,6},{5,7},{6,4},{7,5},{8,10},{9,11},{10,... | collective-permute-start | bytes 3538952 | tf_op jit(solution)/shard_map/ppermute | solution.py:778
  443.4 31.3 %collective-permute-start.44 = (bf16[768,768]{1,0:T(8,128)(2,1)}, bf16[768,768]{1,0:T(8,128)(2,1)}, u32[]{:S(2)}, u32[]{:S(2)}) collective-permute-start(bf16[768,768]{1,0:T(8,128)(2,1)} %add_convert_fusion.8), channel_id=1, source_target_pairs={{0,1},{1,0},{2,3},{3,2},{4,5},{5,4},{6,7},{7,6},{8,9},{9,8},{10,11... | collective-permute-start | bytes 3538952 | tf_op jit(solution)/shard_map/ppermute | solution.py:778
  448.9 28.0 %collective-permute-start.43 = (bf16[768,768]{1,0:T(8,128)(2,1)}, bf16[768,768]{1,0:T(8,128)(2,1)}, u32[]{:S(2)}, u32[]{:S(2)}) collective-permute-start(bf16[768,768]{1,0:T(8,128)(2,1)} %add_convert_fusion.9), channel_id=1, source_target_pairs={{0,2},{1,3},{2,0},{3,1},{4,6},{5,7},{6,4},{7,5},{8,10},{9,11},{10,... | collective-permute-start | bytes 3538952 | tf_op jit(solution)/shard_map/ppermute | solution.py:778
  481.3 44.1 %collective-permute-start.49 = (bf16[768,768]{1,0:T(8,128)(2,1)}, bf16[768,768]{1,0:T(8,128)(2,1)}, u32[]{:S(2)}, u32[]{:S(2)}) collective-permute-start(bf16[768,768]{1,0:T(8,128)(2,1)} %add_convert_fusion.4), channel_id=1, source_target_pairs={{0,1},{1,0},{2,3},{3,2},{4,5},{5,4},{6,7},{7,6},{8,9},{9,8},{10,11... | collective-permute-start | bytes 3538952 | tf_op jit(solution)/shard_map/ppermute | solution.py:778
  485.8 39.6 %collective-permute-start.48 = (bf16[768,768]{1,0:T(8,128)(2,1)}, bf16[768,768]{1,0:T(8,128)(2,1)}, u32[]{:S(2)}, u32[]{:S(2)}) collective-permute-start(bf16[768,768]{1,0:T(8,128)(2,1)} %add_convert_fusion.5), channel_id=1, source_target_pairs={{0,2},{1,3},{2,0},{3,1},{4,6},{5,7},{6,4},{7,5},{8,10},{9,11},{10,... | collective-permute-start | bytes 3538952 | tf_op jit(solution)/shard_map/ppermute | solution.py:778
  487.2 38.1 %collective-permute-start.46 = (bf16[384,768]{1,0:T(8,128)(2,1)}, bf16[384,768]{1,0:T(8,128)(2,1)}, u32[]{:S(2)}, u32[]{:S(2)}) collective-permute-start(bf16[384,768]{1,0:T(8,128)(2,1)} %get-tuple-element.429), channel_id=1, source_target_pairs={{0,2},{1,3},{2,0},{3,1},{4,6},{5,7},{6,4},{7,5},{8,10},{9,11},{10,... | collective-permute-start | bytes 1769480 | tf_op jit(solution)/shard_map/ppermute | solution.py:778
  488.7 36.7 %collective-permute-start.47 = (bf16[384,768]{1,0:T(8,128)(2,1)S(1)}, bf16[384,768]{1,0:T(8,128)(2,1)}, u32[]{:S(2)}, u32[]{:S(2)}) collective-permute-start(bf16[384,768]{1,0:T(8,128)(2,1)S(1)} %get-tuple-element.428), channel_id=1, source_target_pairs={{0,1},{1,0},{2,3},{3,2},{4,5},{5,4},{6,7},{7,6},{8,9},{9,8},{10,11... | collective-permute-start | bytes 1769480 | tf_op jit(solution)/shard_map/ppermute | solution.py:778
  493.2 40.9 %collective-permute-start.45 = (bf16[768,768]{1,0:T(8,128)(2,1)}, bf16[768,768]{1,0:T(8,128)(2,1)}, u32[]{:S(2)}, u32[]{:S(2)}) collective-permute-start(bf16[768,768]{1,0:T(8,128)(2,1)} %convolution_convert_fusion.2), channel_id=1, source_target_pairs={{0,4},{4,0},{1,5},{5,1},{2,6},{6,2},{3,7},{7,3},{8,12},{12,8},{9,1... | collective-permute-start | bytes 3538952 | tf_op jit(solution)/shard_map/ppermute | solution.py:778
  534.1 158.6 %reduce-scatter.6.cloned.1.call-start = ((), (), s32[]{:S(2)}) async-start(), calls=%async_computation.6 | async-start | bytes 1474560 | tf_op jit(solution)/shard_map/reduce_scatter | solution.py:895
  539.1 52.9 %collective-permute-start.50 = (bf16[768,768]{1,0:T(8,128)(2,1)}, bf16[768,768]{1,0:T(8,128)(2,1)}, u32[]{:S(2)}, u32[]{:S(2)}) collective-permute-start(bf16[768,768]{1,0:T(8,128)(2,1)} %add_convert_fusion.3), channel_id=1, source_target_pairs={{0,2},{1,3},{2,0},{3,1},{4,6},{5,7},{6,4},{7,5},{8,10},{9,11},{10,... | collective-permute-start | bytes 3538952 | tf_op jit(solution)/shard_map/ppermute | solution.py:778
  543.9 48.2 %collective-permute-start.52 = (bf16[768,768]{1,0:T(8,128)(2,1)}, bf16[768,768]{1,0:T(8,128)(2,1)}, u32[]{:S(2)}, u32[]{:S(2)}) collective-permute-start(bf16[768,768]{1,0:T(8,128)(2,1)} %add_convert_fusion.2), channel_id=1, source_target_pairs={{0,1},{1,0},{2,3},{3,2},{4,5},{5,4},{6,7},{7,6},{8,9},{9,8},{10,11... | collective-permute-start | bytes 3538952 | tf_op jit(solution)/shard_map/ppermute | solution.py:778
  557.0 149.2 %reduce-scatter.8.cloned.1.call-start = ((), (), s32[]{:S(2)}) async-start(), calls=%async_computation.7 | async-start | bytes 1474560 | tf_op jit(solution)/shard_map/reduce_scatter | solution.py:895
  641.9 29.1 %collective-permute-start.61 = (f32[8,128,128]{2,1,0:T(8,128)S(1)}, f32[8,128,128]{2,1,0:T(8,128)S(1)}, u32[]{:S(2)}, u32[]{:S(2)}) collective-permute-start(f32[8,128,128]{2,1,0:T(8,128)S(1)} %slice.426), channel_id=1, source_target_pairs={{0,2},{1,3},{2,0},{3,1},{4,6},{5,7},{6,4},{7,5},{8,10},{9,11},{10,... | collective-permute-start | bytes 1572872 | tf_op jit(solution)/shard_map/ppermute | solution.py:778
  (134 other events, 1290.6 us)
Sparse Core Ops, SparseCore 0:
  10.4 33.1 all-gather.8
  45.8 29.9 all-gather.4
  77.3 29.5 all-gather.6
  534.2 33.2 reduce-scatter.3
  569.6 27.8 reduce-scatter.5
  636.9 29.6 reduce-scatter.7

commit v3 on v2

--- a/solution.py
+++ b/solution.py
@@ -106,6 +106,16 @@
         total = term if total is None else total + term
         at += block.shape[0]
     return total
+
+
+def launch(kernel, args, wait, in_specs, **options):
+    inputs = len(args)
+
+    def body(*refs):
+        kernel(*refs[:inputs], *refs[inputs + len(wait) :])
+
+    in_specs = [*in_specs, *[pl.BlockSpec(memory_space=pl.ANY)] * len(wait)]
+    return pl.pallas_call(body, in_specs=in_specs, **options)(*args, *wait)
 
 
 def split(refs, counts):
@@ -227,14 +237,16 @@
     s_ref[...] = dot(bc_ref[:, :NS], xw_s[...], TN).astype(BF16)
 
 
-def project(g, normed, blocks, conv_w, conv_b, bc, wf):
+def project(g, normed, blocks, conv_w, conv_b, bc, wf, wait=()):
     rows = normed.shape[0] - HALO - TAIL
     ext = rows + HALO
     inner = blocks[0][0].shape[1]
     heads = inner // HEAD
-    tile = 256 if inner % 256 == 0 else LANES
-    return pl.pallas_call(
+    tile = inner
+    return launch(
         functools.partial(proj_kernel, tile, len(blocks)),
+        (normed, *(array for array, _ in blocks), conv_w, conv_b, bc, wf,),
+        wait,
         grid=(1,),
         in_specs=[
             pl.BlockSpec((ext, D), lambda i: (0, 0)),
@@ -258,19 +270,21 @@
         compiler_params=pltpu.CompilerParams(vmem_limit_bytes=VMEM),
         cost_estimate=cost(10),
         name="project",
-    )(normed, *(array for array, _ in blocks), conv_w, conv_b, bc, wf)
+    )
 
 
 def product_kernel(count, n_ref, *refs):
     refs[count][...] = times(n_ref, refs[:count]).astype(BF16)
 
 
-def product(left, blocks):
+def product(left, blocks, wait=()):
     rows = left.shape[0]
     inner = blocks[0][0].shape[1]
     tile = 256 if inner % 256 == 0 else LANES
-    return pl.pallas_call(
+    return launch(
         functools.partial(product_kernel, len(blocks)),
+        (left, *(array for array, _ in blocks),),
+        wait,
         grid=(inner // tile,),
         in_specs=[whole_spec(left), *(pl.BlockSpec((D // 2, tile), functools.partial(lambda index, j: (index, j), index)) for _, index in blocks)],
         out_specs=pl.BlockSpec((rows, tile), lambda j: (0, j)),
@@ -278,7 +292,7 @@
         compiler_params=pltpu.CompilerParams(vmem_limit_bytes=VMEM),
         cost_estimate=cost(4),
         name="product",
-    )(left, *(array for array, _ in blocks))
+    )
 
 
 def scan_kernel(x_ref, bc_ref, c2_ref, cd_ref, cdt_ref, s0_ref, skip_ref, y_ref, sin_ref, state, ya_s, xw_s):
@@ -315,16 +329,18 @@
         state[...] += dot(in_map, xw_s[...], TN)
         return carry
 
-    lax.fori_loop(0, rows // CHUNK, chunk, 0)
-
-
-def scan(g, x, bc, c2, cd, cdt, state, skip):
+    lax.fori_loop(0, rows // CHUNK, chunk, 0, unroll=2)
+
+
+def scan(g, x, bc, c2, cd, cdt, state, skip, wait=()):
     rows = x.shape[0]
     heads = c2.shape[2]
     inner = heads * HEAD
     count = rows // CHUNK
-    return pl.pallas_call(
+    return launch(
         scan_kernel,
+        (x, bc, c2, cd, cdt, state, skip,),
+        wait,
         grid=(1,),
         in_specs=[
             whole_spec(x),
@@ -351,7 +367,7 @@
         compiler_params=pltpu.CompilerParams(vmem_limit_bytes=VMEM),
         cost_estimate=cost(9),
         name="scan",
-    )(x, bc, c2, cd, cdt, state, skip)
+    )
 
 
 def gate_kernel(groups, width, out_counts, z_counts, *refs):
@@ -385,7 +401,7 @@
                 ga_s[here, wide] = gated
                 return sums[0] + gated * gated, sums[1] + gs_s[here, wide] * gain_ref[:, wide] * gated
 
-            squares, dots = lax.fori_loop(0, tiles, measure, (squares, dots))
+            squares, dots = lax.fori_loop(0, tiles, measure, (squares, dots), unroll=True)
         inverse = lax.rsqrt(jnp.sum(squares, axis=1, keepdims=True) / DI + EPSILON)
         pull = inverse * inverse * inverse * (jnp.sum(dots, axis=1, keepdims=True) / DI)
         inverse = jnp.broadcast_to(inverse, (CHUNK, LANES))
@@ -597,7 +613,7 @@
         q_ref[0, :, here] = jnp.concatenate(q_rows, axis=0)
         return carry
 
-    lax.fori_loop(0, count, chunk, 0)
+    lax.fori_loop(0, count, chunk, 0, unroll=2)
     for q in range(heads // 2):
         lanes = slice(q * LANES, (q + 1) * LANES)
         empty = jnp.zeros((HALO, LANES), F32)
@@ -605,14 +621,16 @@
     dpre_ref[HALO + rows :] = jnp.zeros((TAIL, inner), BF16)
 
 
-def back(g, pre, dy, bc, c2, cd, c2t, states, pull, skip, conv_w, conv_b):
+def back(g, pre, dy, bc, c2, cd, c2t, states, pull, skip, conv_w, conv_b, wait=()):
     ext = pre.shape[0]
     rows = ext - HALO
     heads = c2.shape[2]
     inner = heads * HEAD
     count = rows // CHUNK
-    return pl.pallas_call(
+    return launch(
         back_kernel,
+        (pre, dy, bc, c2, cd, c2t, states, pull, skip, conv_w, conv_b,),
+        wait,
         grid=(1,),
         in_specs=[
             whole_spec(pre),
@@ -654,7 +672,7 @@
         compiler_params=pltpu.CompilerParams(vmem_limit_bytes=VMEM),
         cost_estimate=cost(18),
         name="back",
-    )(pre, dy, bc, c2, cd, c2t, states, pull, skip, conv_w, conv_b)
+    )
 
 
 def map_back_kernel(pre_ref, grad_ref, cw_ref, cb_ref, dpre_ref, acc_ref, next_s):
@@ -741,15 +759,17 @@
     natural(gh_ref, grad_s, flag_ref, width)
 
 
-def final(ds, ws, dm, wm, dt, wt, halo, dn, hidden, cot, gain, flag, width):
+def final(ds, ws, dm, wm, dt, wt, halo, dn, hidden, cot, gain, flag, width, wait=()):
     groups = len(ds)
     rows = hidden.shape[0]
     inner = ds[0].shape[1]
     tile = 256
     row = lambda i: (i, 0)
     fixed = lambda i: (0, 0)
-    return pl.pallas_call(
+    return launch(
         functools.partial(final_kernel, groups, width, tuple(map(len, ws))),
+        (*ds, *arrays(ws), dm, wm, dt, wt, halo, dn, hidden, cot, gain, flag,),
+        wait,
         grid=(rows // tile,),
         in_specs=[
             *map(whole_spec, ds),
@@ -771,7 +791,7 @@
         compiler_params=pltpu.CompilerParams(vmem_limit_bytes=VMEM),
         cost_estimate=cost(20),
         name="final",
-    )(*ds, *arrays(ws), dm, wm, dt, wt, halo, dn, hidden, cot, gain, flag)
+    )
 
 
 def across(value, axis, size, bit):
@@ -872,11 +892,6 @@
 
         def send(self, g, right):
             part = self.partial(g, right)
-            if tp == 4 and g == 3 and self.via is None:
-                self.add[1].append(jnp.pad(near(part[:half], 2), ((0, half), (0, 0))))
-                self.add[2].append(jnp.pad(near(part[half:], 1), ((half, 0), (0, 0))))
-                coming.extend([self.add[1][-1], self.add[2][-1]])
-                return part
             if tp == 4 and g == 3:
                 got, at = near(part, 3 - self.via), self.via
             else:
@@ -885,18 +900,20 @@
             coming.append(got)
             return part
 
-        def halves(self, g):
-            return (1, 2) if tp == 4 and g == 3 and self.via is None else (0,)
-
         def finish(self, right):
             return self.partial(0, right)
 
     def scatter(total):
-        return lax.psum_scatter(total, "z", scatter_dimension=0, tiled=True).astype(F32)
+        return lax.psum_scatter(total, "z", scatter_dimension=0, tiled=True)
 
     def everywhere(vector):
-        for axis, size, bit in steps:
-            vector = vector + across(vector, axis, size, bit)
+        for axis, size in (("z", zn), ("tensor", tp), ("core", 2)):
+            if size == 4:
+                one, two, three = (across(vector, axis, size, gap) for gap in (1, 2, 3))
+                vector = (vector + one) + (two + three)
+            else:
+                for bit in bits(size):
+                    vector = vector + across(vector, axis, size, bit)
         return vector
 
     flag = jnp.full((8, LANES), core, F32)
@@ -938,20 +955,12 @@
         a = jnp.pad(a.reshape(tp, heads), ((0, 0), (0, pitch - heads))).reshape(1, tp * pitch)
         return jnp.pad(a, ((0, 0), (0, LANES - tp * pitch)))
 
-    x_near, z_mine = after((x_near, z_mine), normed_ext)
-    x_cut, x_far = send_far(x_near)
-    z_mine = after(z_mine, *x_near)
-    z_own_other, z_near = swap(z_mine), send_own(z_mine)
-    cotangent, conv_weight, conv_bias, step_bias, decay_log, skip_gain, gate_gain = after(
-        (cotangent, conv_weight, conv_bias, step_bias, decay_log, skip_gain, gate_gain), *x_cut
-    )
-    cotangent = to_own(cotangent)
+    skip_gain, gate_gain, cotangent_late = after((skip_gain, gate_gain, cotangent), normed_ext)
     conv_x, bias_x = regroup(conv_weight[:, :DI]), regroup(conv_bias[None, :DI])
     conv_m, bias_m = conv_weight[:, DI:], conv_bias[None, DI:]
-    step_bias, decay_log, skip_gain, gate_gain = (regroup(a[None]) for a in (step_bias, decay_log, skip_gain, gate_gain))
-    skip = jnp.repeat(skip_gain, HEAD, axis=1)
+    step_bias, decay_log = (regroup(a[None]) for a in (step_bias, decay_log))
     pre_m, bc, v, c2, cd, c2t, cdt, wf, ei, total = prep(
-        normed_ext, after(map_w, *x_cut, x_own_other, out_mine, cotangent, conv_x, bias_x, skip, gate_gain), step_w, conv_m, bias_m, per_pitch(step_bias), per_pitch(decay_log), tp, heads, pitch
+        normed_ext, after(map_w, x_own_other, conv_x, bias_x), step_w, conv_m, bias_m, per_pitch(step_bias), per_pitch(decay_log), tp, heads, pitch
     )
     total = total[:, : tp * pitch].reshape(tp, pitch)[:, :heads].reshape(1, H)
     device_decay = jnp.repeat(jnp.exp2(total), HEAD, axis=1)
@@ -983,91 +992,100 @@
     first = []
 
     def run_project(g, *others):
-        pre[g], x[g], local[g] = project(g, after(normed_ext, *others), x_w[g], conv_x, bias_x, bc, wf)
+        pre[g], x[g], local[g] = project(g, normed_ext, x_w[g], conv_x, bias_x, bc, wf, others)
         first.append(pass_on(local[g], forward, g))
 
     def run_scan(g, *others):
-        y[g], states[g] = scan(g, after(x[g], *others), bc, c2, cd, cdt, start[g], skip)
-
+        y[g], states[g] = scan(g, x[g], bc, c2, cd, cdt, start[g], skip, others)
+
+    cotangent, skip_gain, gate_gain = after((cotangent_late, skip_gain, gate_gain), bc)
+    cotangent, skip_gain, gate_gain = to_own(cotangent), regroup(skip_gain[None]), regroup(gate_gain[None])
+    skip = jnp.repeat(skip_gain, HEAD, axis=1)
+    x_near, z_mine = after((x_near, z_mine), bc, cotangent)
+    x_cut, x_far = send_far(x_near)
+    z_mine = after(z_mine, *x_cut)
+    z_own_other, z_near = swap(z_mine), send_own(z_mine)
     x_w = [[(x_mine, 0), (x_own_other, 0)]]
-    run_project(0)
+    run_project(0, *x_cut)
     x_rest = jnp.concatenate(after(x_near + x_far, x[0]), axis=0)
     x_w = places(x_mine, x_own_other, x_rest)
-    z = [product(after(normed, x_rest, z_own_other), [(z_mine, 0), (z_own_other, 0)])]
-    run_project(1, z[0], x_w[1][1][0])
+    run_project(1, x_w[1][1][0], skip, gate_gain, z_own_other)
     z_near = after(z_near, x[1], *first[0].values())
     z_cut, z_far = send_far(z_near)
     if tp > 2:
-        run_project(2, *z_cut)
+        run_project(2, x[1], out_mine, *z_cut)
     z_rest = jnp.concatenate(after(z_near + z_far, x[min(2, tp - 1)], *first[1].values()), axis=0)
     z_w = places(z_mine, z_own_other, z_rest)
     for g in range(3, tp):
         run_project(g, z_rest, x[g - 1])
-    z.append(product(after(normed, x[tp - 1], z_w[1][1][0], *first[-2].values()), z_w[1]))
-    start = after(chain(local, first, forward), z[1])
+    z = [product(normed, z_w[0], (x[tp - 1], *first[-2].values()))]
+    start = chain(local, first, forward)
     out_mine = after(out_mine, *start)
     out_own_other, out_near = swap(out_mine), send_own(out_mine)
-    run_scan(0)
-    run_scan(1, y[0], out_own_other)
+    run_scan(0, z[0])
+    run_scan(1, y[0], out_own_other, z_w[1][1][0])
     out_near = after(out_near, y[1])
     out_cut, out_far = send_far(out_near)
     if tp > 2:
-        run_scan(2, *out_cut)
+        run_scan(2, y[1], *out_cut)
     out_rest = jnp.concatenate(after(out_near + out_far, y[min(2, tp - 1)]), axis=0)
     out_w = places(out_mine, out_own_other, out_rest)
     for g in range(3, tp):
         run_scan(g, out_rest, y[g - 1])
-    normed_late = after(normed, y[tp - 1], out_rest, out_w[1][1][0])
-    z += [product(normed_late, z_w[g]) for g in range(2, tp)]
+    z += [product(normed, z_w[g], (y[tp - 1], out_w[1][1][0])) for g in range(1, tp)]
 
     scaled, dy, dz, local_pull, block_out, dn_z, gain_sums = gate(
         y, z, out_w, z_w, cotangent, hidden, gate_gain, bc, ei, flag, width
     )
     pulls = chain(local_pull, [pass_on(local_pull[g ^ 1], backward, g ^ 1) for g in reversed(groups)], backward)
-    out_grad, z_grad, x_grad = Scatter(cotangent, 1), Scatter(normed, 2), Scatter(normed_ext, None)
+    out_grad, z_grad, x_grad = Scatter(cotangent, 1), Scatter(normed, 2), Scatter(normed_ext, 1)
     dpre, dbc, sums, q, da = ([None] * tp for _ in range(5))
     last = tp - 1
     order = list(reversed(groups))
     swapped = [out_grad.swap(last, scaled[last]), z_grad.swap(last, dz[last])]
-    swapped += [out_grad.swap(g, after(scaled[g], *swapped)) for g in order[1:]]
-    ready = swapped + pulls
-    waiting = ready + [out_grad.send(last, after(scaled[last], *ready)), z_grad.send(last, after(dz[last], *ready))]
-    later = []
+    far_out = out_grad.send(last, after(scaled[last], *swapped))
+    ready = [out_grad.swap(g, after(scaled[g], far_out)) for g in order[1:]]
+    far_z = z_grad.send(last, after(dz[last], *ready, *pulls))
+    waiting = ready + [far_out, far_z] + pulls
+    finished = []
     for at, g in enumerate(order):
         dpre[g], dbc[g], sums[g], q[g], da[g] = back(
-            g, pre[g], after(dy[g], *waiting), bc, c2, cd, c2t, states[g], pulls[g], skip, conv_x, bias_x
+            g, pre[g], dy[g], bc, c2, cd, c2t, states[g], pulls[g], skip, conv_x, bias_x, waiting
         )
-        arrivals = [dpre[g]] + coming
+        arrivals = [dpre[g]] + coming + finished
         coming.clear()
-        now = lambda value: after(value, *arrivals)
         waiting = []
+        now = lambda value: after(value, *arrivals, *waiting)
+        if at == 0:
+            waiting += [out_grad.send(i, now(scaled[i])) for i in order[1:-1]]
+        if at == 1:
+            waiting.append(x_grad.send(order[0], now(dpre[order[0]])))
+        if at == last - 1 and at > 0:
+            waiting += [x_grad.send(i, now(dpre[i])) for i in order[1:-2]]
         if at < last:
             waiting.append(x_grad.swap(g, now(dpre[g])))
         if at == 0:
-            waiting += [out_grad.send(i, now(scaled[i])) for i in order[1:-1]]
+            waiting += [z_grad.swap(i, now(dz[i])) for i in order[1:]]
+            waiting += [z_grad.send(i, now(dz[i])) for i in order[1:-1]]
+            del coming[-len(order[1:-1]) :]
+        if at == last - 1 and at > 0:
             waiting.append(x_grad.send(g, now(dpre[g])))
-            later, coming[:] = coming[-len(x_grad.halves(g)) :], coming[: -len(x_grad.halves(g))]
-            waiting += [z_grad.swap(i, now(dz[i])) for i in order[1:]]
         if at == 1:
-            coming += later
             total = out_grad.finish(now(scaled[0]))
-            waiting, total = lax.optimization_barrier((waiting, total))
+            waiting.append(total)
             grad_out = scatter(total)
-            waiting += [z_grad.send(i, now(dz[i])) for i in order[1:-1]]
-        if at == last - 1:
-            waiting += [x_grad.send(i, now(dpre[i])) for i in order[1:-1]]
+            total = z_grad.finish(now(dz[0]))
+            waiting.append(total)
+            grad_z = scatter(total)
+            finished = [grad_out]
         if at == min(2, last):
-            total = z_grad.finish(now(dz[0]))
-            waiting, total = lax.optimization_barrier((waiting, total))
-            grad_z = scatter(total)
-            waiting.append(grad_out)
+            finished = [grad_z]
     x_grad.swap(0, now(dpre[0]))
     total = x_grad.finish(now(dpre[0]))
+    grad_x = scatter(total)
     q, da, sums = after((q, da, sums), total)
-    dbc_all, total = lax.optimization_barrier((after(functools.reduce(jnp.add, dbc), *waiting), total))
-    grad_x = scatter(total)
+    dbc_all = after(functools.reduce(jnp.add, dbc), total)
     dpre_m, sums_m = map_back(pre_m, dbc_all, conv_m, bias_m)
-    dn_z = after(dn_z, grad_z)
 
     v = v.reshape(H, rows)
     q, da = (jnp.concatenate(a, axis=0).reshape(H, rows) for a in (q, da))
@@ -1087,22 +1105,27 @@
     grad_step = dot(dstep_t[: tp * pitch], normed).reshape(tp, pitch, 2, zn, width)[:, :heads]
     grad_step = strip(pad_step(jnp.transpose(grad_step, (2, 3, 0, 1, 4)).reshape(-1, heads, width)))
     grad_small = jnp.concatenate([grad_map, pick(grad_step, group_order, 0)], axis=-2)
-    for axis, count, bit in reversed(steps):
-        keep = grad_small.shape[0] // 2
-        grad_small = grad_small[:keep] + across(grad_small[keep:], axis, count, bit)
-    grad_small = grad_small[0]
-    map_shard = jnp.concatenate([grad_small[:map_rows], grad_small[map_rows : 2 * map_rows]], axis=1)
-    step_shard = grad_small[2 * map_rows :].reshape(strips, pitch, LANES)
-    step_shard = jnp.concatenate([step_shard[i] for i in range(strips)], axis=1)[:heads, :width].T
-
+    def to_owners(parts, axis, count):
+        parts = parts.reshape((count, -1) + parts.shape[1:])
+        total = parts[0]
+        for gap in range(1, count):
+            total = total + across(parts[gap], axis, count, gap)
+        return total
+
+    grad_small = to_owners(grad_small, "core", 2)
     halo = jnp.zeros((HALO, DI + 2 * NS), BF16)
     edge = jnp.concatenate([a[:HALO] for a in dpre + [dpre_m]], axis=1)
     for gap in sorted({i ^ j for i, j in backward}):
         part = lax.ppermute(edge, "tensor", [(i, j) for i, j in backward if i ^ j == gap])
         halo = halo + jnp.concatenate([part[:, span_of(g ^ gap)] for g in groups] + [part[:, DI:]], axis=1)
     grad_hidden, norm_sums = final(
-        dpre, x_w, dpre_m, map_w, dstep_rows, step_w, halo, dn_z, hidden, cotangent, norm_gain[None], flag, width
-    )
+        dpre, x_w, dpre_m, map_w, dstep_rows, step_w, halo, dn_z, hidden, cotangent, norm_gain[None], flag, width, (grad_x,)
+    )
+    grad_small = to_owners(to_owners(after(grad_small, norm_sums), "tensor", tp), "z", zn)[0]
+    map_shard = jnp.concatenate([grad_small[:map_rows], grad_small[map_rows : 2 * map_rows]], axis=1)
+    step_shard = grad_small[2 * map_rows :].reshape(strips, pitch, LANES)
+    step_shard = jnp.concatenate([step_shard[i] for i in range(strips)], axis=1)[:heads, :width].T
+
     fold8 = lambda a: a.reshape(-1, 8, a.shape[-1]).sum(1)
     sums = jnp.concatenate([fold8(part) for part in sums], axis=1)
     taps = jnp.concatenate([regroup(sums[:5]), fold8(sums_m)], axis=1)
@@ -1114,7 +1137,7 @@
         ]
     )
     vector = [taps.reshape(-1), regroup(per_head).reshape(-1), regroup(fold8(gain_sums))[0]]
-    vector = everywhere(after(jnp.concatenate(vector + [from_own(jnp.sum(norm_sums, axis=0))]), grad_x))
+    vector = everywhere(jnp.concatenate(vector + [from_own(jnp.sum(norm_sums, axis=0))]))
     wide = DI + 2 * NS
     cuts = [KW * wide, wide, H, H, H, DI, D]
     parts, at = [], 0
@@ -1125,7 +1148,7 @@
         block_out,
         grad_hidden,
         parts[6],
-        jnp.stack([grad_z, grad_x], axis=1),
+        jnp.stack([grad_z, grad_x], axis=1).astype(F32),
         step_shard,
         map_shard,
         parts[0].reshape(KW, wide),
@@ -1134,7 +1157,7 @@
         parts[3],
         parts[4],
         parts[5],
-        grad_out,
+        grad_out.astype(F32),
     )
 
 

time: 723 us -> 715 us (0.989)
  Pallas kernels: 315 us -> 288 us
  local copies, waits for them, and re-layouts: 93.3 us -> 108 us
  other arithmetic: 28.4 us -> 35.8 us
  starting transfers between devices: 71 us -> 78.3 us
    pallas_call x17, Pallas kernels: 233 us -> 216 us  [launch(): return pl.pallas_call(body, in_specs=in_specs, **options)(*args, *wait)]
    all_gather x1, waiting for transfers between devices: 13 us -> 0.01 us  [shards(): z_mine = lax.all_gather(after(shard_z, shard_x), 'z', axis=0, tiled=True)]
    ppermute x55 -> x58, waiting for transfers between devices: 67.1 us -> 77.6 us  [across(): return lax.ppermute(value, axis, [(i, i ^ bit) for i in range(size)])]
    reduce_scatter x3, waiting for transfers between devices: 10.5 us -> 0.02 us  [scatter(): return lax.psum_scatter(total, 'z', scatter_dimension=0, tiled=True)]
    pallas_call x1, Pallas kernels: 67.2 us -> 58.1 us  [gate(): pl.pallas_call(functools.partial(gate_kernel, groups, width, tuple(map(le...]
    ppermute x8, waiting for transfers between devices: 21.3 us -> 28.8 us  [pass_on(): lax.ppermute(value, 'tensor', [(i, j) for i, j in pairs if i ^ j == gap])]
    unnamed x200 -> x188, local copies, waits for them, and re-layouts: 31.3 us -> 38.6 us
    ppermute x55 -> x58, starting transfers between devices: 49.7 us -> 54.6 us  [across(): return lax.ppermute(value, axis, [(i, i ^ bit) for i in range(size)])]
  transfers between devices with their start and end apart: 71 -> 74, of which waited for: 31 -> 31; matrix products, arithmetic and copies ran while one was open for 23% -> 20% of each run, Pallas kernels for 33% -> 30%
where the time goes in v3:
time: 715 us; the launch traced here: 707 us
  Pallas kernels  288 us (40%)
  local copies, waits for them, and re-layouts  108 us (15%)
  waiting for transfers between devices  107 us (15%)
  starting transfers between devices  78.3 us (11%)
  matrix products  74.5 us (10%)
  other arithmetic  35.8 us (5%)
  between operations  16.2 us (2%)
    pallas_call x17, Pallas kernels, launch(): return pl.pallas_call(body, in_specs=in_specs, **options)(*args, *wait)  216 us
    ppermute x58, waiting for transfers between devices, across(): return lax.ppermute(value, axis, [(i, i ^ bit) for i in range(size)])  77.6 us
    dot_general x26, matrix products, dot(): lax.dot_general(a, b, dims, precision=precision, preferred_element_type=F32)  74.5 us
    pallas_call x1, Pallas kernels, gate(): pl.pallas_call(functools.partial(gate_kernel, groups, width, tuple(map(le...  58.1 us
    ppermute x58, starting transfers between devices, across(): return lax.ppermute(value, axis, [(i, i ^ bit) for i in range(size)])  54.6 us
    unnamed x188, local copies, waits for them, and re-layouts  38.6 us
    ppermute x8, waiting for transfers between devices, pass_on(): lax.ppermute(value, 'tensor', [(i, j) for i, j in pairs if i ^ j == gap])  28.8 us
    ppermute x8, starting transfers between devices, pass_on(): lax.ppermute(value, 'tensor', [(i, j) for i, j in pairs if i ^ j == gap])  18.3 us
  transfers between devices with their start and end apart: 74, of which 31 were waited for; matrix products, arithmetic and copies ran while one was open for 20% of the time, Pallas kernels for 30%

profile of v3, /device:TPU:0, one launch (start us, length us, event | category | flops | bytes accessed | tf_op | source)
XLA Modules:
  0.0 707.4 jit_solution(6036890095076647947)
XLA Ops:
  66.5 10.6 %prep.1 = (bf16[1040,256]{1,0:T(8,128)(2,1)}, bf16[1024,256]{1,0:T(8,128)(2,1)}, f32[4,12,1024]{2,1,0:T(8,128)}, f32[4,1024,12]{2,1,0:T(8,128)}, f32[4,1024,12]{...) custom-call(bf16[1152,1536]{1,0:T(8,128)(2,1)} %pad.40.n_ref.refs_0_, ...), custom_call_target="tpu_custom_call" | custom-call | bytes 11 | tf_op jit(solution)/shard_map/prep/pallas_call | solution.py:192
  94.0 9.7 %project.4 = (bf16[1040,768]{1,0:T(8,128)(2,1)}, bf16[1024,768]{1,0:T(8,128)(2,1)}, bf16[128,768]{1,0:T(8,128)(2,1)}) custom-call(bf16[1152,1536]{1,0:T(8,128)(2,1)} %pad.40.n_ref.refs_0_, bf16[768,768]{1,0:T(8,128)(2,1)} %bitcast.163, bf16[768,768]{1,0:T(8,128)(2,1)} %copy-done.10, f32[4,3072]{1,0:T(4,128)} %broadcast_select_fusion.5.refs_3_.refs_9_, ...), custom_call_target="tpu_custom_call" | custom-call | bytes 10 | tf_op jit(solution)/shard_map/project/pallas_call | solution.py:118
  129.7 9.7 %project.5 = (bf16[1040,768]{1,0:T(8,128)(2,1)}, bf16[1024,768]{1,0:T(8,128)(2,1)}, bf16[128,768]{1,0:T(8,128)(2,1)}) custom-call(bf16[1152,1536]{1,0:T(8,128)(2,1)} %pad.40.n_ref.refs_0_, bf16[2304,768]{1,0:T(8,128)(2,1)} %constant_dynamic-update-slice_fusion.12.refs_1_.refs_6_.refs_8_.refs_10_, bf16[2304,768]{1,0:T(8,128)(2,1)} %copy-done.1, ...), custom_call_target="tpu_custom_call" | custom-call | bytes 10 | tf_op jit(solution)/shard_map/project/pallas_call | solution.py:118
  139.5 6.1 collective-permute-done.16.refs_5_
  153.1 9.7 %project.6 = (bf16[1040,768]{1,0:T(8,128)(2,1)}, bf16[1024,768]{1,0:T(8,128)(2,1)}, bf16[128,768]{1,0:T(8,128)(2,1)}) custom-call(bf16[1152,1536]{1,0:T(8,128)(2,1)} %pad.40.n_ref.refs_0_, bf16[2304,768]{1,0:T(8,128)(2,1)} %constant_dynamic-update-slice_fusion.12.refs_1_.refs_6_.refs_8_.refs_10_, bf16[2304,768]{1,0:T(8,128)(2,1)} %copy-done.1, ...), custom_call_target="tpu_custom_call" | custom-call | bytes 10 | tf_op jit(solution)/shard_map/project/pallas_call | solution.py:118
  175.2 9.8 %project.7 = (bf16[1040,768]{1,0:T(8,128)(2,1)}, bf16[1024,768]{1,0:T(8,128)(2,1)}, bf16[128,768]{1,0:T(8,128)(2,1)}) custom-call(bf16[1152,1536]{1,0:T(8,128)(2,1)} %pad.40.n_ref.refs_0_, bf16[2304,768]{1,0:T(8,128)(2,1)} %constant_dynamic-update-slice_fusion.12.refs_1_.refs_6_.refs_8_.refs_10_, bf16[2304,768]{1,0:T(8,128)(2,1)} %copy-done.1, ...), custom_call_target="tpu_custom_call" | custom-call | bytes 10 | tf_op jit(solution)/shard_map/project/pallas_call | solution.py:118
  199.7 6.3 product.4.refs_7_.refs_4_
  206.0 9.8 %scan.4 = (bf16[1024,768]{1,0:T(8,128)(2,1)}, bf16[8,128,768]{2,1,0:T(8,128)(2,1)}) custom-call(bf16[1024,768]{1,0:T(8,128)(2,1)} %get-tuple-element.182.refs_0_, bf16[1024,256]{1,0:T(8,128)(2,1)} %get-tuple-element.170.refs_5_.refs_1_.refs_27_.refs_2_, f32[4,1024,12]{2,1,0:T(8,128)} %get-tuple-element.183.refs_2_.refs_3_, ...), custom_call_target="tpu_custom_call" | custom-call | bytes 9 | tf_op jit(solution)/shard_map/scan/pallas_call | solution.py:118
  216.8 9.7 %scan.5 = (bf16[1024,768]{1,0:T(8,128)(2,1)}, bf16[8,128,768]{2,1,0:T(8,128)(2,1)}) custom-call(bf16[1024,768]{1,0:T(8,128)(2,1)} %get-tuple-element.195.refs_7_.refs_0_, bf16[1024,256]{1,0:T(8,128)(2,1)} %get-tuple-element.170.refs_5_.refs_1_.refs_27_.refs_2_, f32[4,1024,12]{2,1,0:T(8,128)} %get-tuple-element.183.refs_2_.refs_3_, ...), custom_call_target="tpu_custom_call" | custom-call | bytes 9 | tf_op jit(solution)/shard_map/scan/pallas_call | solution.py:118
  229.8 9.7 %scan.6 = (bf16[1024,768]{1,0:T(8,128)(2,1)}, bf16[8,128,768]{2,1,0:T(8,128)(2,1)}) custom-call(bf16[1024,768]{1,0:T(8,128)(2,1)} %get-tuple-element.200.refs_8_.refs_0_, bf16[1024,256]{1,0:T(8,128)(2,1)} %get-tuple-element.170.refs_5_.refs_1_.refs_27_.refs_2_, f32[4,1024,12]{2,1,0:T(8,128)} %get-tuple-element.183.refs_2_.refs_3_, ...), custom_call_target="tpu_custom_call" | custom-call | bytes 9 | tf_op jit(solution)/shard_map/scan/pallas_call | solution.py:118
  254.6 9.8 %scan.7 = (bf16[1024,768]{1,0:T(8,128)(2,1)}, bf16[8,128,768]{2,1,0:T(8,128)(2,1)}) custom-call(bf16[1024,768]{1,0:T(8,128)(2,1)} %get-tuple-element.205.refs_3_.refs_0_, bf16[1024,256]{1,0:T(8,128)(2,1)} %get-tuple-element.170.refs_5_.refs_1_.refs_27_.refs_2_, f32[4,1024,12]{2,1,0:T(8,128)} %get-tuple-element.183.refs_2_.refs_3_, ...), custom_call_target="tpu_custom_call" | custom-call | bytes 9 | tf_op jit(solution)/shard_map/scan/pallas_call | solution.py:118
  266.2 6.3 product.7.refs_7_
  272.5 6.3 product.6.refs_6_
  278.8 6.3 product.5.refs_5_
  285.7 58.1 %gate.1 = (bf16[1024,768]{1,0:T(8,128)(2,1)}, bf16[1024,768]{1,0:T(8,128)(2,1)}, bf16[1024,768]{1,0:T(8,128)(2,1)}, bf16[1024,768]{1,0:T(8,128)(2,1)}, bf16[1024...) custom-call(bf16[1024,768]{1,0:T(8,128)(2,1)} %get-tuple-element.207, ...), custom_call_target="tpu_custom_call" | custom-call | bytes 55 | tf_op jit(solution)/shard_map/gate/pallas_call | solution.py:478
  361.9 7.0 collective-permute-done.28.refs_16_.refs_7_
  383.7 21.7 %back.4 = (bf16[1152,768]{1,0:T(8,128)(2,1)}, f32[1024,256]{1,0:T(8,128)}, f32[48,768]{1,0:T(8,128)}, f32[1,12,1024]{2,1,0:T(8,128)}, f32[1,12,1024]{2,1,0:T(8,128)}) custom-call(bf16[1040,768]{1,0:T(8,128)(2,1)} %get-tuple-element.231.refs_0_, bf16[1024,768]{1,0:T(8,128)(2,1)} %get-tuple-element.232.refs_1_, ...), custom_call_target="tpu_custom_call" | custom-call | bytes 18 | tf_op jit(solution)/shard_map/back/pallas_call | solution.py:118
  405.4 5.1 collective-permute-done.38
  438.2 22.2 %back.5 = (bf16[1152,768]{1,0:T(8,128)(2,1)}, f32[1024,256]{1,0:T(8,128)}, f32[48,768]{1,0:T(8,128)}, f32[1,12,1024]{2,1,0:T(8,128)}, f32[1,12,1024]{2,1,0:T(8,128)}) custom-call(bf16[1040,768]{1,0:T(8,128)(2,1)} %get-tuple-element.226.refs_0_, bf16[1024,768]{1,0:T(8,128)(2,1)} %get-tuple-element.227.refs_1_, ...), custom_call_target="tpu_custom_call" | custom-call | bytes 18 | tf_op jit(solution)/shard_map/back/pallas_call | solution.py:118
  480.4 22.5 %collective-permute-done.47 = bf16[768,768]{1,0:T(8,128)(2,1)S(1)} collective-permute-done((bf16[768,768]{1,0:T(8,128)(2,1)}, bf16[768,768]{1,0:T(8,128)(2,1)S(1)}, u32[]{:S(2)}, u32[]{:S(2)}) %collective-permute-start.47) | collective-permute-done | bytes 1179680 | tf_op jit(solution)/shard_map/ppermute | solution.py:798
  507.4 21.8 %back.6 = (bf16[1152,768]{1,0:T(8,128)(2,1)}, f32[1024,256]{1,0:T(8,128)}, f32[48,768]{1,0:T(8,128)}, f32[1,12,1024]{2,1,0:T(8,128)}, f32[1,12,1024]{2,1,0:T(8,128)}) custom-call(bf16[1040,768]{1,0:T(8,128)(2,1)} %get-tuple-element.258.refs_0_, bf16[1024,768]{1,0:T(8,128)(2,1)} %get-tuple-element.259.refs_1_, ...), custom_call_target="tpu_custom_call" | custom-call | bytes 18 | tf_op jit(solution)/shard_map/back/pallas_call | solution.py:118
  554.9 21.7 %back.7 = (bf16[1152,768]{1,0:T(8,128)(2,1)}, f32[1024,256]{1,0:T(8,128)}, f32[48,768]{1,0:T(8,128)}, f32[1,12,1024]{2,1,0:T(8,128)}, f32[1,12,1024]{2,1,0:T(8,128)}) custom-call(bf16[1040,768]{1,0:T(8,128)(2,1)} %get-tuple-element.221.refs_0_, bf16[1024,768]{1,0:T(8,128)(2,1)} %get-tuple-element.222.refs_1_, ...), custom_call_target="tpu_custom_call" | custom-call | bytes 18 | tf_op jit(solution)/shard_map/back/pallas_call | solution.py:118
  631.5 25.2 %final.1 = (f32[1024,1536]{1,0:T(8,128)}, f32[8,1536]{1,0:T(8,128)}) custom-call(bf16[1152,768]{1,0:T(8,128)(2,1)} %get-tuple-element.275.refs_0_, bf16[1152,768]{1,0:T(8,128)(2,1)} %get-tuple-element.268.refs_1_, bf16[1152,768]{1,0:T(8,128)(2,1)} %get-tuple-element.266.refs_2_, bf16[1152,768]{1,0:T(8,128)(2,1)} %get-tuple-element.261.refs_3_, ...), custom_call_target="tpu_custom_call" | custom-call | bytes 20 | tf_op jit(solution)/shard_map/final/pallas_call | solution.py:118
  662.8 6.7 collective-permute-done.55
  (542 shorter events, 359.3 us)
Async XLA Ops:
  7.2 52.2 %all-gather.9.cloned.1.call-start = ((), (), s32[]{:S(2)}) async-start(), calls=%async_computation.8 | async-start | bytes 1474560 | tf_op jit(solution)/shard_map/all_gather | solution.py:921
  10.3 78.6 %all-gather.5.cloned.1.call-start = ((), (), s32[]{:S(2)}) async-start(), calls=%async_computation.3 | async-start | bytes 1474560 | tf_op jit(solution)/shard_map/all_gather | solution.py:922
  14.3 138.8 %all-gather.7.cloned.1.call-start = ((), (), s32[]{:S(2)}) async-start(), calls=%async_computation.4 | async-start | bytes 1474560 | tf_op jit(solution)/shard_map/all_gather | solution.py:923
  59.5 29.5 %collective-permute-start.7 = (bf16[768,768]{1,0:T(8,128)(2,1)}, bf16[768,768]{1,0:T(8,128)(2,1)}, u32[]{:S(2)}, u32[]{:S(2)}) collective-permute-start(bf16[768,768]{1,0:T(8,128)(2,1)} %bitcast.161), channel_id=1, source_target_pairs={{0,1},{1,0},{2,3},{3,2},{4,5},{5,4},{6,7},{7,6},{8,9},{9,8},{10,11... | collective-permute-start | bytes 3538952 | tf_op jit(solution)/shard_map/ppermute | solution.py:798
  59.6 29.4 %collective-permute-start.8 = (bf16[768,768]{1,0:T(8,128)(2,1)}, bf16[768,768]{1,0:T(8,128)(2,1)}, u32[]{:S(2)}, u32[]{:S(2)}) collective-permute-start(bf16[768,768]{1,0:T(8,128)(2,1)} %bitcast.162), channel_id=1, source_target_pairs={{0,2},{1,3},{2,0},{3,1},{4,6},{5,7},{6,4},{7,5},{8,10},{9,11},{10,... | collective-permute-start | bytes 3538952 | tf_op jit(solution)/shard_map/ppermute | solution.py:798
  115.3 30.3 %collective-permute-start.14 = (bf16[768,768]{1,0:T(8,128)(2,1)}, bf16[768,768]{1,0:T(8,128)(2,1)}, u32[]{:S(2)}, u32[]{:S(2)}) collective-permute-start(bf16[768,768]{1,0:T(8,128)(2,1)} %all-gather.5.cloned.1.call-done.refs_1_.refs_16_), channel_id=1, source_target_pairs={{0,1},{1,0},{2,3},{3,2},{4,5},{5,4},{6,7},{7,6},{8,9},{9,8},{10,11... | collective-permute-start | bytes 3538952 | tf_op jit(solution)/shard_map/ppermute | solution.py:798
  115.7 29.9 %collective-permute-start.15 = (bf16[768,768]{1,0:T(8,128)(2,1)}, bf16[768,768]{1,0:T(8,128)(2,1)}, u32[]{:S(2)}, u32[]{:S(2)}) collective-permute-start(bf16[768,768]{1,0:T(8,128)(2,1)} %all-gather.5.cloned.1.call-done.refs_1_.refs_16_), channel_id=1, source_target_pairs={{0,2},{1,3},{2,0},{3,1},{4,6},{5,7},{6,4},{7,5},{8,10},{9,11},{10,... | collective-permute-start | bytes 3538952 | tf_op jit(solution)/shard_map/ppermute | solution.py:798
  116.2 413.0 %reduce-scatter.4.cloned.1.call-start = ((), (), s32[]{:S(2)}) async-start(), calls=%async_computation.5 | async-start | bytes 1474560 | tf_op jit(solution)/shard_map/reduce_scatter | solution.py:907
  169.9 45.9 %collective-permute-start.22 = (bf16[2304,768]{1,0:T(8,128)(2,1)S(1)}, bf16[2304,768]{1,0:T(8,128)(2,1)}, u32[]{:S(2)}, u32[]{:S(2)}) collective-permute-start(bf16[2304,768]{1,0:T(8,128)(2,1)S(1)} %constant_dynamic-update-slice_fusion.16.refs_7_.refs_1_.refs_18_.refs_20_.refs_22_), channel_id=1, source_target_pairs={{0,4},{4,0},{1,5},{5,1},{2,6},{6,2},{3,7},{7,3},{8,12},{12,8},{9,1... | collective-permute-start | bytes 10616840 | tf_op jit(solution)/shard_map/ppermute | solution.py:798
  190.7 35.8 %collective-permute-start.23 = (bf16[768,768]{1,0:T(8,128)(2,1)S(1)}, bf16[768,768]{1,0:T(8,128)(2,1)}, u32[]{:S(2)}, u32[]{:S(2)}) collective-permute-start(bf16[768,768]{1,0:T(8,128)(2,1)S(1)} %copy-done.11), channel_id=1, source_target_pairs={{0,1},{1,0},{2,3},{3,2},{4,5},{5,4},{6,7},{7,6},{8,9},{9,8},{10,11... | collective-permute-start | bytes 3538952 | tf_op jit(solution)/shard_map/ppermute | solution.py:798
  193.2 33.3 %collective-permute-start.24 = (bf16[768,768]{1,0:T(8,128)(2,1)S(1)}, bf16[768,768]{1,0:T(8,128)(2,1)}, u32[]{:S(2)}, u32[]{:S(2)}) collective-permute-start(bf16[768,768]{1,0:T(8,128)(2,1)S(1)} %copy-done.11), channel_id=1, source_target_pairs={{0,2},{1,3},{2,0},{3,1},{4,6},{5,7},{6,4},{7,5},{8,10},{9,11},{10,... | collective-permute-start | bytes 3538952 | tf_op jit(solution)/shard_map/ppermute | solution.py:798
  355.6 25.4 %collective-permute-start.35 = (bf16[768,768]{1,0:T(8,128)(2,1)S(1)}, bf16[768,768]{1,0:T(8,128)(2,1)}, u32[]{:S(2)}, u32[]{:S(2)}) collective-permute-start(bf16[768,768]{1,0:T(8,128)(2,1)S(1)} %convolution_convert_fusion.7), channel_id=1, source_target_pairs={{0,4},{4,0},{1,5},{5,1},{2,6},{6,2},{3,7},{7,3},{8,12},{12,8},{9,1... | collective-permute-start | bytes 3538952 | tf_op jit(solution)/shard_map/ppermute | solution.py:798
  376.9 28.5 %collective-permute-start.37 = (bf16[768,768]{1,0:T(8,128)(2,1)}, bf16[768,768]{1,0:T(8,128)(2,1)}, u32[]{:S(2)}, u32[]{:S(2)}) collective-permute-start(bf16[768,768]{1,0:T(8,128)(2,1)} %add_convert_fusion.11.refs_14_), channel_id=1, source_target_pairs={{0,2},{1,3},{2,0},{3,1},{4,6},{5,7},{6,4},{7,5},{8,10},{9,11},{10,... | collective-permute-start | bytes 3538952 | tf_op jit(solution)/shard_map/ppermute | solution.py:798
  383.6 26.9 %collective-permute-start.38 = (bf16[768,768]{1,0:T(8,128)(2,1)}, bf16[768,768]{1,0:T(8,128)(2,1)}, u32[]{:S(2)}, u32[]{:S(2)}) collective-permute-start(bf16[768,768]{1,0:T(8,128)(2,1)} %add_convert_fusion.10.refs_15_), channel_id=1, source_target_pairs={{0,1},{1,0},{2,3},{3,2},{4,5},{5,4},{6,7},{7,6},{8,9},{9,8},{10,11... | collective-permute-start | bytes 3538952 | tf_op jit(solution)/shard_map/ppermute | solution.py:798
  429.0 31.4 %collective-permute-start.44 = (bf16[768,768]{1,0:T(8,128)(2,1)}, bf16[768,768]{1,0:T(8,128)(2,1)}, u32[]{:S(2)}, u32[]{:S(2)}) collective-permute-start(bf16[768,768]{1,0:T(8,128)(2,1)} %add_convert_fusion.8.refs_12_), channel_id=1, source_target_pairs={{0,1},{1,0},{2,3},{3,2},{4,5},{5,4},{6,7},{7,6},{8,9},{9,8},{10,11... | collective-permute-start | bytes 3538952 | tf_op jit(solution)/shard_map/ppermute | solution.py:798
  429.3 31.1 %collective-permute-start.43 = (bf16[768,768]{1,0:T(8,128)(2,1)}, bf16[768,768]{1,0:T(8,128)(2,1)}, u32[]{:S(2)}, u32[]{:S(2)}) collective-permute-start(bf16[768,768]{1,0:T(8,128)(2,1)} %add_convert_fusion.9.refs_11_), channel_id=1, source_target_pairs={{0,2},{1,3},{2,0},{3,1},{4,6},{5,7},{6,4},{7,5},{8,10},{9,11},{10,... | collective-permute-start | bytes 3538952 | tf_op jit(solution)/shard_map/ppermute | solution.py:798
  474.5 102.1 %reduce-scatter.6.cloned.1.call-start = ((), (), s32[]{:S(2)}) async-start(), calls=%async_computation.6 | async-start | bytes 1474560 | tf_op jit(solution)/shard_map/reduce_scatter | solution.py:907
  474.6 28.3 %collective-permute-start.47 = (bf16[768,768]{1,0:T(8,128)(2,1)}, bf16[768,768]{1,0:T(8,128)(2,1)S(1)}, u32[]{:S(2)}, u32[]{:S(2)}) collective-permute-start(bf16[768,768]{1,0:T(8,128)(2,1)} %add_convert_fusion.6.refs_18_), channel_id=1, source_target_pairs={{0,1},{1,0},{2,3},{3,2},{4,5},{5,4},{6,7},{7,6},{8,9},{9,8},{10,11... | collective-permute-start | bytes 3538952 | tf_op jit(solution)/shard_map/ppermute | solution.py:798
  475.5 29.1 %collective-permute-start.46 = (bf16[768,768]{1,0:T(8,128)(2,1)}, bf16[768,768]{1,0:T(8,128)(2,1)S(1)}, u32[]{:S(2)}, u32[]{:S(2)}) collective-permute-start(bf16[768,768]{1,0:T(8,128)(2,1)} %add_convert_fusion.7.refs_17_), channel_id=1, source_target_pairs={{0,2},{1,3},{2,0},{3,1},{4,6},{5,7},{6,4},{7,5},{8,10},{9,11},{10,... | collective-permute-start | bytes 3538952 | tf_op jit(solution)/shard_map/ppermute | solution.py:798
  476.4 52.8 %collective-permute-start.48 = (bf16[768,768]{1,0:T(8,128)(2,1)}, bf16[768,768]{1,0:T(8,128)(2,1)}, u32[]{:S(2)}, u32[]{:S(2)}) collective-permute-start(bf16[768,768]{1,0:T(8,128)(2,1)} %add_convert_fusion.5.refs_11_), channel_id=1, source_target_pairs={{0,2},{1,3},{2,0},{3,1},{4,6},{5,7},{6,4},{7,5},{8,10},{9,11},{10,... | collective-permute-start | bytes 3538952 | tf_op jit(solution)/shard_map/ppermute | solution.py:798
  536.9 94.0 %reduce-scatter.8.cloned.1.call-start = ((), (), s32[]{:S(2)}) async-start(), calls=%async_computation.7 | async-start | bytes 1474560 | tf_op jit(solution)/shard_map/reduce_scatter | solution.py:907
  536.9 39.7 %collective-permute-start.50 = (bf16[768,768]{1,0:T(8,128)(2,1)}, bf16[768,768]{1,0:T(8,128)(2,1)}, u32[]{:S(2)}, u32[]{:S(2)}) collective-permute-start(bf16[768,768]{1,0:T(8,128)(2,1)} %add_convert_fusion.2.refs_11_), channel_id=1, source_target_pairs={{0,2},{1,3},{2,0},{3,1},{4,6},{5,7},{6,4},{7,5},{8,10},{9,11},{10,... | collective-permute-start | bytes 3538952 | tf_op jit(solution)/shard_map/ppermute | solution.py:798
  545.0 31.6 %collective-permute-start.51 = (bf16[768,768]{1,0:T(8,128)(2,1)}, bf16[768,768]{1,0:T(8,128)(2,1)}, u32[]{:S(2)}, u32[]{:S(2)}) collective-permute-start(bf16[768,768]{1,0:T(8,128)(2,1)} %add_convert_fusion.1.refs_13_), channel_id=1, source_target_pairs={{0,1},{1,0},{2,3},{3,2},{4,5},{5,4},{6,7},{7,6},{8,9},{9,8},{10,11... | collective-permute-start | bytes 3538952 | tf_op jit(solution)/shard_map/ppermute | solution.py:798
  616.8 45.8 %collective-permute-start.61 = (f32[16,128,128]{2,1,0:T(8,128)}, f32[16,128,128]{2,1,0:T(8,128)S(1)}, u32[]{:S(2)}, u32[]{:S(2)}) collective-permute-start(f32[16,128,128]{2,1,0:T(8,128)} %slice.424), channel_id=1, source_target_pairs={{0,4},{4,0},{1,5},{5,1},{2,6},{6,2},{3,7},{7,3},{8,12},{12,8},{9,1... | collective-permute-start | bytes 3145736 | tf_op jit(solution)/shard_map/ppermute | solution.py:798
  (131 other events, 1247.2 us)
Sparse Core Ops, SparseCore 0:
  10.4 33.2 all-gather.8
  45.3 29.5 all-gather.4
  116.3 32.4 all-gather.6
  474.7 30.0 reduce-scatter.3
  536.9 30.8 reduce-scatter.5
  591.0 30.2 reduce-scatter.7

commit v4 on v3

--- a/solution.py
+++ b/solution.py
@@ -1074,11 +1074,11 @@
             total = out_grad.finish(now(scaled[0]))
             waiting.append(total)
             grad_out = scatter(total)
+            finished = [grad_out]
+        if at == min(2, last):
             total = z_grad.finish(now(dz[0]))
             waiting.append(total)
             grad_z = scatter(total)
-            finished = [grad_out]
-        if at == min(2, last):
             finished = [grad_z]
     x_grad.swap(0, now(dpre[0]))
     total = x_grad.finish(now(dpre[0]))

time: 715 us -> 712 us (level)
    unnamed x188 -> x196, local copies, waits for them, and re-layouts: 38.6 us -> 39.9 us
  transfers between devices with their start and end apart: 74 -> 74, of which waited for: 31 -> 34; matrix products, arithmetic and copies ran while one was open for 20% -> 19% of each run, Pallas kernels for 30% -> 30%
where the time goes in v4:
time: 712 us; the launch traced here: 704 us
  Pallas kernels  288 us (40%)
  local copies, waits for them, and re-layouts  109 us (15%)
  waiting for transfers between devices  106 us (15%)
  starting transfers between devices  78.6 us (11%)
  matrix products  71.1 us (10%)
  other arithmetic  35.9 us (5%)
  between operations  16 us (2%)
    pallas_call x17, Pallas kernels, launch(): return pl.pallas_call(body, in_specs=in_specs, **options)(*args, *wait)  216 us
    ppermute x58, waiting for transfers between devices, across(): return lax.ppermute(value, axis, [(i, i ^ bit) for i in range(size)])  75.1 us
    dot_general x26, matrix products, dot(): lax.dot_general(a, b, dims, precision=precision, preferred_element_type=F32)  71.1 us
    pallas_call x1, Pallas kernels, gate(): pl.pallas_call(functools.partial(gate_kernel, groups, width, tuple(map(le...  58.1 us
    ppermute x58, starting transfers between devices, across(): return lax.ppermute(value, axis, [(i, i ^ bit) for i in range(size)])  54.7 us
    unnamed x196, local copies, waits for them, and re-layouts  39.9 us
    ppermute x8, waiting for transfers between devices, pass_on(): lax.ppermute(value, 'tensor', [(i, j) for i, j in pairs if i ^ j == gap])  28.6 us
    ppermute x8, starting transfers between devices, pass_on(): lax.ppermute(value, 'tensor', [(i, j) for i, j in pairs if i ^ j == gap])  18.4 us
  transfers between devices with their start and end apart: 74, of which 34 were waited for; matrix products, arithmetic and copies ran while one was open for 19% of the time, Pallas kernels for 30%

profile of v4, /device:TPU:0, one launch (start us, length us, event | category | flops | bytes accessed | tf_op | source)
XLA Modules:
  0.0 704.5 jit_solution(9372215652644103697)
XLA Ops:
  66.5 10.6 %prep.1 = (bf16[1040,256]{1,0:T(8,128)(2,1)}, bf16[1024,256]{1,0:T(8,128)(2,1)}, f32[4,12,1024]{2,1,0:T(8,128)}, f32[4,1024,12]{2,1,0:T(8,128)}, f32[4,1024,12]{...) custom-call(bf16[1152,1536]{1,0:T(8,128)(2,1)} %pad.40.n_ref.refs_0_, ...), custom_call_target="tpu_custom_call" | custom-call | bytes 11 | tf_op jit(solution)/shard_map/prep/pallas_call | solution.py:192
  93.9 9.7 %project.4 = (bf16[1040,768]{1,0:T(8,128)(2,1)}, bf16[1024,768]{1,0:T(8,128)(2,1)}, bf16[128,768]{1,0:T(8,128)(2,1)}) custom-call(bf16[1152,1536]{1,0:T(8,128)(2,1)} %pad.40.n_ref.refs_0_, bf16[768,768]{1,0:T(8,128)(2,1)} %bitcast.163, bf16[768,768]{1,0:T(8,128)(2,1)} %copy-done.10, f32[4,3072]{1,0:T(4,128)} %broadcast_select_fusion.5.refs_3_.refs_9_, ...), custom_call_target="tpu_custom_call" | custom-call | bytes 10 | tf_op jit(solution)/shard_map/project/pallas_call | solution.py:118
  129.9 9.7 %project.5 = (bf16[1040,768]{1,0:T(8,128)(2,1)}, bf16[1024,768]{1,0:T(8,128)(2,1)}, bf16[128,768]{1,0:T(8,128)(2,1)}) custom-call(bf16[1152,1536]{1,0:T(8,128)(2,1)} %pad.40.n_ref.refs_0_, bf16[2304,768]{1,0:T(8,128)(2,1)} %constant_dynamic-update-slice_fusion.12.refs_1_.refs_6_.refs_8_.refs_10_, bf16[2304,768]{1,0:T(8,128)(2,1)} %copy-done.1, ...), custom_call_target="tpu_custom_call" | custom-call | bytes 10 | tf_op jit(solution)/shard_map/project/pallas_call | solution.py:118
  139.6 6.0 collective-permute-done.16.refs_5_
  153.1 9.7 %project.6 = (bf16[1040,768]{1,0:T(8,128)(2,1)}, bf16[1024,768]{1,0:T(8,128)(2,1)}, bf16[128,768]{1,0:T(8,128)(2,1)}) custom-call(bf16[1152,1536]{1,0:T(8,128)(2,1)} %pad.40.n_ref.refs_0_, bf16[2304,768]{1,0:T(8,128)(2,1)} %constant_dynamic-update-slice_fusion.12.refs_1_.refs_6_.refs_8_.refs_10_, bf16[2304,768]{1,0:T(8,128)(2,1)} %copy-done.1, ...), custom_call_target="tpu_custom_call" | custom-call | bytes 10 | tf_op jit(solution)/shard_map/project/pallas_call | solution.py:118
  175.2 9.7 %project.7 = (bf16[1040,768]{1,0:T(8,128)(2,1)}, bf16[1024,768]{1,0:T(8,128)(2,1)}, bf16[128,768]{1,0:T(8,128)(2,1)}) custom-call(bf16[1152,1536]{1,0:T(8,128)(2,1)} %pad.40.n_ref.refs_0_, bf16[2304,768]{1,0:T(8,128)(2,1)} %constant_dynamic-update-slice_fusion.12.refs_1_.refs_6_.refs_8_.refs_10_, bf16[2304,768]{1,0:T(8,128)(2,1)} %copy-done.1, ...), custom_call_target="tpu_custom_call" | custom-call | bytes 10 | tf_op jit(solution)/shard_map/project/pallas_call | solution.py:118
  194.6 5.0 slice_bitcast_fusion.4
  199.6 6.3 product.4.refs_7_.refs_4_
  205.9 9.8 %scan.4 = (bf16[1024,768]{1,0:T(8,128)(2,1)}, bf16[8,128,768]{2,1,0:T(8,128)(2,1)}) custom-call(bf16[1024,768]{1,0:T(8,128)(2,1)} %get-tuple-element.182.refs_0_, bf16[1024,256]{1,0:T(8,128)(2,1)} %get-tuple-element.170.refs_5_.refs_1_.refs_27_.refs_2_, f32[4,1024,12]{2,1,0:T(8,128)} %get-tuple-element.183.refs_2_.refs_3_, ...), custom_call_target="tpu_custom_call" | custom-call | bytes 9 | tf_op jit(solution)/shard_map/scan/pallas_call | solution.py:118
  216.7 9.7 %scan.5 = (bf16[1024,768]{1,0:T(8,128)(2,1)}, bf16[8,128,768]{2,1,0:T(8,128)(2,1)}) custom-call(bf16[1024,768]{1,0:T(8,128)(2,1)} %get-tuple-element.195.refs_7_.refs_0_, bf16[1024,256]{1,0:T(8,128)(2,1)} %get-tuple-element.170.refs_5_.refs_1_.refs_27_.refs_2_, f32[4,1024,12]{2,1,0:T(8,128)} %get-tuple-element.183.refs_2_.refs_3_, ...), custom_call_target="tpu_custom_call" | custom-call | bytes 9 | tf_op jit(solution)/shard_map/scan/pallas_call | solution.py:118
  229.7 9.7 %scan.6 = (bf16[1024,768]{1,0:T(8,128)(2,1)}, bf16[8,128,768]{2,1,0:T(8,128)(2,1)}) custom-call(bf16[1024,768]{1,0:T(8,128)(2,1)} %get-tuple-element.200.refs_8_.refs_0_, bf16[1024,256]{1,0:T(8,128)(2,1)} %get-tuple-element.170.refs_5_.refs_1_.refs_27_.refs_2_, f32[4,1024,12]{2,1,0:T(8,128)} %get-tuple-element.183.refs_2_.refs_3_, ...), custom_call_target="tpu_custom_call" | custom-call | bytes 9 | tf_op jit(solution)/shard_map/scan/pallas_call | solution.py:118
  254.5 9.8 %scan.7 = (bf16[1024,768]{1,0:T(8,128)(2,1)}, bf16[8,128,768]{2,1,0:T(8,128)(2,1)}) custom-call(bf16[1024,768]{1,0:T(8,128)(2,1)} %get-tuple-element.205.refs_3_.refs_0_, bf16[1024,256]{1,0:T(8,128)(2,1)} %get-tuple-element.170.refs_5_.refs_1_.refs_27_.refs_2_, f32[4,1024,12]{2,1,0:T(8,128)} %get-tuple-element.183.refs_2_.refs_3_, ...), custom_call_target="tpu_custom_call" | custom-call | bytes 9 | tf_op jit(solution)/shard_map/scan/pallas_call | solution.py:118
  266.1 6.3 product.7.refs_7_
  272.4 6.3 product.6.refs_6_
  278.7 6.3 product.5.refs_5_
  285.6 58.1 %gate.1 = (bf16[1024,768]{1,0:T(8,128)(2,1)}, bf16[1024,768]{1,0:T(8,128)(2,1)}, bf16[1024,768]{1,0:T(8,128)(2,1)}, bf16[1024,768]{1,0:T(8,128)(2,1)}, bf16[1024...) custom-call(bf16[1024,768]{1,0:T(8,128)(2,1)} %get-tuple-element.207, ...), custom_call_target="tpu_custom_call" | custom-call | bytes 55 | tf_op jit(solution)/shard_map/gate/pallas_call | solution.py:478
  361.8 7.0 collective-permute-done.28.refs_16_.refs_7_
  383.5 21.7 %back.4 = (bf16[1152,768]{1,0:T(8,128)(2,1)}, f32[1024,256]{1,0:T(8,128)}, f32[48,768]{1,0:T(8,128)}, f32[1,12,1024]{2,1,0:T(8,128)}, f32[1,12,1024]{2,1,0:T(8,128)}) custom-call(bf16[1040,768]{1,0:T(8,128)(2,1)} %get-tuple-element.231.refs_0_, bf16[1024,768]{1,0:T(8,128)(2,1)} %get-tuple-element.232.refs_1_, ...), custom_call_target="tpu_custom_call" | custom-call | bytes 18 | tf_op jit(solution)/shard_map/back/pallas_call | solution.py:118
  405.2 5.1 collective-permute-done.38
  438.0 21.9 %back.5 = (bf16[1152,768]{1,0:T(8,128)(2,1)}, f32[1024,256]{1,0:T(8,128)}, f32[48,768]{1,0:T(8,128)}, f32[1,12,1024]{2,1,0:T(8,128)}, f32[1,12,1024]{2,1,0:T(8,128)}) custom-call(bf16[1040,768]{1,0:T(8,128)(2,1)} %get-tuple-element.226.refs_0_, bf16[1024,768]{1,0:T(8,128)(2,1)} %get-tuple-element.227.refs_1_, ...), custom_call_target="tpu_custom_call" | custom-call | bytes 18 | tf_op jit(solution)/shard_map/back/pallas_call | solution.py:118
  475.7 22.1 %back.6 = (bf16[1152,768]{1,0:T(8,128)(2,1)}, f32[1024,256]{1,0:T(8,128)}, f32[48,768]{1,0:T(8,128)}, f32[1,12,1024]{2,1,0:T(8,128)}, f32[1,12,1024]{2,1,0:T(8,128)}) custom-call(bf16[1040,768]{1,0:T(8,128)(2,1)} %get-tuple-element.258.refs_0_, bf16[1024,768]{1,0:T(8,128)(2,1)} %get-tuple-element.259.refs_1_, ...), custom_call_target="tpu_custom_call" | custom-call | bytes 18 | tf_op jit(solution)/shard_map/back/pallas_call | solution.py:118
  520.7 18.6 %collective-permute-done.49 = bf16[768,768]{1,0:T(8,128)(2,1)S(1)} collective-permute-done((bf16[768,768]{1,0:T(8,128)(2,1)S(1)}, bf16[768,768]{1,0:T(8,128)(2,1)S(1)}, u32[]{:S(2)}, u32[]{:S(2)}) %collective-permute-start.49) | collective-permute-done | bytes 1179680 | tf_op jit(solution)/shard_map/ppermute | solution.py:798
  554.4 21.7 %back.7 = (bf16[1152,768]{1,0:T(8,128)(2,1)}, f32[1024,256]{1,0:T(8,128)}, f32[48,768]{1,0:T(8,128)}, f32[1,12,1024]{2,1,0:T(8,128)}, f32[1,12,1024]{2,1,0:T(8,128)}) custom-call(bf16[1040,768]{1,0:T(8,128)(2,1)} %get-tuple-element.221.refs_0_, bf16[1024,768]{1,0:T(8,128)(2,1)} %get-tuple-element.222.refs_1_, ...), custom_call_target="tpu_custom_call" | custom-call | bytes 18 | tf_op jit(solution)/shard_map/back/pallas_call | solution.py:118
  630.9 25.3 %final.1 = (f32[1024,1536]{1,0:T(8,128)}, f32[8,1536]{1,0:T(8,128)}) custom-call(bf16[1152,768]{1,0:T(8,128)(2,1)} %get-tuple-element.275.refs_0_, bf16[1152,768]{1,0:T(8,128)(2,1)} %get-tuple-element.267.refs_1_, bf16[1152,768]{1,0:T(8,128)(2,1)} %get-tuple-element.265.refs_2_, bf16[1152,768]{1,0:T(8,128)(2,1)} %get-tuple-element.261.refs_3_, ...), custom_call_target="tpu_custom_call" | custom-call | bytes 20 | tf_op jit(solution)/shard_map/final/pallas_call | solution.py:118
  (550 shorter events, 362.5 us)
Async XLA Ops:
  7.2 52.1 %all-gather.9.cloned.1.call-start = ((), (), s32[]{:S(2)}) async-start(), calls=%async_computation.8 | async-start | bytes 1474560 | tf_op jit(solution)/shard_map/all_gather | solution.py:921
  10.3 78.6 %all-gather.5.cloned.1.call-start = ((), (), s32[]{:S(2)}) async-start(), calls=%async_computation.3 | async-start | bytes 1474560 | tf_op jit(solution)/shard_map/all_gather | solution.py:922
  14.3 138.8 %all-gather.7.cloned.1.call-start = ((), (), s32[]{:S(2)}) async-start(), calls=%async_computation.4 | async-start | bytes 1474560 | tf_op jit(solution)/shard_map/all_gather | solution.py:923
  59.4 29.5 %collective-permute-start.7 = (bf16[768,768]{1,0:T(8,128)(2,1)}, bf16[768,768]{1,0:T(8,128)(2,1)}, u32[]{:S(2)}, u32[]{:S(2)}) collective-permute-start(bf16[768,768]{1,0:T(8,128)(2,1)} %bitcast.161), channel_id=1, source_target_pairs={{0,1},{1,0},{2,3},{3,2},{4,5},{5,4},{6,7},{7,6},{8,9},{9,8},{10,11... | collective-permute-start | bytes 3538952 | tf_op jit(solution)/shard_map/ppermute | solution.py:798
  59.5 29.4 %collective-permute-start.8 = (bf16[768,768]{1,0:T(8,128)(2,1)}, bf16[768,768]{1,0:T(8,128)(2,1)}, u32[]{:S(2)}, u32[]{:S(2)}) collective-permute-start(bf16[768,768]{1,0:T(8,128)(2,1)} %bitcast.162), channel_id=1, source_target_pairs={{0,2},{1,3},{2,0},{3,1},{4,6},{5,7},{6,4},{7,5},{8,10},{9,11},{10,... | collective-permute-start | bytes 3538952 | tf_op jit(solution)/shard_map/ppermute | solution.py:798
  115.3 30.3 %collective-permute-start.14 = (bf16[768,768]{1,0:T(8,128)(2,1)}, bf16[768,768]{1,0:T(8,128)(2,1)}, u32[]{:S(2)}, u32[]{:S(2)}) collective-permute-start(bf16[768,768]{1,0:T(8,128)(2,1)} %all-gather.5.cloned.1.call-done.refs_1_.refs_16_), channel_id=1, source_target_pairs={{0,1},{1,0},{2,3},{3,2},{4,5},{5,4},{6,7},{7,6},{8,9},{9,8},{10,11... | collective-permute-start | bytes 3538952 | tf_op jit(solution)/shard_map/ppermute | solution.py:798
  115.7 29.9 %collective-permute-start.15 = (bf16[768,768]{1,0:T(8,128)(2,1)}, bf16[768,768]{1,0:T(8,128)(2,1)}, u32[]{:S(2)}, u32[]{:S(2)}) collective-permute-start(bf16[768,768]{1,0:T(8,128)(2,1)} %all-gather.5.cloned.1.call-done.refs_1_.refs_16_), channel_id=1, source_target_pairs={{0,2},{1,3},{2,0},{3,1},{4,6},{5,7},{6,4},{7,5},{8,10},{9,11},{10,... | collective-permute-start | bytes 3538952 | tf_op jit(solution)/shard_map/ppermute | solution.py:798
  116.2 388.1 %reduce-scatter.4.cloned.1.call-start = ((), (), s32[]{:S(2)}) async-start(), calls=%async_computation.5 | async-start | bytes 1474560 | tf_op jit(solution)/shard_map/reduce_scatter | solution.py:907
  169.9 45.8 %collective-permute-start.22 = (bf16[2304,768]{1,0:T(8,128)(2,1)S(1)}, bf16[2304,768]{1,0:T(8,128)(2,1)}, u32[]{:S(2)}, u32[]{:S(2)}) collective-permute-start(bf16[2304,768]{1,0:T(8,128)(2,1)S(1)} %constant_dynamic-update-slice_fusion.16.refs_7_.refs_1_.refs_18_.refs_20_.refs_22_), channel_id=1, source_target_pairs={{0,4},{4,0},{1,5},{5,1},{2,6},{6,2},{3,7},{7,3},{8,12},{12,8},{9,1... | collective-permute-start | bytes 10616840 | tf_op jit(solution)/shard_map/ppermute | solution.py:798
  190.6 35.8 %collective-permute-start.23 = (bf16[768,768]{1,0:T(8,128)(2,1)S(1)}, bf16[768,768]{1,0:T(8,128)(2,1)}, u32[]{:S(2)}, u32[]{:S(2)}) collective-permute-start(bf16[768,768]{1,0:T(8,128)(2,1)S(1)} %copy-done.11), channel_id=1, source_target_pairs={{0,1},{1,0},{2,3},{3,2},{4,5},{5,4},{6,7},{7,6},{8,9},{9,8},{10,11... | collective-permute-start | bytes 3538952 | tf_op jit(solution)/shard_map/ppermute | solution.py:798
  193.1 33.3 %collective-permute-start.24 = (bf16[768,768]{1,0:T(8,128)(2,1)S(1)}, bf16[768,768]{1,0:T(8,128)(2,1)}, u32[]{:S(2)}, u32[]{:S(2)}) collective-permute-start(bf16[768,768]{1,0:T(8,128)(2,1)S(1)} %copy-done.11), channel_id=1, source_target_pairs={{0,2},{1,3},{2,0},{3,1},{4,6},{5,7},{6,4},{7,5},{8,10},{9,11},{10,... | collective-permute-start | bytes 3538952 | tf_op jit(solution)/shard_map/ppermute | solution.py:798
  355.5 25.4 %collective-permute-start.35 = (bf16[768,768]{1,0:T(8,128)(2,1)S(1)}, bf16[768,768]{1,0:T(8,128)(2,1)}, u32[]{:S(2)}, u32[]{:S(2)}) collective-permute-start(bf16[768,768]{1,0:T(8,128)(2,1)S(1)} %convolution_convert_fusion.7), channel_id=1, source_target_pairs={{0,4},{4,0},{1,5},{5,1},{2,6},{6,2},{3,7},{7,3},{8,12},{12,8},{9,1... | collective-permute-start | bytes 3538952 | tf_op jit(solution)/shard_map/ppermute | solution.py:798
  376.8 28.4 %collective-permute-start.37 = (bf16[768,768]{1,0:T(8,128)(2,1)}, bf16[768,768]{1,0:T(8,128)(2,1)}, u32[]{:S(2)}, u32[]{:S(2)}) collective-permute-start(bf16[768,768]{1,0:T(8,128)(2,1)} %add_convert_fusion.11.refs_14_), channel_id=1, source_target_pairs={{0,2},{1,3},{2,0},{3,1},{4,6},{5,7},{6,4},{7,5},{8,10},{9,11},{10,... | collective-permute-start | bytes 3538952 | tf_op jit(solution)/shard_map/ppermute | solution.py:798
  383.5 26.9 %collective-permute-start.38 = (bf16[768,768]{1,0:T(8,128)(2,1)}, bf16[768,768]{1,0:T(8,128)(2,1)}, u32[]{:S(2)}, u32[]{:S(2)}) collective-permute-start(bf16[768,768]{1,0:T(8,128)(2,1)} %add_convert_fusion.10.refs_15_), channel_id=1, source_target_pairs={{0,1},{1,0},{2,3},{3,2},{4,5},{5,4},{6,7},{7,6},{8,9},{9,8},{10,11... | collective-permute-start | bytes 3538952 | tf_op jit(solution)/shard_map/ppermute | solution.py:798
  428.9 31.0 %collective-permute-start.44 = (bf16[768,768]{1,0:T(8,128)(2,1)}, bf16[768,768]{1,0:T(8,128)(2,1)}, u32[]{:S(2)}, u32[]{:S(2)}) collective-permute-start(bf16[768,768]{1,0:T(8,128)(2,1)} %add_convert_fusion.8.refs_12_), channel_id=1, source_target_pairs={{0,1},{1,0},{2,3},{3,2},{4,5},{5,4},{6,7},{7,6},{8,9},{9,8},{10,11... | collective-permute-start | bytes 3538952 | tf_op jit(solution)/shard_map/ppermute | solution.py:798
  429.2 30.7 %collective-permute-start.43 = (bf16[768,768]{1,0:T(8,128)(2,1)}, bf16[768,768]{1,0:T(8,128)(2,1)}, u32[]{:S(2)}, u32[]{:S(2)}) collective-permute-start(bf16[768,768]{1,0:T(8,128)(2,1)} %add_convert_fusion.9.refs_11_), channel_id=1, source_target_pairs={{0,2},{1,3},{2,0},{3,1},{4,6},{5,7},{6,4},{7,5},{8,10},{9,11},{10,... | collective-permute-start | bytes 3538952 | tf_op jit(solution)/shard_map/ppermute | solution.py:798
  474.1 102.0 %reduce-scatter.6.cloned.1.call-start = ((), (), s32[]{:S(2)}) async-start(), calls=%async_computation.6 | async-start | bytes 1474560 | tf_op jit(solution)/shard_map/reduce_scatter | solution.py:907
  474.1 28.4 %collective-permute-start.46 = (bf16[768,768]{1,0:T(8,128)(2,1)}, bf16[768,768]{1,0:T(8,128)(2,1)}, u32[]{:S(2)}, u32[]{:S(2)}) collective-permute-start(bf16[768,768]{1,0:T(8,128)(2,1)} %add_convert_fusion.5.refs_11_), channel_id=1, source_target_pairs={{0,2},{1,3},{2,0},{3,1},{4,6},{5,7},{6,4},{7,5},{8,10},{9,11},{10,... | collective-permute-start | bytes 3538952 | tf_op jit(solution)/shard_map/ppermute | solution.py:798
  510.9 28.4 %collective-permute-start.49 = (bf16[768,768]{1,0:T(8,128)(2,1)S(1)}, bf16[768,768]{1,0:T(8,128)(2,1)S(1)}, u32[]{:S(2)}, u32[]{:S(2)}) collective-permute-start(bf16[768,768]{1,0:T(8,128)(2,1)S(1)} %copy-done.24), channel_id=1, source_target_pairs={{0,1},{1,0},{2,3},{3,2},{4,5},{5,4},{6,7},{7,6},{8,9},{9,8},{10,11... | collective-permute-start | bytes 3538952 | tf_op jit(solution)/shard_map/ppermute | solution.py:798
  512.5 28.0 %collective-permute-start.48 = (bf16[768,768]{1,0:T(8,128)(2,1)S(1)}, bf16[768,768]{1,0:T(8,128)(2,1)S(1)}, u32[]{:S(2)}, u32[]{:S(2)}) collective-permute-start(bf16[768,768]{1,0:T(8,128)(2,1)S(1)} %copy-done.23), channel_id=1, source_target_pairs={{0,2},{1,3},{2,0},{3,1},{4,6},{5,7},{6,4},{7,5},{8,10},{9,11},{10,... | collective-permute-start | bytes 3538952 | tf_op jit(solution)/shard_map/ppermute | solution.py:798
  543.4 86.9 %reduce-scatter.8.cloned.1.call-start = ((), (), s32[]{:S(2)}) async-start(), calls=%async_computation.7 | async-start | bytes 1474560 | tf_op jit(solution)/shard_map/reduce_scatter | solution.py:907
  543.4 32.6 %collective-permute-start.50 = (bf16[768,768]{1,0:T(8,128)(2,1)}, bf16[768,768]{1,0:T(8,128)(2,1)}, u32[]{:S(2)}, u32[]{:S(2)}) collective-permute-start(bf16[768,768]{1,0:T(8,128)(2,1)} %add_convert_fusion.3.refs_11_), channel_id=1, source_target_pairs={{0,2},{1,3},{2,0},{3,1},{4,6},{5,7},{6,4},{7,5},{8,10},{9,11},{10,... | collective-permute-start | bytes 3538952 | tf_op jit(solution)/shard_map/ppermute | solution.py:798
  544.9 31.1 %collective-permute-start.51 = (bf16[768,768]{1,0:T(8,128)(2,1)}, bf16[768,768]{1,0:T(8,128)(2,1)}, u32[]{:S(2)}, u32[]{:S(2)}) collective-permute-start(bf16[768,768]{1,0:T(8,128)(2,1)} %add_convert_fusion.2.refs_13_), channel_id=1, source_target_pairs={{0,1},{1,0},{2,3},{3,2},{4,5},{5,4},{6,7},{7,6},{8,9},{9,8},{10,11... | collective-permute-start | bytes 3538952 | tf_op jit(solution)/shard_map/ppermute | solution.py:798
  616.3 45.5 %collective-permute-start.61 = (f32[16,128,128]{2,1,0:T(8,128)}, f32[16,128,128]{2,1,0:T(8,128)S(1)}, u32[]{:S(2)}, u32[]{:S(2)}) collective-permute-start(f32[16,128,128]{2,1,0:T(8,128)} %slice.424), channel_id=1, source_target_pairs={{0,4},{4,0},{1,5},{5,1},{2,6},{6,2},{3,7},{7,3},{8,12},{12,8},{9,1... | collective-permute-start | bytes 3145736 | tf_op jit(solution)/shard_map/ppermute | solution.py:798
  (135 other events, 1303.1 us)
Sparse Core Ops, SparseCore 0:
  10.4 33.1 all-gather.8
  45.2 29.7 all-gather.4
  116.4 32.4 all-gather.6
  474.2 30.0 reduce-scatter.3
  543.5 28.2 reduce-scatter.5
  590.4 27.7 reduce-scatter.7
